TPU v7x, 512 devices: a whole 4x8x8 slice. The times are simulated.
512 devices in a mesh: seq: 64 (over z, y_lo, core), head: 8 (over y_hi, x).
Axes of the slice: x: 4, y: 8 (y_hi: 2, y_lo: 4; y = y_hi * 4 + y_lo), z: 8, core: 2. Of those that a mesh axis runs over, the one named last changes fastest.
Arguments:
- queries: bfloat16 [16384, 2048], P('seq', 'head'), may hold values from -1.5 to 1.5
- keys: bfloat16 [16384, 2048], P('seq', 'head'), may hold values from -1.5 to 1.5
- values: bfloat16 [16384, 2048], P('seq', 'head'), may hold values from -6 to 6
- out_grad: bfloat16 [16384, 2048], P('seq', 'head'), may hold values from -96 to 96
- random_blocks: int32 [256, 3], replicated, may hold values from 2 to 255, as said below
- w_query: bfloat16 [2048, 2048], P(None, 'head'), may hold values from -0.125 to 0.125
- w_key: bfloat16 [2048, 2048], P(None, 'head'), may hold values from -0.125 to 0.125
- w_value: bfloat16 [2048, 2048], P(None, 'head'), may hold values from -0.125 to 0.125
Outputs:
- input_grad: bfloat16 [16384, 2048], P('seq', 'head')
Inputs may be any that keep to these rules, and one draw needn't show every extreme that they name: `random_blocks`: row q names 3 distinct blocks, none global. Seen as 64 shards of 4 consecutive blocks in a loop, no entry of a shard's rows lies in that shard or in the shard just before or after it in the loop, and the rows of one shard name blocks of any one other shard at most 1 times in all; some pair of shards reaches 1.
All inputs are finite; a program needn't handle non-finite values.
Results may differ from a plain program's by a relative error of at most 0.015.
Values may be sent and summed in bfloat16 or wider, within the bound.
No kernel may reach another device: no remote copies, remote signals or barrier semaphores. Data moves between devices by JAX's collectives and lax.ppermute only.
A program may use at most 128 MiB of HBM per device.

v0:
```python
import math

import jax
import jax.numpy as jnp
from jax import lax
from jax.sharding import PartitionSpec as P

HD = 128
BLK = 64
GLOB = 2
RAND = 3


def from_root(value, axis, root):
    mine = lax.axis_index(axis) == root
    return lax.psum(jnp.where(mine, value, jnp.zeros_like(value)), axis)


def block_attention(query_blocks, grad_blocks, key_sets, value_sets, column_weights, score_scale):
    scores = (
        jnp.einsum("qhid,qhjd->qhij", query_blocks, key_sets, preferred_element_type=jnp.float32)
        * score_scale
    )
    weighted = jnp.exp(scores) * column_weights[:, None, None, :]
    probabilities = weighted / jnp.sum(weighted, axis=3, keepdims=True)
    probs_low = probabilities.astype(jnp.bfloat16)
    outputs = jnp.einsum(
        "qhij,qhjd->qhid", probs_low, value_sets, preferred_element_type=jnp.float32
    )
    row_delta = jnp.sum(grad_blocks.astype(jnp.float32) * outputs, axis=3)
    grad_probs = jnp.einsum(
        "qhid,qhjd->qhij", grad_blocks, value_sets, preferred_element_type=jnp.float32
    )
    grad_low = (probabilities * (grad_probs - row_delta[:, :, :, None])).astype(jnp.bfloat16)
    query_grad = score_scale * jnp.einsum(
        "qhij,qhjd->qhid", grad_low, key_sets, preferred_element_type=jnp.float32
    )
    return (query_grad, probs_low, grad_low)


def body(queries, keys, values, out_grad, random_blocks, w_query, w_key, w_value):
    tokens_here, head_width = queries.shape
    per_shard = tokens_here // BLK
    shards = lax.axis_size("seq")
    position = lax.axis_index("seq")
    heads_here = head_width // HD
    listed = GLOB + 3 + RAND
    capacity = (RAND * per_shard + shards - 4) // (shards - 3)
    score_scale = 1.0 / math.sqrt(HD)
    ref_total = RAND * per_shard
    pair_blocks = (
        jnp.concatenate([keys, values], axis=1)
        .reshape(per_shard, BLK, 2 * heads_here, HD)
        .transpose(0, 2, 1, 3)
    )
    global_pair = from_root(pair_blocks[:GLOB], "seq", 0)
    block_table = random_blocks.reshape(shards, ref_total)
    owners = block_table // per_shard
    earlier = jnp.arange(ref_total)[None, :] < jnp.arange(ref_total)[:, None]
    same_owner = owners[:, :, None] == owners[:, None, :]
    occurrence = jnp.sum(same_owner & earlier[None], axis=2)
    from_here = owners == position
    slot_hits = from_here[:, :, None] & (
        occurrence[:, :, None] == jnp.arange(capacity)[None, None, :]
    )
    chosen = jnp.sum(
        jnp.where(slot_hits, (block_table - position * per_shard)[:, :, None], 0), axis=1
    )
    in_use = jnp.any(slot_hits, axis=1)
    target_index = jnp.arange(shards)[:, None]
    first_slot = jnp.arange(capacity)[None, :] == 0
    to_left = (target_index == (position - 1) % shards) & first_slot
    to_right = (target_index == (position + 1) % shards) & first_slot
    chosen = jnp.where(to_left, 0, jnp.where(to_right, per_shard - 1, chosen))
    in_use = in_use | to_left | to_right
    send_index = chosen.reshape(-1)
    send_live = in_use.reshape(-1)
    outgoing = jnp.where(
        send_live[:, None, None, None],
        jnp.take(pair_blocks, send_index, axis=0),
        jnp.zeros((), jnp.bfloat16),
    )
    incoming = lax.all_to_all(outgoing, "seq", split_axis=0, concat_axis=0, tiled=True)
    my_table = lax.dynamic_index_in_dim(block_table, position, 0, keepdims=False)
    my_owner = my_table // per_shard
    my_occurrence = lax.dynamic_index_in_dim(occurrence, position, 0, keepdims=False)
    recv_slot = my_owner * capacity + my_occurrence
    random_pair = jnp.take(incoming, recv_slot, axis=0).reshape(
        per_shard, RAND, 2 * heads_here, BLK, HD
    )
    left_slot = (position - 1) % shards * capacity
    right_slot = (position + 1) % shards * capacity
    left_rim = lax.dynamic_index_in_dim(incoming, left_slot, 0)
    right_rim = lax.dynamic_index_in_dim(incoming, right_slot, 0)
    before = jnp.concatenate([left_rim, pair_blocks[:-1]], axis=0)
    following = jnp.concatenate([pair_blocks[1:], right_rim], axis=0)
    pair_sets = jnp.concatenate(
        [
            jnp.broadcast_to(global_pair[None], (per_shard, GLOB, 2 * heads_here, BLK, HD)),
            before[:, None],
            pair_blocks[:, None],
            following[:, None],
            random_pair,
        ],
        axis=1,
    )
    all_sets = pair_sets.transpose(0, 2, 1, 3, 4).reshape(
        per_shard, 2 * heads_here, listed * BLK, HD
    )
    total_blocks = per_shard * shards
    block_ids = position * per_shard + jnp.arange(per_shard)
    window_ids = jnp.stack(
        [(block_ids - 1) % total_blocks, block_ids, (block_ids + 1) % total_blocks], axis=1
    )
    repeated = jnp.any(jnp.arange(GLOB)[None, :, None] == window_ids[:, None, :], axis=2)
    entry_weights = jnp.concatenate(
        [
            jnp.where(repeated, 0.0, 1.0).astype(jnp.float32),
            jnp.ones((per_shard, 3 + RAND), jnp.float32),
        ],
        axis=1,
    )
    column_weights = jnp.repeat(entry_weights, BLK, axis=1)
    key_sets = all_sets[:, :heads_here]
    value_sets = all_sets[:, heads_here:]
    query_blocks = queries.reshape(per_shard, BLK, heads_here, HD).transpose(0, 2, 1, 3)
    grad_blocks = out_grad.reshape(per_shard, BLK, heads_here, HD).transpose(0, 2, 1, 3)
    query_grad, probs_low, grad_low = block_attention(
        query_blocks, grad_blocks, key_sets, value_sets, column_weights, score_scale
    )
    key_part = score_scale * jnp.einsum(
        "qhij,qhid->qhjd", grad_low, query_blocks, preferred_element_type=jnp.float32
    )
    value_part = jnp.einsum(
        "qhij,qhid->qhjd", probs_low, grad_blocks, preferred_element_type=jnp.float32
    )
    pair_grads = (
        jnp.concatenate([key_part, value_part], axis=1)
        .reshape(per_shard, 2 * heads_here, listed, BLK, HD)
        .transpose(0, 2, 1, 3, 4)
    )
    own_grads = pair_grads[:, GLOB + 1]
    own_grads = own_grads.at[:-1].add(pair_grads[1:, GLOB])
    own_grads = own_grads.at[1:].add(pair_grads[:-1, GLOB + 2])
    global_total = lax.psum(jnp.sum(pair_grads[:, :GLOB], axis=0), "seq")
    own_grads = own_grads.at[:GLOB].add(jnp.where(position == 0, global_total, 0.0))
    slot_count = shards * capacity
    random_grads = pair_grads[:, GLOB + 3 :].reshape(ref_total, 2 * heads_here, BLK, HD)
    outgoing_grads = jnp.zeros((slot_count, 2 * heads_here, BLK, HD), jnp.float32)
    outgoing_grads = outgoing_grads.at[recv_slot].add(random_grads)
    outgoing_grads = outgoing_grads.at[left_slot].add(pair_grads[0, GLOB])
    outgoing_grads = outgoing_grads.at[right_slot].add(pair_grads[-1, GLOB + 2])
    returned = lax.all_to_all(outgoing_grads, "seq", split_axis=0, concat_axis=0, tiled=True)
    own_grads = own_grads.at[send_index].add(
        jnp.where(send_live[:, None, None, None], returned, 0.0)
    )
    query_low = (
        query_grad.astype(jnp.bfloat16).transpose(0, 2, 1, 3).reshape(tokens_here, head_width)
    )
    key_low = (
        own_grads[:, :heads_here]
        .astype(jnp.bfloat16)
        .transpose(0, 2, 1, 3)
        .reshape(tokens_here, head_width)
    )
    value_low = (
        own_grads[:, heads_here:]
        .astype(jnp.bfloat16)
        .transpose(0, 2, 1, 3)
        .reshape(tokens_here, head_width)
    )
    contract = (((1,), (1,)), ((), ()))
    term_rows = lax.dot_general(w_query, query_low, contract, preferred_element_type=jnp.float32)
    term_rows = term_rows + lax.dot_general(
        w_key, key_low, contract, preferred_element_type=jnp.float32
    )
    term_rows = term_rows + lax.dot_general(
        w_value, value_low, contract, preferred_element_type=jnp.float32
    )
    features = lax.psum_scatter(
        term_rows.astype(jnp.bfloat16), "head", scatter_dimension=0, tiled=True
    ).astype(jnp.float32)
    return features.T.astype(jnp.bfloat16)


def solution(mesh):
    in_specs = (
        P("seq", "head"),
        P("seq", "head"),
        P("seq", "head"),
        P("seq", "head"),
        P(),
        P(None, "head"),
        P(None, "head"),
        P(None, "head"),
    )
    out_specs = P("seq", "head")
    return jax.shard_map(body, mesh=mesh, in_specs=in_specs, out_specs=out_specs, check_vma=False)
```

profile of v0, /device:TPU:1, one launch (start us, length us, event | category | flops | bytes accessed | tf_op | source)
XLA Modules:
  0.0 1253.2 jit_solution(16728224273111162761)
XLA Ops:
  6.5 0.9 copy.148
  7.6 0.1 convert_reduce_fusion
  7.8 0.1 copy.153
  7.9 0.1 eq.121
  8.1 0.7 fusion.58
  8.8 0.7 select_reduce_fusion
  9.5 0.1 reduce_sum.56
  9.6 0.1 reduce_sum.57
  9.8 1.0 pad_maximum_fusion.1
  10.9 0.1 reduce_or.26
  11.1 0.1 reduce_or.27
  11.2 3.1 gather_fusion
  14.3 4.0 select_select_fusion
  18.2 15.7 %all-to-all-start = ((bf16[64,4,64,128]{3,2,1,0:T(8,128)(2,1)}), bf16[64,4,64,128]{3,2,1,0:T(8,128)(2,1)}, u32[]{:S(2)}, u32[]{:S(2)}) async-start(bf16[64,4,64,128]{3,2,1,0:T(8,128)(2,1)} %select_select_fusion), calls=%async_computation | async-start | bytes 8388608 | tf_op jit(solution)/shard_map/all_to_all | solution.py:83
  34.1 0.7 slice_select_fusion
  34.8 0.2 dynamic-slice_reduce_fusion
  35.2 0.2 fusion.48
  35.4 0.6 compare_and_fusion
  36.0 0.9 fusion.60
  37.1 0.7 reshape.545
  37.8 0.7 and_reduce_fusion
  38.6 484.7 %all-reduce.4.cloned.1.call-done = bf16[2,4,64,128]{3,2,1,0:T(8,128)(2,1)} async-done(((bf16[2,4,64,128]{3,2,1,0:T(8,128)(2,1)}), bf16[2,4,64,128]{3,2,1,0:T(8,128)(2,1)}) %all-reduce.4.cloned.1.call-update) | async-done | bytes 131088 | tf_op jit(solution)/shard_map/psum | solution.py:16
  523.3 1.0 broadcast_dynamic-update-slice_fusion
  524.4 0.9 constant_dynamic-slice_fusion.1
  525.3 1.0 fusion.21
  526.3 1.0 fusion.22
  527.3 3.7 gather_fusion.1
  531.0 1.5 select_dynamic-update-slice_fusion
  532.5 1.3 copy-done.3
  533.9 1.9 copy.158
  535.8 0.5 fusion.5
  536.3 0.8 fusion.14
  537.1 0.4 fusion.9
  537.5 0.5 fusion.23
  538.0 0.5 fusion.7
  538.5 0.8 copy-done.4
  539.4 0.5 convolution_multiply_fusion
  539.9 0.4 pad_maximum_fusion
  540.3 0.3 copy.211
  540.6 1.6 copy-done.1
  542.2 2.0 copy-done.2
  544.2 1.3 slice.213
  545.4 4.3 broadcast_in_dim.125
  549.7 4.7 scatter_fusion
  554.4 2.2 fusion.26
  556.6 2.3 fusion.27
  558.9 7.7 all-to-all-start.1
  566.6 1.4 fusion.10
  568.0 0.1 copy.162
  568.1 2.0 slice_reduce_fusion
  570.2 0.2 reduce-scatter.2.cloned.1.call-start
  570.4 1.1 slice_bitcast_fusion
  571.5 1.9 fusion.32
  573.4 1.2 fusion.19
  574.5 1.1 fusion.16
  575.6 556.7 %all-reduce.6.cloned.1.call-done = f32[2,4,64,128]{3,2,1,0:T(8,128)} async-done(((f32[2,4,64,128]{3,2,1,0:T(8,128)}), f32[2,4,64,128]{3,2,1,0:T(8,128)}) %all-reduce.6.cloned.1.call-update) | async-done | bytes 262160 | tf_op jit(solution)/shard_map/psum | solution.py:145
  1132.4 8.5 broadcast_select_fusion
  1140.9 12.3 scatter_fusion.1
  1153.3 0.1 copy.167
  1153.5 0.1 copy.168
  1153.6 0.9 copy-done.6
  1154.5 2.1 convolution_add_fusion.1
  1156.6 1.5 fusion.1
  1158.1 88.5 %reduce-scatter.2.cloned.1.call-done = bf16[256,256]{0,1:T(8,128)(2,1)} async-done(((bf16[2048,256]{0,1:T(8,128)(2,1)}), bf16[256,256]{0,1:T(8,128)(2,1)}) %reduce-scatter.2.cloned.1.call-update) | async-done | bytes 131088 | tf_op jit(solution)/shard_map/reduce_scatter | solution.py:180
  (62 shorter events, 1.4 us)
Async XLA Ops:
  6.5 565.0 %copy-start = (bf16[2048,256]{1,0:T(8,128)(2,1)S(1)}, bf16[2048,256]{1,0:T(8,128)(2,1)}, u32[]{:S(2)}) copy-start(bf16[2048,256]{1,0:T(8,128)(2,1)} %param.23) | copy-start | bytes 3145732
  9.8 1.2 copy-start.10
  18.2 18.9 %copy-start.8 = (bf16[256,256]{1,0:T(8,128)(2,1)S(1)}, bf16[256,256]{1,0:T(8,128)(2,1)}, u32[]{:S(2)}) copy-start(bf16[256,256]{1,0:T(8,128)(2,1)} %param.18) | copy-start | bytes 393220
  18.2 19.5 %copy-start.9 = (bf16[256,256]{1,0:T(8,128)(2,1)S(1)}, bf16[256,256]{1,0:T(8,128)(2,1)}, u32[]{:S(2)}) copy-start(bf16[256,256]{1,0:T(8,128)(2,1)} %param.21) | copy-start | bytes 393220
  18.2 19.6 %copy-start.14 = (s32[4]{0:T(128)S(1)}, s32[4]{0:T(128)}, u32[]{:S(2)}) copy-start(s32[4]{0:T(128)} %constant.252.clone.1) | copy-start | bytes 52
  18.2 506.1 %all-to-all-start = ((bf16[64,4,64,128]{3,2,1,0:T(8,128)(2,1)}), bf16[64,4,64,128]{3,2,1,0:T(8,128)(2,1)}, u32[]{:S(2)}, u32[]{:S(2)}) async-start(bf16[64,4,64,128]{3,2,1,0:T(8,128)(2,1)} %select_select_fusion), calls=%async_computation | async-start | bytes 8388608 | tf_op jit(solution)/shard_map/all_to_all | solution.py:83
  34.0 489.3 %all-reduce.4.cloned.1.call-start = ((), (), s32[]{:S(2)}) async-start(), calls=%async_computation.3 | async-start | bytes 262144 | tf_op jit(solution)/shard_map/psum | solution.py:16
  35.4 1.7 copy-start.12
  532.5 1.4 copy-start.3
  533.9 1.9 copy-start.5
  538.5 0.8 copy-start.4
  540.3 1.9 copy-start.1
  542.2 2.0 copy-start.2
  545.4 4.3 copy-start.13
  558.9 573.5 %all-to-all-start.1 = ((f32[64,4,64,128]{3,2,1,0:T(8,128)}), f32[64,4,64,128]{3,2,1,0:T(8,128)}, u32[]{:S(2)}, u32[]{:S(2)}) async-start(f32[64,4,64,128]{3,2,1,0:T(8,128)} %fusion.27), calls=%async_computation.1 | async-start | bytes 16777216 | tf_op jit(solution)/shard_map/all_to_all | solution.py:153
  566.6 565.7 %all-reduce.6.cloned.1.call-start = ((), (), s32[]{:S(2)}) async-start(), calls=%async_computation.4 | async-start | bytes 524288 | tf_op jit(solution)/shard_map/psum | solution.py:145
  570.2 676.5 %reduce-scatter.2.cloned.1.call-start = ((), (), s32[]{:S(2)}) async-start(), calls=%async_computation.5 | async-start | bytes 1179648 | tf_op jit(solution)/shard_map/reduce_scatter | solution.py:180
  1132.4 8.6 copy-start.11
  1153.2 1.2 copy-start.6
  1154.5 2.2 copy-start.7
Sparse Core Ops, SparseCore 0:
  37.7 485.5 all-reduce.3
  570.6 561.6 all-reduce.5
  1158.2 88.3 reduce-scatter.1
where the time goes:
time: 1250 us
  waiting for transfers between devices  1130 us (90%)
  other arithmetic  48.1 us (4%)
  local copies, waits for them, and re-layouts  28.5 us (2%)
  starting transfers between devices  23.7 us (2%)
  between operations  13.6 us (1%)
    psum x1, waiting for transfers between devices, body(): global_total = lax.psum(jnp.sum(pair_grads[:, :GLOB], axis=0), 'seq')  557 us
    psum x1, waiting for transfers between devices, from_root(): return lax.psum(jnp.where(mine, value, jnp.zeros_like(value)), axis)  485 us
    reduce_scatter x1, waiting for transfers between devices, body(): lax.psum_scatter(term_rows.astype(jnp.bfloat16), 'head', scatter_dimensio...  88.5 us
  transfers between devices with their start and end apart: 5, of which 3 were waited for; matrix products, arithmetic and copies ran while one was open for 1% of the time, Pallas kernels for 0%

commit v1 on v0

v1 whole, which is shorter than its diff:
```python
import functools
import math

import jax
import jax.numpy as jnp
from jax import lax
from jax.experimental import pallas as pl
from jax.experimental.pallas import tpu as pltpu
from jax.sharding import PartitionSpec as P

HD = 128
BLK = 64
GLOB = 2
RAND = 3
PER = 4
SLOTS = GLOB + 2 + PER * RAND
QUAD = 4
LANES = QUAD * HD
VMEM_LIMIT = 40 * 1024 * 1024


def nt(a, b):
    return lax.dot_general(a, b, (((1,), (1,)), ((), ())), preferred_element_type=jnp.float32)


def nn(a, b):
    return lax.dot_general(a, b, (((1,), (0,)), ((), ())), preferred_element_type=jnp.float32)


def tn(a, b):
    return lax.dot_general(a, b, (((0,), (0,)), ((), ())), preferred_element_type=jnp.float32)


def one_hot(hits):
    return jnp.where(hits, 1.0, 0.0).astype(jnp.bfloat16)


def source_row(order, low):
    return ((order >> 1) & 3) * BLK + (order >> 3) * QUAD + (order & 1) * 2 + low


def pack_kernel(keys_ref, values_ref, out_ref):
    order = lax.broadcasted_iota(jnp.int32, (128, 256), 0)
    row = lax.broadcasted_iota(jnp.int32, (128, 256), 1)
    for low in range(2):
        moved = one_hot(row == source_row(order, low))
        for kind, ref in enumerate((keys_ref, values_ref)):
            rows = nn(moved, ref[...]).astype(jnp.bfloat16)
            for head in range(2):
                at = (2 * head + kind) * 128
                out_ref[at : at + 128, low * HD : (low + 1) * HD] = rows[:, head * HD : (head + 1) * HD]


def pick_kernel(index_ref, table_ref, out_ref):
    index = index_ref[...]
    place = lax.broadcasted_iota(jnp.int32, (index.shape[0], table_ref.shape[0]), 1)
    table = table_ref[...]
    for high in range(2):
        hits = one_hot(place == index * 2 + high)
        out_ref[:, high * 256 : (high + 1) * 256] = nn(hits, table).astype(jnp.bfloat16)


def sum_kernel(index_ref, shares_ref, out_ref):
    place = lax.broadcasted_iota(jnp.int32, (out_ref.shape[0], index_ref.shape[1]), 0)
    total = None
    for high in range(2):
        hits = one_hot(place == index_ref[...] * 2 + high)
        part = nn(hits, shares_ref[:, high * 256 : (high + 1) * 256])
        total = part if total is None else total + part
    out_ref[...] = total.astype(jnp.bfloat16)


def attention_kernel(
    shard_ref, q_ref, k_ref, v_ref, g_ref, remote_ref, dq_ref, dk_ref, dv_ref, shares_ref
):
    scale = 1.0 / math.sqrt(HD)
    first_block = shard_ref[0] * PER
    key_row = lax.broadcasted_iota(jnp.int32, (256, 256), 0)
    q_block = lax.broadcasted_iota(jnp.int32, (256, 256), 1) >> 6
    own_gap = (key_row >> 6) - q_block
    own_mask = (own_gap >= -1) & (own_gap <= 1)
    slot = key_row & (SLOTS - 1)
    offset = slot - (GLOB + 2) - RAND * q_block
    in_window = ((first_block + q_block - slot + 1) & 255) <= 2
    far_mask = (
        ((slot < GLOB) & jnp.logical_not(in_window))
        | ((slot == GLOB) & (q_block == 0))
        | ((slot == GLOB + 1) & (q_block == PER - 1))
        | ((slot >= GLOB + 2) & (offset >= 0) & (offset < RAND))
    )
    q = q_ref[...]
    g = g_ref[...]
    key_parts = [k_ref[...]]
    value_parts = [v_ref[...]]
    for quad in range(QUAD):
        lanes = slice(quad * HD, (quad + 1) * HD)
        key_parts.append(remote_ref[0:256, lanes])
        value_parts.append(remote_ref[256:512, lanes])
    masks = [own_mask] + [far_mask] * QUAD
    weighted = [
        jnp.where(mask, jnp.exp(nt(k, q) * scale), 0.0) for k, mask in zip(key_parts, masks)
    ]
    total = functools.reduce(jnp.add, [jnp.sum(w, axis=0, keepdims=True) for w in weighted])
    inverse = 1.0 / total
    grad_probs = [nt(v, g) for v in value_parts]
    probs = [w * inverse for w in weighted]
    probs_low = [p.astype(jnp.bfloat16) for p in probs]
    delta = functools.reduce(
        jnp.add,
        [
            jnp.sum(p.astype(jnp.float32) * d, axis=0, keepdims=True)
            for p, d in zip(probs_low, grad_probs)
        ],
    )
    grad_low = [(p * (d - delta)).astype(jnp.bfloat16) for p, d in zip(probs, grad_probs)]
    dq = functools.reduce(jnp.add, [tn(k, w) for k, w in zip(key_parts, grad_low)])
    dq_ref[...] = (scale * dq).T.astype(jnp.bfloat16)
    for part in range(QUAD + 1):
        dk = scale * nn(grad_low[part], q)
        dv = nn(probs_low[part], g)
        if part == 0:
            dk_ref[...] = dk
            dv_ref[...] = dv
        else:
            lanes = slice((part - 1) * HD, part * HD)
            shares_ref[0:256, lanes] = dk.astype(jnp.bfloat16)
            shares_ref[256:512, lanes] = dv.astype(jnp.bfloat16)


def project_kernel(dq_ref, dk_ref, dv_ref, back_ref, wq_ref, wk_ref, wv_ref, out_ref, low_k, low_v):
    @pl.when(pl.program_id(0) == 0)
    def _():
        row = lax.broadcasted_iota(jnp.int32, (256, 128), 0)
        order = lax.broadcasted_iota(jnp.int32, (256, 128), 1)
        moved = [one_hot(row == source_row(order, low)) for low in range(2)]
        for kind, (own_ref, low_ref) in enumerate(((dk_ref, low_k), (dv_ref, low_v))):
            for head in range(2):
                at = (2 * head + kind) * 128
                lanes = slice(head * HD, (head + 1) * HD)
                remote = nn(moved[0], back_ref[at : at + 128, 0:HD]) + nn(
                    moved[1], back_ref[at : at + 128, HD : 2 * HD]
                )
                low_ref[:, lanes] = (own_ref[:, lanes] + remote).astype(jnp.bfloat16)

    term = nt(dq_ref[...], wq_ref[...]) + nt(low_k[...], wk_ref[...]) + nt(low_v[...], wv_ref[...])
    out_ref[...] = term.astype(jnp.bfloat16)


def params(**kwargs):
    return pltpu.CompilerParams(vmem_limit_bytes=VMEM_LIMIT, **kwargs)


def shape(dims, dtype=jnp.bfloat16):
    return jax.ShapeDtypeStruct(dims, dtype)


def whole(dims):
    return pl.BlockSpec(dims, lambda *ids: (0,) * len(dims))


def swap(rows, shards, axis):
    parts = rows.reshape(shards, rows.shape[0] // shards, rows.shape[1])
    return lax.all_to_all(parts, axis, split_axis=0, concat_axis=0, tiled=True).reshape(rows.shape)


def body(queries, keys, values, out_grad, random_blocks, w_query, w_key, w_value):
    shards = lax.axis_size("seq")
    groups = lax.axis_size("head")
    total_blocks = shards * PER
    width = 2 * HD
    first = jnp.arange(shards, dtype=jnp.int32)[:, None] * PER
    table = jnp.concatenate(
        [
            jnp.broadcast_to(jnp.arange(GLOB, dtype=jnp.int32)[None], (shards, GLOB)),
            (first - 1) % total_blocks,
            (first + PER) % total_blocks,
            random_blocks.reshape(shards, PER * RAND),
        ],
        axis=1,
    )
    wanted = shards * SLOTS

    packed = pl.pallas_call(
        pack_kernel,
        out_shape=shape((shards * 8, width)),
        compiler_params=params(),
        name="pack",
    )(keys, values)
    stripes = swap(packed, shards, "seq")

    chunk = wanted // 4
    picked = pl.pallas_call(
        pick_kernel,
        grid=(4,),
        in_specs=[pl.BlockSpec((chunk, 1), lambda i: (i, 0)), whole((shards * 8, width))],
        out_specs=pl.BlockSpec((chunk, LANES), lambda i: (i, 0)),
        out_shape=shape((wanted, LANES)),
        compiler_params=params(),
        name="pick",
    )(table.reshape(wanted, 1), stripes)
    remote = swap(picked, shards, "seq")

    by_head = pl.BlockSpec((256, HD), lambda h: (0, h))
    by_head_far = pl.BlockSpec((512, LANES), lambda h: (h, 0))
    query_low, own_key, own_value, shares = pl.pallas_call(
        attention_kernel,
        grid=(2,),
        in_specs=[pl.BlockSpec(memory_space=pltpu.SMEM)] + [by_head] * 4 + [by_head_far],
        out_specs=[by_head, by_head, by_head, by_head_far],
        out_shape=[
            shape((256, width)),
            shape((256, width), jnp.float32),
            shape((256, width), jnp.float32),
            shape((wanted, LANES)),
        ],
        compiler_params=params(),
        name="attention",
    )(
        lax.axis_index("seq").astype(jnp.int32).reshape(1),
        queries,
        keys,
        values,
        out_grad,
        remote,
    )
    returned = swap(shares, shards, "seq")

    summed = pl.pallas_call(
        sum_kernel,
        out_shape=shape((shards * 8, width)),
        compiler_params=params(),
        name="sum_shares",
    )(table.reshape(1, wanted), returned)
    back = swap(summed, shards, "seq")

    out_features = w_query.shape[0]
    per_group = out_features // groups
    w_spec = pl.BlockSpec((per_group, width), lambda i: (i, 0))
    terms = pl.pallas_call(
        project_kernel,
        grid=(groups,),
        in_specs=[
            whole((256, width)),
            whole((256, width)),
            whole((256, width)),
            whole((shards * 8, width)),
            w_spec,
            w_spec,
            w_spec,
        ],
        out_specs=pl.BlockSpec((256, per_group), lambda i: (i, 0)),
        out_shape=shape((groups * 256, per_group)),
        scratch_shapes=[pltpu.VMEM((256, width), jnp.bfloat16)] * 2,
        compiler_params=params(),
        name="project",
    )(query_low, own_key, own_value, back, w_query, w_key, w_value)
    parts = lax.all_to_all(
        terms.reshape(groups, 256, per_group), "head", split_axis=0, concat_axis=0, tiled=True
    )
    return jnp.sum(parts.astype(jnp.float32), axis=0).astype(jnp.bfloat16)


def solution(mesh):
    in_specs = (
        P("seq", "head"),
        P("seq", "head"),
        P("seq", "head"),
        P("seq", "head"),
        P(),
        P(None, "head"),
        P(None, "head"),
        P(None, "head"),
    )
    out_specs = P("seq", "head")
    return jax.shard_map(body, mesh=mesh, in_specs=in_specs, out_specs=out_specs, check_vma=False)
```

time: 1250 us -> 169 us (0.14)
  the two profiles are of different devices: /device:TPU:1 before, /device:TPU:8 now
where the time goes in v1:
time: 169 us; the launch traced here: 168 us
  waiting for transfers between devices  68.7 us (41%)
  blocking collectives  55.7 us (33%)
  starting transfers between devices  25.8 us (15%)
  Pallas kernels  11.2 us (7%)
  local copies, waits for them, and re-layouts  5.53 us (3%)
    all_to_all x3, waiting for transfers between devices, swap(): lax.all_to_all(parts, axis, split_axis=0, concat_axis=0, tiled=True)  68.7 us
    all_to_all x1, blocking collectives, body(): lax.all_to_all(terms.reshape(groups, 256, per_group), 'head', split_axis=...  37.3 us
    all_to_all x3, starting transfers between devices, swap(): lax.all_to_all(parts, axis, split_axis=0, concat_axis=0, tiled=True)  25.8 us
    all_to_all x1, blocking collectives, swap(): lax.all_to_all(parts, axis, split_axis=0, concat_axis=0, tiled=True)  18.3 us
    pallas_call x1, Pallas kernels, body(): pl.pallas_call(attention_kernel, grid=(2,), in_specs=[pl.BlockSpec(memory...  4.31 us
    unnamed x27, local copies, waits for them, and re-layouts  4.21 us
  transfers between devices with their start and end apart: 3, of which 3 were waited for; matrix products, arithmetic and copies ran while one was open for 1% of the time, Pallas kernels for 0%

profile of v1, /device:TPU:8, one launch (start us, length us, event | category | flops | bytes accessed | tf_op | source)
XLA Modules:
  0.0 168.1 jit_solution(13128484296190007257)
XLA Ops:
  0.0 0.0 copy-start.3
  0.0 0.9 copy-done.3
  0.9 0.0 copy-start.5
  0.9 0.9 copy-done.5
  1.8 0.9 pack.1
  2.8 0.0 copy-start.12
  2.8 14.5 %all-to-all-start = ((bf16[64,8,256]{2,1,0:T(8,128)(2,1)}), bf16[64,8,256]{2,1,0:T(8,128)(2,1)S(1)}, u32[]{:S(2)}, u32[]{:S(2)}) async-start(bf16[64,8,256]{2,1,0:T(8,128)(2,1)} %bitcast.1), calls=%async_computation | async-start | bytes 524288 | tf_op jit(solution)/shard_map/all_to_all | solution.py:163
  17.3 0.0 copy-done.12
  17.3 0.1 copy.16
  17.4 0.1 reshape.134
  17.6 0.1 pad_add_fusion
  17.7 0.0 copy-start.11
  17.7 0.3 reshape.146.index_ref
  18.0 0.3 copy-done.11
  18.3 11.7 %all-to-all-done = bf16[64,8,256]{2,1,0:T(8,128)(2,1)S(1)} async-done(((bf16[64,8,256]{2,1,0:T(8,128)(2,1)}), bf16[64,8,256]{2,1,0:T(8,128)(2,1)S(1)}, u32[]{:S(2)}, u32[]{:S(2)}) %all-to-all-start) | async-done | bytes 262176 | tf_op jit(solution)/shard_map/all_to_all | solution.py:163
  30.0 2.5 %pick.1 = bf16[1024,512]{1,0:T(8,128)(2,1)} custom-call(s32[1024,1]{1,0:T(8,128)S(1)} %reshape.146.index_ref, bf16[512,256]{1,0:T(8,128)(2,1)S(1)} %bitcast.13), custom_call_target="tpu_custom_call" | custom-call | tf_op jit(solution)/shard_map/pick/pallas_call | solution.py:192
  32.5 0.0 copy-start.4
  32.5 0.0 copy-start.6
  32.5 0.0 copy-start.9
  32.5 0.0 copy-start.10
  32.5 5.6 %all-to-all-start.1 = ((bf16[64,16,512]{2,1,0:T(8,128)(2,1)}), bf16[64,16,512]{2,1,0:T(8,128)(2,1)S(1)}, u32[]{:S(2)}, u32[]{:S(2)}) async-start(bf16[64,16,512]{2,1,0:T(8,128)(2,1)} %bitcast.3), calls=%async_computation.1 | async-start | bytes 2097152 | tf_op jit(solution)/shard_map/all_to_all | solution.py:163
  38.0 29.1 %all-to-all-done.1 = bf16[64,16,512]{2,1,0:T(8,128)(2,1)S(1)} async-done(((bf16[64,16,512]{2,1,0:T(8,128)(2,1)}), bf16[64,16,512]{2,1,0:T(8,128)(2,1)S(1)}, u32[]{:S(2)}, u32[]{:S(2)}) %all-to-all-start.1) | async-done | bytes 1048608 | tf_op jit(solution)/shard_map/all_to_all | solution.py:163
  67.1 0.0 copy-done.4
  67.1 0.0 copy-done.6
  67.1 0.0 copy-done.9
  67.1 0.0 copy-done.10
  67.1 4.3 %attention.1 = (bf16[256,256]{1,0:T(8,128)(2,1)S(1)}, f32[256,256]{1,0:T(8,128)S(1)}, f32[256,256]{1,0:T(8,128)S(1)}, bf16[1024,512]{1,0:T(8,128)(2,1)}) custom-call(s32[1]{0:T(128)} %bitcast.shard_ref, bf16[256,256]{1,0:T(8,128)(2,1)S(1)} %copy-done.9, bf16[256,256]{1,0:T(8,128)(2,1)S(1)} %copy-done.4, bf16[256,256]{1,0:T(8,128)(2,1)S(1)} %copy-done.6, ...), custom_call_target="tpu_custom_call" | custom-call | tf_op jit(solution)/shard_map/attention/pallas_call | solution.py:205
  71.4 0.0 copy-start.7
  71.4 0.7 copy-done.7
  72.1 0.0 copy-start.1
  72.1 5.8 %all-to-all-start.2 = ((bf16[64,16,512]{2,1,0:T(8,128)(2,1)}), bf16[64,16,512]{2,1,0:T(8,128)(2,1)S(1)}, u32[]{:S(2)}, u32[]{:S(2)}) async-start(bf16[64,16,512]{2,1,0:T(8,128)(2,1)} %bitcast.5), calls=%async_computation.2 | async-start | bytes 2097152 | tf_op jit(solution)/shard_map/all_to_all | solution.py:163
  77.9 0.0 copy-start
  77.9 0.9 reshape.140.index_ref
  78.8 28.0 %all-to-all-done.2 = bf16[64,16,512]{2,1,0:T(8,128)(2,1)S(1)} async-done(((bf16[64,16,512]{2,1,0:T(8,128)(2,1)}), bf16[64,16,512]{2,1,0:T(8,128)(2,1)S(1)}, u32[]{:S(2)}, u32[]{:S(2)}) %all-to-all-start.2) | async-done | bytes 1048608 | tf_op jit(solution)/shard_map/all_to_all | solution.py:163
  106.8 0.7 sum_shares.1
  107.6 0.0 copy-start.8
  107.6 18.3 %all_to_all.25 = bf16[64,8,256]{2,1,0:T(8,128)(2,1)S(1)} all-to-all(bf16[64,8,256]{2,1,0:T(8,128)(2,1)S(1)} %bitcast.15), channel_id=1, replica_groups=mesh['seq'=64,'head'=8] {'seq'}, dimensions={0} | all-to-all | bytes 524288 | tf_op jit(solution)/shard_map/all_to_all | solution.py:163
  125.9 0.0 copy-done.1
  125.9 0.0 copy-done
  125.9 0.0 copy-done.8
  125.9 0.0 copy-start.2
  125.9 1.2 copy-done.2
  127.1 2.8 %project.1 = bf16[2048,256]{1,0:T(8,128)(2,1)S(1)} custom-call(bf16[256,256]{1,0:T(8,128)(2,1)S(1)} %get-tuple-element.9.dq_ref, f32[256,256]{1,0:T(8,128)S(1)} %get-tuple-element.10.dk_ref, f32[256,256]{1,0:T(8,128)S(1)} %copy-done.8, bf16[512,256]{1,0:T(8,128)(2,1)S(1)} %bitcast.14, bf16[2048,256]{1,0:T(8,128)(2,1)S(1)} %copy-done, ...), custom_call_target="tpu_custom_call" | custom-call | tf_op jit(solution)/shard_map/project/pallas_call | solution.py:239
  129.9 37.3 %all_to_all.26 = bf16[8,256,256]{2,1,0:T(8,128)(2,1)S(1)} all-to-all(bf16[8,256,256]{2,1,0:T(8,128)(2,1)S(1)} %bitcast.10), channel_id=1, replica_groups=mesh['seq'=64,'head'=8] {'head'}, dimensions={0} | all-to-all | bytes 2097152 | tf_op jit(solution)/shard_map/all_to_all | solution.py:257
  167.3 0.8 reduce_sum.12
  (2 shorter events, 0.0 us)
Async XLA Ops:
  0.0 0.9 copy-start.3
  0.9 0.9 copy-start.5
  2.8 14.5 %copy-start.12 = (s32[256,3]{0,1:T(4,128)S(1)}, s32[256,3]{0,1:T(4,128)}, u32[]{:S(2)}) copy-start(s32[256,3]{0,1:T(4,128)} %param.12) | copy-start | bytes 9220
  2.8 27.2 %all-to-all-start = ((bf16[64,8,256]{2,1,0:T(8,128)(2,1)}), bf16[64,8,256]{2,1,0:T(8,128)(2,1)S(1)}, u32[]{:S(2)}, u32[]{:S(2)}) async-start(bf16[64,8,256]{2,1,0:T(8,128)(2,1)} %bitcast.1), calls=%async_computation | async-start | bytes 524288 | tf_op jit(solution)/shard_map/all_to_all | solution.py:163
  17.7 0.6 copy-start.11
  32.5 34.6 %copy-start.4 = (bf16[256,256]{1,0:T(8,128)(2,1)S(1)}, bf16[256,256]{1,0:T(8,128)(2,1)}, u32[]{:S(2)}) copy-start(bf16[256,256]{1,0:T(8,128)(2,1)} %k_ref.1) | copy-start | bytes 393220
  32.5 34.6 %copy-start.6 = (bf16[256,256]{1,0:T(8,128)(2,1)S(1)}, bf16[256,256]{1,0:T(8,128)(2,1)}, u32[]{:S(2)}) copy-start(bf16[256,256]{1,0:T(8,128)(2,1)} %v_ref.1) | copy-start | bytes 393220
  32.5 34.6 %copy-start.9 = (bf16[256,256]{1,0:T(8,128)(2,1)S(1)}, bf16[256,256]{1,0:T(8,128)(2,1)}, u32[]{:S(2)}) copy-start(bf16[256,256]{1,0:T(8,128)(2,1)} %q_ref.1) | copy-start | bytes 393220
  32.5 34.6 %copy-start.10 = (bf16[256,256]{1,0:T(8,128)(2,1)S(1)}, bf16[256,256]{1,0:T(8,128)(2,1)}, u32[]{:S(2)}) copy-start(bf16[256,256]{1,0:T(8,128)(2,1)} %g_ref.1) | copy-start | bytes 393220
  32.5 34.6 %all-to-all-start.1 = ((bf16[64,16,512]{2,1,0:T(8,128)(2,1)}), bf16[64,16,512]{2,1,0:T(8,128)(2,1)S(1)}, u32[]{:S(2)}, u32[]{:S(2)}) async-start(bf16[64,16,512]{2,1,0:T(8,128)(2,1)} %bitcast.3), calls=%async_computation.1 | async-start | bytes 2097152 | tf_op jit(solution)/shard_map/all_to_all | solution.py:163
  71.4 0.7 copy-start.7
  72.1 53.8 %copy-start.1 = (bf16[2048,256]{1,0:T(8,128)(2,1)S(1)}, bf16[2048,256]{1,0:T(8,128)(2,1)}, u32[]{:S(2)}) copy-start(bf16[2048,256]{1,0:T(8,128)(2,1)} %wk_ref.1) | copy-start | bytes 3145732
  72.1 34.7 %all-to-all-start.2 = ((bf16[64,16,512]{2,1,0:T(8,128)(2,1)}), bf16[64,16,512]{2,1,0:T(8,128)(2,1)S(1)}, u32[]{:S(2)}, u32[]{:S(2)}) async-start(bf16[64,16,512]{2,1,0:T(8,128)(2,1)} %bitcast.5), calls=%async_computation.2 | async-start | bytes 2097152 | tf_op jit(solution)/shard_map/all_to_all | solution.py:163
  77.9 48.0 %copy-start = (bf16[2048,256]{1,0:T(8,128)(2,1)S(1)}, bf16[2048,256]{1,0:T(8,128)(2,1)}, u32[]{:S(2)}) copy-start(bf16[2048,256]{1,0:T(8,128)(2,1)} %wq_ref.1) | copy-start | bytes 3145732
  107.6 18.4 %copy-start.8 = (f32[256,256]{1,0:T(8,128)S(1)}, f32[256,256]{1,0:T(8,128)}, u32[]{:S(2)}) copy-start(f32[256,256]{1,0:T(8,128)} %copy-done.7) | copy-start | bytes 786436
  125.9 1.2 copy-start.2

commit v2 on v1

--- a/solution.py
+++ b/solution.py
@@ -6,6 +6,7 @@
 from jax import lax
 from jax.experimental import pallas as pl
 from jax.experimental.pallas import tpu as pltpu
+from jax.sharding import Mesh
 from jax.sharding import PartitionSpec as P
 
 HD = 128
@@ -16,6 +17,7 @@
 SLOTS = GLOB + 2 + PER * RAND
 QUAD = 4
 LANES = QUAD * HD
+X_SIZE = 4
 VMEM_LIMIT = 40 * 1024 * 1024
 
 
@@ -127,23 +129,37 @@
             shares_ref[256:512, lanes] = dv.astype(jnp.bfloat16)
 
 
-def project_kernel(dq_ref, dk_ref, dv_ref, back_ref, wq_ref, wk_ref, wv_ref, out_ref, low_k, low_v):
-    @pl.when(pl.program_id(0) == 0)
-    def _():
-        row = lax.broadcasted_iota(jnp.int32, (256, 128), 0)
-        order = lax.broadcasted_iota(jnp.int32, (256, 128), 1)
-        moved = [one_hot(row == source_row(order, low)) for low in range(2)]
-        for kind, (own_ref, low_ref) in enumerate(((dk_ref, low_k), (dv_ref, low_v))):
-            for head in range(2):
-                at = (2 * head + kind) * 128
-                lanes = slice(head * HD, (head + 1) * HD)
-                remote = nn(moved[0], back_ref[at : at + 128, 0:HD]) + nn(
-                    moved[1], back_ref[at : at + 128, HD : 2 * HD]
-                )
-                low_ref[:, lanes] = (own_ref[:, lanes] + remote).astype(jnp.bfloat16)
-
-    term = nt(dq_ref[...], wq_ref[...]) + nt(low_k[...], wk_ref[...]) + nt(low_v[...], wv_ref[...])
-    out_ref[...] = term.astype(jnp.bfloat16)
+def unpack_kernel(dk_ref, dv_ref, back_ref, out_ref):
+    row = lax.broadcasted_iota(jnp.int32, (256, 128), 0)
+    order = lax.broadcasted_iota(jnp.int32, (256, 128), 1)
+    moved = [one_hot(row == source_row(order, low)) for low in range(2)]
+    for kind, own_ref in enumerate((dk_ref, dv_ref)):
+        for head in range(2):
+            at = (2 * head + kind) * 128
+            lanes = slice(head * HD, (head + 1) * HD)
+            remote = nn(moved[0], back_ref[at : at + 128, 0:HD]) + nn(
+                moved[1], back_ref[at : at + 128, HD : 2 * HD]
+            )
+            to = kind * 256 + head * HD
+            out_ref[:, to : to + HD] = (own_ref[:, lanes] + remote).astype(jnp.bfloat16)
+
+
+def project_kernel(where_ref, dq_ref, dkv_ref, *rest):
+    weight_refs, (mine_ref, theirs_ref) = rest[:X_SIZE], rest[X_SIZE:]
+    half, x = where_ref[0], where_ref[1]
+
+    def term(which):
+        total = None
+        for shift, w_ref in enumerate(weight_refs):
+            group = (x - shift) & (X_SIZE - 1)
+            parts = (dq_ref[group], dkv_ref[group, :, 0:256], dkv_ref[group, :, 256:512])
+            for kind, part in enumerate(parts):
+                part = nt(part, w_ref[kind, which])
+                total = part if total is None else total + part
+        return total
+
+    theirs_ref[...] = term(1 - half).astype(jnp.bfloat16)
+    mine_ref[...] = term(half)
 
 
 def params(**kwargs):
@@ -165,7 +181,15 @@
 
 def body(queries, keys, values, out_grad, random_blocks, w_query, w_key, w_value):
     shards = lax.axis_size("seq")
-    groups = lax.axis_size("head")
+    half = lax.axis_index("h")
+    x = lax.axis_index("x")
+    by_feature = jnp.stack([w_query, w_key, w_value]).reshape(3, 2, X_SIZE, 256, 256)
+    weights = []
+    for shift in range(X_SIZE):
+        cut = lax.dynamic_index_in_dim(by_feature, (x + shift) % X_SIZE, 2, keepdims=False)
+        if shift:
+            cut = lax.ppermute(cut, "x", [(i, (i + shift) % X_SIZE) for i in range(X_SIZE)])
+        weights.append(cut)
     total_blocks = shards * PER
     width = 2 * HD
     first = jnp.arange(shards, dtype=jnp.int32)[:, None] * PER
@@ -233,43 +257,31 @@
     )(table.reshape(1, wanted), returned)
     back = swap(summed, shards, "seq")
 
-    out_features = w_query.shape[0]
-    per_group = out_features // groups
-    w_spec = pl.BlockSpec((per_group, width), lambda i: (i, 0))
-    terms = pl.pallas_call(
+    key_value_low = pl.pallas_call(
+        unpack_kernel,
+        out_shape=shape((256, 2 * width)),
+        compiler_params=params(),
+        name="unpack",
+    )(own_key, own_value, back)
+
+    all_query = lax.all_gather(query_low, "x")
+    all_key_value = lax.all_gather(key_value_low, "x")
+    mine, theirs = pl.pallas_call(
         project_kernel,
-        grid=(groups,),
-        in_specs=[
-            whole((256, width)),
-            whole((256, width)),
-            whole((256, width)),
-            whole((shards * 8, width)),
-            w_spec,
-            w_spec,
-            w_spec,
-        ],
-        out_specs=pl.BlockSpec((256, per_group), lambda i: (i, 0)),
-        out_shape=shape((groups * 256, per_group)),
-        scratch_shapes=[pltpu.VMEM((256, width), jnp.bfloat16)] * 2,
+        in_specs=[pl.BlockSpec(memory_space=pltpu.SMEM)] + [pl.BlockSpec()] * (2 + X_SIZE),
+        out_shape=[shape((256, width), jnp.float32), shape((256, width))],
         compiler_params=params(),
         name="project",
-    )(query_low, own_key, own_value, back, w_query, w_key, w_value)
-    parts = lax.all_to_all(
-        terms.reshape(groups, 256, per_group), "head", split_axis=0, concat_axis=0, tiled=True
-    )
-    return jnp.sum(parts.astype(jnp.float32), axis=0).astype(jnp.bfloat16)
+    )(jnp.stack([half, x]).astype(jnp.int32), all_query, all_key_value, *weights)
+    halves = lax.all_gather(theirs, "h")
+    other = lax.dynamic_index_in_dim(halves, 1 - half, 0, keepdims=False)
+    return (mine + other.astype(jnp.float32)).astype(jnp.bfloat16)
 
 
 def solution(mesh):
-    in_specs = (
-        P("seq", "head"),
-        P("seq", "head"),
-        P("seq", "head"),
-        P("seq", "head"),
-        P(),
-        P(None, "head"),
-        P(None, "head"),
-        P(None, "head"),
-    )
-    out_specs = P("seq", "head")
-    return jax.shard_map(body, mesh=mesh, in_specs=in_specs, out_specs=out_specs, check_vma=False)
+    shards = mesh.shape["seq"]
+    split = Mesh(mesh.devices.reshape(shards, -1, X_SIZE), ("seq", "h", "x"))
+    head = ("h", "x")
+    by_token = P("seq", head)
+    in_specs = (by_token,) * 4 + (P(),) + (P(None, head),) * 3
+    return jax.shard_map(body, mesh=split, in_specs=in_specs, out_specs=by_token, check_vma=False)

time: 169 us -> 217 us (1.28)
  the two profiles are of different devices: /device:TPU:8 before, /device:TPU:1 now
where the time goes in v2:
time: 217 us; the launch traced here: 215 us
  blocking collectives  75.4 us (35%)
  waiting for transfers between devices  69.2 us (32%)
  starting transfers between devices  36.8 us (17%)
  between operations  13.6 us (6%)
  Pallas kernels  11.6 us (5%)
  local copies, waits for them, and re-layouts  5.78 us (3%)
  other arithmetic  2.76 us (1%)
    all_to_all x3, waiting for transfers between devices, swap(): lax.all_to_all(parts, axis, split_axis=0, concat_axis=0, tiled=True)  69.1 us
    all_gather x1, blocking collectives, body(): all_query = lax.all_gather(query_low, 'x')  46.1 us
    all_to_all x3, starting transfers between devices, swap(): lax.all_to_all(parts, axis, split_axis=0, concat_axis=0, tiled=True)  26.2 us
    all_to_all x1, blocking collectives, swap(): lax.all_to_all(parts, axis, split_axis=0, concat_axis=0, tiled=True)  19.5 us
    ppermute x3, starting transfers between devices, body(): lax.ppermute(cut, 'x', [(i, (i + shift) % X_SIZE) for i in range(X_SIZE)])  10.5 us
    all_gather x1, blocking collectives, body(): halves = lax.all_gather(theirs, 'h')  9.91 us
  transfers between devices with their start and end apart: 7, of which 3 were waited for; matrix products, arithmetic and copies ran while one was open for 2% of the time, Pallas kernels for 0%

profile of v2, /device:TPU:1, one launch (start us, length us, event | category | flops | bytes accessed | tf_op | source)
XLA Modules:
  0.0 215.1 jit_solution(393284504436499191)
XLA Ops:
  6.5 0.0 copy-start.1
  6.5 0.9 copy-done.1
  7.4 0.0 copy-start.3
  7.4 0.9 copy-done.3
  8.3 0.0 copy-start.2
  8.3 0.0 copy-start.4
  8.3 0.0 copy-start.5
  8.4 0.0 copy-start.6
  8.4 0.9 pack.1
  9.3 15.4 %all-to-all-start = ((bf16[64,8,256]{2,1,0:T(8,128)(2,1)}), bf16[64,8,256]{2,1,0:T(8,128)(2,1)S(1)}, u32[]{:S(2)}, u32[]{:S(2)}) async-start(bf16[64,8,256]{2,1,0:T(8,128)(2,1)} %bitcast.3), calls=%async_computation | async-start | bytes 524288 | tf_op jit(solution)/shard_map/all_to_all | solution.py:179
  24.7 0.8 copy.25
  25.5 0.1 reshape.140
  25.7 0.1 pad_add_fusion
  25.8 0.3 reshape.155.index_ref
  26.1 12.2 %all-to-all-done = bf16[64,8,256]{2,1,0:T(8,128)(2,1)S(1)} async-done(((bf16[64,8,256]{2,1,0:T(8,128)(2,1)}), bf16[64,8,256]{2,1,0:T(8,128)(2,1)S(1)}, u32[]{:S(2)}, u32[]{:S(2)}) %all-to-all-start) | async-done | bytes 262176 | tf_op jit(solution)/shard_map/all_to_all | solution.py:179
  38.2 2.5 %pick.1 = bf16[1024,512]{1,0:T(8,128)(2,1)} custom-call(s32[1024,1]{1,0:T(8,128)S(1)} %reshape.155.index_ref, bf16[512,256]{1,0:T(8,128)(2,1)S(1)} %bitcast.40), custom_call_target="tpu_custom_call" | custom-call | tf_op jit(solution)/shard_map/pick/pallas_call | solution.py:216
  40.7 4.6 %all-to-all-start.1 = ((bf16[64,16,512]{2,1,0:T(8,128)(2,1)}), bf16[64,16,512]{2,1,0:T(8,128)(2,1)S(1)}, u32[]{:S(2)}, u32[]{:S(2)}) async-start(bf16[64,16,512]{2,1,0:T(8,128)(2,1)} %bitcast.5), calls=%async_computation.1 | async-start | bytes 2097152 | tf_op jit(solution)/shard_map/all_to_all | solution.py:179
  45.3 28.6 %all-to-all-done.1 = bf16[64,16,512]{2,1,0:T(8,128)(2,1)S(1)} async-done(((bf16[64,16,512]{2,1,0:T(8,128)(2,1)}), bf16[64,16,512]{2,1,0:T(8,128)(2,1)S(1)}, u32[]{:S(2)}, u32[]{:S(2)}) %all-to-all-start.1) | async-done | bytes 1048608 | tf_op jit(solution)/shard_map/all_to_all | solution.py:179
  73.9 0.0 copy-done.2
  73.9 0.0 copy-done.4
  73.9 0.0 copy-done.5
  73.9 0.0 copy-done.6
  73.9 4.3 %attention.1 = (bf16[256,256]{1,0:T(8,128)(2,1)S(1)}, f32[256,256]{1,0:T(8,128)S(1)}, f32[256,256]{1,0:T(8,128)S(1)}, bf16[1024,512]{1,0:T(8,128)(2,1)}) custom-call(s32[1]{0:T(128)} %bitcast.2.shard_ref, bf16[256,256]{1,0:T(8,128)(2,1)S(1)} %copy-done.5, bf16[256,256]{1,0:T(8,128)(2,1)S(1)} %copy-done.2, bf16[256,256]{1,0:T(8,128)(2,1)S(1)} %copy-done.4, ...), custom_call_target="tpu_custom_call" | custom-call | tf_op jit(solution)/shard_map/attention/pallas_call | solution.py:229
  78.2 0.0 copy-start.7
  78.2 6.2 %all-to-all-start.2 = ((bf16[64,16,512]{2,1,0:T(8,128)(2,1)}), bf16[64,16,512]{2,1,0:T(8,128)(2,1)S(1)}, u32[]{:S(2)}, u32[]{:S(2)}) async-start(bf16[64,16,512]{2,1,0:T(8,128)(2,1)} %bitcast.8), calls=%async_computation.2 | async-start | bytes 2097152 | tf_op jit(solution)/shard_map/all_to_all | solution.py:179
  84.5 0.0 all-gather.5.cloned.1.call-start
  84.5 0.1 reshape.146.index_ref
  84.6 28.4 %all-to-all-done.2 = bf16[64,16,512]{2,1,0:T(8,128)(2,1)S(1)} async-done(((bf16[64,16,512]{2,1,0:T(8,128)(2,1)}), bf16[64,16,512]{2,1,0:T(8,128)(2,1)S(1)}, u32[]{:S(2)}, u32[]{:S(2)}) %all-to-all-start.2) | async-done | bytes 1048608 | tf_op jit(solution)/shard_map/all_to_all | solution.py:179
  113.0 0.7 sum_shares.1
  113.7 19.5 %all_to_all.20 = bf16[64,8,256]{2,1,0:T(8,128)(2,1)S(1)} all-to-all(bf16[64,8,256]{2,1,0:T(8,128)(2,1)S(1)} %bitcast.41), channel_id=1, replica_groups=mesh['seq'=64,'h'=2,'x'=4] {'seq'}, dimensions={0} | all-to-all | bytes 524288 | tf_op jit(solution)/shard_map/all_to_all | solution.py:179
  133.2 1.0 unpack.1
  134.2 0.0 all-gather.5.cloned.1.call-update
  134.2 0.0 copy-done.7
  134.2 1.9 pad_maximum_fusion
  136.1 1.4 dynamic-slice_bitcast_fusion
  137.6 3.1 %collective-permute-start = (bf16[3,2,256,256]{3,2,1,0:T(8,128)(2,1)}, bf16[3,2,256,256]{3,2,1,0:T(8,128)(2,1)S(1)}, u32[]{:S(2)}, u32[]{:S(2)}) collective-permute-start(bf16[3,2,256,256]{3,2,1,0:T(8,128)(2,1)} %get-tuple-element.19), channel_id=1, source_target_pairs={{0,1},{1,2},{2,3},{3,0},{4,5},{5,6},{6,7},{7,4},{8,9},{9,10},{10,1... | collective-permute-start | bytes 2359304 | tf_op jit(solution)/shard_map/ppermute | solution.py:191
  140.7 4.4 %collective-permute-start.1 = (bf16[3,2,256,256]{3,2,1,0:T(8,128)(2,1)}, bf16[3,2,256,256]{3,2,1,0:T(8,128)(2,1)S(1)}, u32[]{:S(2)}, u32[]{:S(2)}) collective-permute-start(bf16[3,2,256,256]{3,2,1,0:T(8,128)(2,1)} %get-tuple-element.18), channel_id=1, source_target_pairs={{0,2},{1,3},{2,0},{3,1},{4,6},{5,7},{6,4},{7,5},{8,10},{9,11},{10,... | collective-permute-start | bytes 2359304 | tf_op jit(solution)/shard_map/ppermute | solution.py:191
  145.1 3.1 %collective-permute-start.2 = (bf16[3,2,256,256]{3,2,1,0:T(8,128)(2,1)}, bf16[3,2,256,256]{3,2,1,0:T(8,128)(2,1)}, u32[]{:S(2)}, u32[]{:S(2)}) collective-permute-start(bf16[3,2,256,256]{3,2,1,0:T(8,128)(2,1)} %get-tuple-element.17), channel_id=1, source_target_pairs={{0,3},{1,0},{2,1},{3,2},{4,7},{5,4},{6,5},{7,6},{8,11},{9,8},{10,9... | collective-permute-start | bytes 2359304 | tf_op jit(solution)/shard_map/ppermute | solution.py:191
  148.1 0.1 pad_add_fusion.1.where_ref
  148.2 46.1 %all-gather = bf16[1024,256]{1,0:T(8,128)(2,1)S(1)} all-gather(bf16[256,256]{1,0:T(8,128)(2,1)S(1)} %get-tuple-element.11), channel_id=2, replica_groups=mesh['seq'=64,'h'=2,'x'=4] {'x'}, dimensions={0}, use_global_device_ids=true | all-gather | bytes 655360 | tf_op jit(solution)/shard_map/all_gather | solution.py:267
  194.3 0.0 collective-permute-done.rest_1_
  194.3 0.0 collective-permute-done.1.rest_2_
  194.3 0.0 collective-permute-done.2.rest_3_
  194.3 0.0 all-gather.5.cloned.1.call-done
  194.3 0.0 copy-start
  194.3 1.2 copy-done
  195.5 2.1 project.1
  197.7 9.9 %all-gather.2 = bf16[512,256]{1,0:T(8,128)(2,1)S(1)} all-gather(bf16[256,256]{1,0:T(8,128)(2,1)S(1)} %get-tuple-element.16), channel_id=4, replica_groups=mesh['seq'=64,'h'=2,'x'=4] {'h'}, dimensions={0}, use_global_device_ids=true | all-gather | bytes 393216 | tf_op jit(solution)/shard_map/all_gather | solution.py:276
  207.6 0.7 fusion
  (2 shorter events, 0.0 us)
Async XLA Ops:
  6.5 0.9 copy-start.1
  7.4 0.9 copy-start.3
  8.3 65.6 %copy-start.2 = (bf16[256,256]{1,0:T(8,128)(2,1)S(1)}, bf16[256,256]{1,0:T(8,128)(2,1)}, u32[]{:S(2)}) copy-start(bf16[256,256]{1,0:T(8,128)(2,1)} %k_ref.1) | copy-start | bytes 393220
  8.3 65.6 %copy-start.4 = (bf16[256,256]{1,0:T(8,128)(2,1)S(1)}, bf16[256,256]{1,0:T(8,128)(2,1)}, u32[]{:S(2)}) copy-start(bf16[256,256]{1,0:T(8,128)(2,1)} %v_ref.1) | copy-start | bytes 393220
  8.3 65.6 %copy-start.5 = (bf16[256,256]{1,0:T(8,128)(2,1)S(1)}, bf16[256,256]{1,0:T(8,128)(2,1)}, u32[]{:S(2)}) copy-start(bf16[256,256]{1,0:T(8,128)(2,1)} %q_ref.1) | copy-start | bytes 393220
  8.4 65.6 %copy-start.6 = (bf16[256,256]{1,0:T(8,128)(2,1)S(1)}, bf16[256,256]{1,0:T(8,128)(2,1)}, u32[]{:S(2)}) copy-start(bf16[256,256]{1,0:T(8,128)(2,1)} %g_ref.1) | copy-start | bytes 393220
  9.3 28.9 %all-to-all-start = ((bf16[64,8,256]{2,1,0:T(8,128)(2,1)}), bf16[64,8,256]{2,1,0:T(8,128)(2,1)S(1)}, u32[]{:S(2)}, u32[]{:S(2)}) async-start(bf16[64,8,256]{2,1,0:T(8,128)(2,1)} %bitcast.3), calls=%async_computation | async-start | bytes 524288 | tf_op jit(solution)/shard_map/all_to_all | solution.py:179
  40.7 33.2 %all-to-all-start.1 = ((bf16[64,16,512]{2,1,0:T(8,128)(2,1)}), bf16[64,16,512]{2,1,0:T(8,128)(2,1)S(1)}, u32[]{:S(2)}, u32[]{:S(2)}) async-start(bf16[64,16,512]{2,1,0:T(8,128)(2,1)} %bitcast.5), calls=%async_computation.1 | async-start | bytes 2097152 | tf_op jit(solution)/shard_map/all_to_all | solution.py:179
  78.2 56.0 %copy-start.7 = (bf16[2048,256]{1,0:T(8,128)(2,1)S(1)}, bf16[2048,256]{1,0:T(8,128)(2,1)}, u32[]{:S(2)}) copy-start(bf16[2048,256]{1,0:T(8,128)(2,1)} %param.15) | copy-start | bytes 3145732
  78.2 34.7 %all-to-all-start.2 = ((bf16[64,16,512]{2,1,0:T(8,128)(2,1)}), bf16[64,16,512]{2,1,0:T(8,128)(2,1)S(1)}, u32[]{:S(2)}, u32[]{:S(2)}) async-start(bf16[64,16,512]{2,1,0:T(8,128)(2,1)} %bitcast.8), calls=%async_computation.2 | async-start | bytes 2097152 | tf_op jit(solution)/shard_map/all_to_all | solution.py:179
  84.5 109.8 %all-gather.5.cloned.1.call-start = ((), (), s32[]{:S(2)}) async-start(), calls=%async_computation.4 | async-start | bytes 1310720 | tf_op jit(solution)/shard_map/all_gather | solution.py:268
  137.6 56.7 %collective-permute-start = (bf16[3,2,256,256]{3,2,1,0:T(8,128)(2,1)}, bf16[3,2,256,256]{3,2,1,0:T(8,128)(2,1)S(1)}, u32[]{:S(2)}, u32[]{:S(2)}) collective-permute-start(bf16[3,2,256,256]{3,2,1,0:T(8,128)(2,1)} %get-tuple-element.19), channel_id=1, source_target_pairs={{0,1},{1,2},{2,3},{3,0},{4,5},{5,6},{6,7},{7,4},{8,9},{9,10},{10,1... | collective-permute-start | bytes 2359304 | tf_op jit(solution)/shard_map/ppermute | solution.py:191
  140.7 53.6 %collective-permute-start.1 = (bf16[3,2,256,256]{3,2,1,0:T(8,128)(2,1)}, bf16[3,2,256,256]{3,2,1,0:T(8,128)(2,1)S(1)}, u32[]{:S(2)}, u32[]{:S(2)}) collective-permute-start(bf16[3,2,256,256]{3,2,1,0:T(8,128)(2,1)} %get-tuple-element.18), channel_id=1, source_target_pairs={{0,2},{1,3},{2,0},{3,1},{4,6},{5,7},{6,4},{7,5},{8,10},{9,11},{10,... | collective-permute-start | bytes 2359304 | tf_op jit(solution)/shard_map/ppermute | solution.py:191
  145.1 49.2 %collective-permute-start.2 = (bf16[3,2,256,256]{3,2,1,0:T(8,128)(2,1)}, bf16[3,2,256,256]{3,2,1,0:T(8,128)(2,1)}, u32[]{:S(2)}, u32[]{:S(2)}) collective-permute-start(bf16[3,2,256,256]{3,2,1,0:T(8,128)(2,1)} %get-tuple-element.17), channel_id=1, source_target_pairs={{0,3},{1,0},{2,1},{3,2},{4,7},{5,4},{6,5},{7,6},{8,11},{9,8},{10,9... | collective-permute-start | bytes 2359304 | tf_op jit(solution)/shard_map/ppermute | solution.py:191
  194.3 1.2 copy-start
Sparse Core Ops, SparseCore 0:
  134.3 41.3 all-gather.4

commit v3 on v1

v3 whole, which is shorter than its diff:
```python
import functools
import math

import jax
import jax.numpy as jnp
from jax import lax
from jax.experimental import pallas as pl
from jax.experimental.pallas import tpu as pltpu
from jax.sharding import Mesh
from jax.sharding import PartitionSpec as P

HD = 128
BLK = 64
GLOB = 2
RAND = 3
PER = 4
SLOTS = GLOB + 2 + PER * RAND
X_SIZE = 4
VMEM_LIMIT = 40 * 1024 * 1024


def nt(a, b):
    return lax.dot_general(a, b, (((1,), (1,)), ((), ())), preferred_element_type=jnp.float32)


def nn(a, b):
    return lax.dot_general(a, b, (((1,), (0,)), ((), ())), preferred_element_type=jnp.float32)


def tn(a, b):
    return lax.dot_general(a, b, (((0,), (0,)), ((), ())), preferred_element_type=jnp.float32)


def one_hot(hits):
    return jnp.where(hits, 1.0, 0.0).astype(jnp.bfloat16)


def iotas(*dims):
    return [lax.broadcasted_iota(jnp.int32, dims, axis) for axis in range(len(dims))]


def pack_kernel(keys_ref, values_ref, out_ref):
    to, row = iotas(512, 256)
    source = (to & 3) * BLK + (to >> 3)
    here = row == source
    is_value = (to & 4) != 0
    rows = nn(one_hot(here & jnp.logical_not(is_value)), keys_ref[...])
    rows = rows + nn(one_hot(here & is_value), values_ref[...])
    out_ref[...] = rows.astype(jnp.bfloat16)


def pick_kernel(place_ref, table_ref, out_ref):
    place = place_ref[...]
    _, row = iotas(place.shape[0], table_ref.shape[0])
    table = table_ref[...]
    for kind in range(2):
        hits = one_hot(row == place + 4 * kind)
        out_ref[:, kind * 256 : (kind + 1) * 256] = nn(hits, table).astype(jnp.bfloat16)


def attention_kernel(
    where_ref, q_ref, k_ref, v_ref, g_ref, remote_ref, dq_ref, dk_ref, dv_ref, shares_ref
):
    scale = 1.0 / math.sqrt(HD)
    first_block = where_ref[0] * PER
    key_row, q_row = iotas(256, 256)
    q_block = q_row >> 6
    own_gap = (key_row >> 6) - q_block
    own_mask = (own_gap >= -1) & (own_gap <= 1)
    slot = key_row & (SLOTS - 1)
    offset = slot - (GLOB + 2) - RAND * q_block
    in_window = ((first_block + q_block - slot + 1) & 255) <= 2
    far_mask = (
        ((slot < GLOB) & jnp.logical_not(in_window))
        | ((slot == GLOB) & (q_block == 0))
        | ((slot == GLOB + 1) & (q_block == PER - 1))
        | ((slot >= GLOB + 2) & (offset >= 0) & (offset < RAND))
    )
    for head in range(2):
        lanes = slice(head * HD, (head + 1) * HD)
        value_lanes = slice(256 + head * HD, 256 + (head + 1) * HD)
        q = q_ref[:, lanes]
        g = g_ref[:, lanes]
        far_rows = [slice(at, at + 256) for at in range(0, remote_ref.shape[0], 256)]
        key_parts = [k_ref[:, lanes]] + [remote_ref[rows, lanes] for rows in far_rows]
        value_parts = [v_ref[:, lanes]] + [remote_ref[rows, value_lanes] for rows in far_rows]
        masks = [own_mask] + [far_mask] * len(far_rows)
        weighted = [
            jnp.where(mask, jnp.exp(nt(k, q) * scale), 0.0) for k, mask in zip(key_parts, masks)
        ]
        total = functools.reduce(jnp.add, [jnp.sum(w, axis=0, keepdims=True) for w in weighted])
        inverse = 1.0 / total
        grad_probs = [nt(v, g) for v in value_parts]
        probs = [w * inverse for w in weighted]
        probs_low = [p.astype(jnp.bfloat16) for p in probs]
        delta = functools.reduce(
            jnp.add,
            [
                jnp.sum(p.astype(jnp.float32) * d, axis=0, keepdims=True)
                for p, d in zip(probs_low, grad_probs)
            ],
        )
        grad_low = [(p * (d - delta)).astype(jnp.bfloat16) for p, d in zip(probs, grad_probs)]
        dq = functools.reduce(jnp.add, [tn(k, w) for k, w in zip(key_parts, grad_low)])
        dq_ref[:, lanes] = (scale * dq).T.astype(jnp.bfloat16)
        for part in range(len(masks)):
            dk = (scale * nn(grad_low[part], q)).astype(jnp.bfloat16)
            dv = nn(probs_low[part], g).astype(jnp.bfloat16)
            if part == 0:
                dk_ref[:, lanes] = dk
                dv_ref[:, lanes] = dv
            else:
                shares_ref[far_rows[part - 1], lanes] = dk
                shares_ref[far_rows[part - 1], value_lanes] = dv


def own_kernel(where_ref, dq_ref, dk_ref, dv_ref, wq_ref, wk_ref, wv_ref, *outs):
    x = where_ref[2]
    for shift, out_ref in enumerate(outs):
        to = (x + shift) & (X_SIZE - 1)
        for half in range(2):
            rows = pl.ds(pl.multiple_of((half * X_SIZE + to) * 256, 256), 256)
            term = nt(dq_ref[...], wq_ref[rows, :])
            term = term + nt(dk_ref[...], wk_ref[rows, :])
            term = term + nt(dv_ref[...], wv_ref[rows, :])
            out_ref[:, half * 256 : (half + 1) * 256] = term.astype(jnp.bfloat16)


def own_sum_kernel(where_ref, *refs):
    parts, (mine_ref, theirs_ref) = refs[:X_SIZE], refs[X_SIZE:]
    half = where_ref[1]

    def total(which):
        lanes = pl.ds(pl.multiple_of(which * 256, 256), 256)
        return functools.reduce(jnp.add, [p[:, lanes].astype(jnp.float32) for p in parts])

    mine_ref[...] = total(half)
    theirs_ref[...] = total(1 - half).astype(jnp.bfloat16)


def project_kernel(table_ref, shares_ref, wk_ref, wv_ref, _, out_ref, rows_ref):
    @pl.when(pl.program_id(0) == 0)
    def _():
        block, _ = iotas(256, table_ref.shape[1])
        rows_ref[...] = nn(one_hot(block == table_ref[...]), shares_ref[...]).astype(jnp.bfloat16)

    for half in range(2):
        term = nt(rows_ref[:, 0:256], wk_ref[half, 0]) + nt(rows_ref[:, 256:512], wv_ref[half, 0])
        out_ref[:, half * 256 : (half + 1) * 256] = term.astype(jnp.bfloat16)


def spread_kernel(parts_ref, _, out_ref):
    total = functools.reduce(
        jnp.add, [parts_ref[g * 256 : (g + 1) * 256].astype(jnp.float32) for g in range(X_SIZE)]
    ).astype(jnp.bfloat16)
    to, block = iotas(out_ref.shape[0], 256)
    here = block == ((to >> 4) * 4 + (to & 3))
    rows = None
    for quarter in range(4):
        hits = one_hot(here & (((to >> 2) & 3) == quarter))
        part = nn(hits, total[:, quarter * 128 : (quarter + 1) * 128])
        rows = part if rows is None else rows + part
    out_ref[...] = rows.astype(jnp.bfloat16)


def finish_kernel(rows_ref, mine_ref, other_ref, out_ref):
    token, row = iotas(256, rows_ref.shape[0])
    here = ((row >> 4) == (token & 63)) & ((row & 3) == (token >> 6))
    rows = rows_ref[...]
    for half in range(2):
        lanes = slice(half * 128, (half + 1) * 128)
        far = nn(one_hot(here & (((row >> 2) & 1) == half)), rows)
        near = mine_ref[:, lanes] + other_ref[:, lanes].astype(jnp.float32)
        out_ref[:, lanes] = (far + near).astype(jnp.bfloat16)


def params():
    return pltpu.CompilerParams(vmem_limit_bytes=VMEM_LIMIT)


def shape(dims, dtype=jnp.bfloat16):
    return jax.ShapeDtypeStruct(dims, dtype)


def call(kernel, name, out_shape, **kwargs):
    return pl.pallas_call(
        kernel, out_shape=out_shape, name=name, compiler_params=params(), **kwargs
    )


def swap(rows, parts, axis):
    cut = rows.reshape(parts, rows.shape[0] // parts, rows.shape[1])
    return lax.all_to_all(cut, axis, split_axis=0, concat_axis=0, tiled=True).reshape(rows.shape)


def body(queries, keys, values, out_grad, random_blocks, w_query, w_key, w_value):
    shards = lax.axis_size("seq")
    total_blocks = shards * PER
    wanted = shards * SLOTS
    width = 2 * HD
    where = jnp.stack([lax.axis_index(name) for name in ("seq", "h", "x")]).astype(jnp.int32)
    first = jnp.arange(shards, dtype=jnp.int32)[:, None] * PER
    table = jnp.concatenate(
        [
            jnp.broadcast_to(jnp.arange(GLOB, dtype=jnp.int32)[None], (shards, GLOB)),
            (first - 1) % total_blocks,
            (first + PER) % total_blocks,
            random_blocks.reshape(shards, PER * RAND),
        ],
        axis=1,
    )
    place = ((table >> 2) * 8 + (table & 3)).reshape(wanted, 1)
    scalars = pl.BlockSpec(memory_space=pltpu.SMEM)
    whole = pl.BlockSpec()

    packed = call(pack_kernel, "pack", shape((shards * 8, width)))(keys, values)
    stripes = swap(packed, shards, "seq")

    chunk = wanted // 4
    remote = swap(
        call(
            pick_kernel,
            "pick",
            shape((wanted, 2 * width)),
            grid=(4,),
            in_specs=[
                pl.BlockSpec((chunk, 1), lambda i: (i, 0)),
                pl.BlockSpec((shards * 8, width), lambda i: (0, 0)),
            ],
            out_specs=pl.BlockSpec((chunk, 2 * width), lambda i: (i, 0)),
        )(place, stripes),
        shards,
        "seq",
    )

    query_low, own_key, own_value, shares = call(
        attention_kernel,
        "attention",
        [shape((256, width))] * 3 + [shape((wanted, 2 * width))],
        in_specs=[scalars] + [whole] * 5,
    )(where, queries, keys, values, out_grad, remote)
    returned = swap(shares, shards, "seq")

    own = call(
        own_kernel,
        "own",
        [shape((256, 2 * width))] * X_SIZE,
        in_specs=[scalars] + [whole] * 6,
    )(where, query_low, own_key, own_value, w_query, w_key, w_value)
    near = [own[0]] + [
        lax.ppermute(own[shift], "x", [(i, (i + shift) % X_SIZE) for i in range(X_SIZE)])
        for shift in range(1, X_SIZE)
    ]
    mine, theirs = call(
        own_sum_kernel,
        "own_sum",
        [shape((256, width), jnp.float32), shape((256, width))],
        in_specs=[scalars] + [whole] * X_SIZE,
    )(where, *near)
    other = lax.ppermute(theirs, "h", [(0, 1), (1, 0)])

    unused = pl.BlockSpec(memory_space=pl.ANY)
    w_spec = pl.BlockSpec((2, 1, 256, width), lambda i: (0, i, 0, 0))
    terms = call(
        project_kernel,
        "project",
        shape((X_SIZE * total_blocks, 2 * width)),
        grid=(X_SIZE,),
        in_specs=[
            pl.BlockSpec((1, wanted), lambda i: (0, 0)),
            pl.BlockSpec((wanted, 2 * width), lambda i: (0, 0)),
            w_spec,
            w_spec,
            unused,
        ],
        out_specs=pl.BlockSpec((total_blocks, 2 * width), lambda i: (i, 0)),
        scratch_shapes=[pltpu.VMEM((total_blocks, 2 * width), jnp.bfloat16)],
    )(
        table.reshape(1, wanted),
        returned,
        w_key.reshape(2, X_SIZE, 256, width),
        w_value.reshape(2, X_SIZE, 256, width),
        mine,
    )
    parts = swap(terms, X_SIZE, "x")
    spread = call(
        spread_kernel, "spread", shape((shards * 16, 128)), in_specs=[whole, unused]
    )(parts, other)
    rows = swap(spread, 2 * shards, ("seq", "h"))
    return call(finish_kernel, "finish", shape((256, width)))(rows, mine, other)


def solution(mesh):
    shards = mesh.shape["seq"]
    split = Mesh(mesh.devices.reshape(shards, -1, X_SIZE), ("seq", "h", "x"))
    head = ("h", "x")
    by_token = P("seq", head)
    in_specs = (by_token,) * 4 + (P(),) + (P(None, head),) * 3
    return jax.shard_map(body, mesh=split, in_specs=in_specs, out_specs=by_token, check_vma=False)
```

time: 169 us -> 158 us (0.935)
  the two profiles are of different devices: /device:TPU:8 before, /device:TPU:1 now
where the time goes in v3:
time: 158 us; the launch traced here: 157 us
  waiting for transfers between devices  57.9 us (37%)
  starting transfers between devices  45.9 us (29%)
  blocking collectives  27.5 us (17%)
  Pallas kernels  15.4 us (10%)
  local copies, waits for them, and re-layouts  9.37 us (6%)
    all_to_all x4, waiting for transfers between devices, swap(): lax.all_to_all(cut, axis, split_axis=0, concat_axis=0, tiled=True)  46.4 us
    all_to_all x4, starting transfers between devices, swap(): lax.all_to_all(cut, axis, split_axis=0, concat_axis=0, tiled=True)  30.6 us
    all_to_all x1, blocking collectives, swap(): lax.all_to_all(cut, axis, split_axis=0, concat_axis=0, tiled=True)  27.5 us
    ppermute x3, starting transfers between devices, body(): lax.ppermute(own[shift], 'x', [(i, (i + shift) % X_SIZE) for i in range(X...  10.5 us
    unnamed x35, local copies, waits for them, and re-layouts  8.14 us
    ppermute x3, waiting for transfers between devices, body(): lax.ppermute(own[shift], 'x', [(i, (i + shift) % X_SIZE) for i in range(X...  6.49 us
    ppermute x1, waiting for transfers between devices, body(): other = lax.ppermute(theirs, 'h', [(0, 1), (1, 0)])  4.96 us
    ppermute x1, starting transfers between devices, body(): other = lax.ppermute(theirs, 'h', [(0, 1), (1, 0)])  4.74 us
  transfers between devices with their start and end apart: 8, of which 7 were waited for; matrix products, arithmetic and copies ran while one was open for 1% of the time, Pallas kernels for 2%

profile of v3, /device:TPU:1, one launch (start us, length us, event | category | flops | bytes accessed | tf_op | source)
XLA Modules:
  0.0 157.1 jit_solution(17503718156555186845)
XLA Ops:
  0.0 0.0 copy-start.4
  0.0 0.9 copy-done.4
  0.9 0.0 copy-start.6
  0.9 0.9 copy-done.6
  1.8 1.0 pack.1
  2.8 0.0 copy-start.16
  2.8 15.5 %all-to-all-start = ((bf16[64,8,256]{2,1,0:T(8,128)(2,1)}), bf16[64,8,256]{2,1,0:T(8,128)(2,1)S(1)}, u32[]{:S(2)}, u32[]{:S(2)}) async-start(bf16[64,8,256]{2,1,0:T(8,128)(2,1)} %bitcast.3), calls=%async_computation | async-start | bytes 524288 | tf_op jit(solution)/shard_map/all_to_all | solution.py:193
  18.4 0.0 copy-done.16
  18.4 0.1 copy.16
  18.5 0.1 reshape.169
  18.7 0.7 and_add_fusion
  19.4 0.3 add.64.place_ref
  19.7 12.2 %all-to-all-done = bf16[64,8,256]{2,1,0:T(8,128)(2,1)S(1)} async-done(((bf16[64,8,256]{2,1,0:T(8,128)(2,1)}), bf16[64,8,256]{2,1,0:T(8,128)(2,1)S(1)}, u32[]{:S(2)}, u32[]{:S(2)}) %all-to-all-start) | async-done | bytes 262176 | tf_op jit(solution)/shard_map/all_to_all | solution.py:193
  31.9 2.5 %pick.1 = bf16[1024,512]{1,0:T(8,128)(2,1)} custom-call(s32[1024,1]{1,0:T(8,128)S(1)} %add.64.place_ref, bf16[512,256]{1,0:T(8,128)(2,1)S(1)} %bitcast.20), custom_call_target="tpu_custom_call" | custom-call | tf_op jit(solution)/shard_map/pick/pallas_call | solution.py:221
  34.4 0.0 copy-start.5
  34.4 0.0 copy-start.7
  34.4 0.0 copy-start.12
  34.4 0.0 copy-start.13
  34.4 4.7 %all-to-all-start.1 = ((bf16[64,16,512]{2,1,0:T(8,128)(2,1)}), bf16[64,16,512]{2,1,0:T(8,128)(2,1)S(1)}, u32[]{:S(2)}, u32[]{:S(2)}) async-start(bf16[64,16,512]{2,1,0:T(8,128)(2,1)} %bitcast.5), calls=%async_computation.1 | async-start | bytes 2097152 | tf_op jit(solution)/shard_map/all_to_all | solution.py:193
  39.1 0.1 pad_add_fusion.1.where_ref
  39.2 28.5 %all-to-all-done.1 = bf16[64,16,512]{2,1,0:T(8,128)(2,1)S(1)} async-done(((bf16[64,16,512]{2,1,0:T(8,128)(2,1)}), bf16[64,16,512]{2,1,0:T(8,128)(2,1)S(1)}, u32[]{:S(2)}, u32[]{:S(2)}) %all-to-all-start.1) | async-done | bytes 1048608 | tf_op jit(solution)/shard_map/all_to_all | solution.py:193
  67.7 0.0 copy-done.5
  67.8 0.0 copy-done.7
  67.8 0.0 copy-done.12
  67.8 0.0 copy-done.13
  67.8 3.5 %attention.1 = (bf16[256,256]{1,0:T(8,128)(2,1)S(1)}, bf16[256,256]{1,0:T(8,128)(2,1)S(1)}, bf16[256,256]{1,0:T(8,128)(2,1)S(1)}, bf16[1024,512]{1,0:T(8,128)(2,1)S(1)}) custom-call(s32[3]{0:T(128)S(1)} %pad_add_fusion.1.where_ref, bf16[256,256]{1,0:T(8,128)(2,1)S(1)} %copy-done.12, bf16[256,256]{1,0:T(8,128)(2,1)S(1)} %copy-done.5, ...), custom_call_target="tpu_custom_call" | custom-call | tf_op jit(solution)/shard_map/attention/pallas_call | solution.py:236
  71.2 0.0 copy-start.2
  71.3 1.0 copy-done.2
  72.2 0.0 copy-start
  72.2 0.0 copy-start.1
  72.2 6.2 %all-to-all-start.2 = ((bf16[64,16,512]{2,1,0:T(8,128)(2,1)}), bf16[64,16,512]{2,1,0:T(8,128)(2,1)S(1)}, u32[]{:S(2)}, u32[]{:S(2)}) async-start(bf16[64,16,512]{2,1,0:T(8,128)(2,1)} %bitcast.22), calls=%async_computation.2 | async-start | bytes 2097152 | tf_op jit(solution)/shard_map/all_to_all | solution.py:193
  78.4 0.0 copy-done
  78.5 0.0 copy-done.1
  78.5 0.0 copy-start.3
  78.5 1.2 copy-done.3
  79.7 2.3 %own.1 = (bf16[256,512]{1,0:T(8,128)(2,1)S(1)}, bf16[256,512]{1,0:T(8,128)(2,1)}, bf16[256,512]{1,0:T(8,128)(2,1)}, bf16[256,512]{1,0:T(8,128)(2,1)}) custom-call(s32[3]{0:T(128)S(1)} %pad_add_fusion.1.where_ref, bf16[256,256]{1,0:T(8,128)(2,1)S(1)} %get-tuple-element.16.dq_ref, bf16[256,256]{1,0:T(8,128)(2,1)S(1)} %get-tuple-element.17.dk_ref, ...), custom_call_target="tpu_custom_call" | custom-call | tf_op jit(solution)/shard_map/own/pallas_call | solution.py:244
  82.0 0.0 copy-start.8
  82.0 0.7 copy-done.8
  82.7 3.1 %collective-permute-start = (bf16[256,512]{1,0:T(8,128)(2,1)}, bf16[256,512]{1,0:T(8,128)(2,1)S(1)}, u32[]{:S(2)}, u32[]{:S(2)}) collective-permute-start(bf16[256,512]{1,0:T(8,128)(2,1)} %get-tuple-element.20), channel_id=1, source_target_pairs={{0,1},{1,2},{2,3},{3,0},{4,5},{5,6},{6,7},{7,4},{8,9},{9,10},{10,1... | collective-permute-start | bytes 786440 | tf_op jit(solution)/shard_map/ppermute | solution.py:251
  85.8 4.4 %collective-permute-start.1 = (bf16[256,512]{1,0:T(8,128)(2,1)}, bf16[256,512]{1,0:T(8,128)(2,1)}, u32[]{:S(2)}, u32[]{:S(2)}) collective-permute-start(bf16[256,512]{1,0:T(8,128)(2,1)} %get-tuple-element.21), channel_id=1, source_target_pairs={{0,2},{1,3},{2,0},{3,1},{4,6},{5,7},{6,4},{7,5},{8,10},{9,11},{10,... | collective-permute-start | bytes 786440 | tf_op jit(solution)/shard_map/ppermute | solution.py:251
  90.2 3.1 %collective-permute-start.2 = (bf16[256,512]{1,0:T(8,128)(2,1)}, bf16[256,512]{1,0:T(8,128)(2,1)}, u32[]{:S(2)}, u32[]{:S(2)}) collective-permute-start(bf16[256,512]{1,0:T(8,128)(2,1)} %get-tuple-element.22), channel_id=1, source_target_pairs={{0,3},{1,0},{2,1},{3,2},{4,7},{5,4},{6,5},{7,6},{8,11},{9,8},{10,9... | collective-permute-start | bytes 786440 | tf_op jit(solution)/shard_map/ppermute | solution.py:251
  93.2 0.8 reshape.170.table_ref
  94.1 0.0 collective-permute-done.refs_1_
  94.1 0.0 copy-start.10
  94.1 0.7 copy-done.10
  94.8 5.3 %collective-permute-done.1.refs_2_ = bf16[256,512]{1,0:T(8,128)(2,1)} collective-permute-done((bf16[256,512]{1,0:T(8,128)(2,1)}, bf16[256,512]{1,0:T(8,128)(2,1)}, u32[]{:S(2)}, u32[]{:S(2)}) %collective-permute-start.1) | collective-permute-done | bytes 262176 | tf_op jit(solution)/shard_map/ppermute | solution.py:251
  100.1 1.2 collective-permute-done.2.refs_3_
  101.3 0.0 copy-start.9
  101.3 0.9 copy-done.9
  102.2 0.0 copy-start.11
  102.2 0.9 copy-done.11
  103.2 1.2 own_sum.1
  104.4 0.0 copy-start.14
  104.4 0.6 copy-done.14
  105.0 1.9 %all-to-all-done.2 = bf16[64,16,512]{2,1,0:T(8,128)(2,1)S(1)} async-done(((bf16[64,16,512]{2,1,0:T(8,128)(2,1)}), bf16[64,16,512]{2,1,0:T(8,128)(2,1)S(1)}, u32[]{:S(2)}, u32[]{:S(2)}) %all-to-all-start.2) | async-done | bytes 1048608 | tf_op jit(solution)/shard_map/all_to_all | solution.py:193
  106.9 3.0 %project.1 = bf16[1024,512]{1,0:T(8,128)(2,1)} custom-call(s32[1,1024]{1,0:T(1,128)S(1)} %reshape.170.table_ref, bf16[1024,512]{1,0:T(8,128)(2,1)S(1)} %bitcast.15, bf16[2,4,256,256]{3,2,1,0:T(8,128)(2,1)S(1)} %bitcast.16, bf16[2,4,256,256]{3,2,1,0:T(8,128)(2,1)S(1)} %bitcast.17, f32[256,256]{1,0:T(8,128)S(1)} %get-tuple-element.23._.mine_ref), custom_call_target="tpu_custom_call" | custom-call | tf_op jit(solution)/shard_map/project/pallas_call | solution.py:264
  109.9 4.1 %all-to-all-start.3 = ((bf16[4,256,512]{2,1,0:T(8,128)(2,1)}), bf16[4,256,512]{2,1,0:T(8,128)(2,1)S(1)}, u32[]{:S(2)}, u32[]{:S(2)}) async-start(bf16[4,256,512]{2,1,0:T(8,128)(2,1)} %bitcast.11), calls=%async_computation.3 | async-start | bytes 2097152 | tf_op jit(solution)/shard_map/all_to_all | solution.py:193
  114.1 0.0 copy-done.15
  114.1 4.7 %collective-permute-start.3 = (bf16[256,256]{1,0:T(8,128)(2,1)S(1)}, bf16[256,256]{1,0:T(8,128)(2,1)S(1)}, u32[]{:S(2)}, u32[]{:S(2)}) collective-permute-start(bf16[256,256]{1,0:T(8,128)(2,1)S(1)} %copy-done.15), channel_id=1, source_target_pairs={{0,4},{4,0},{1,5},{5,1},{2,6},{6,2},{3,7},{7,3},{8,12},{12,8},{9,1... | collective-permute-start | bytes 393224 | tf_op jit(solution)/shard_map/ppermute | solution.py:260
  118.9 5.0 %collective-permute-done.3._.other_ref = bf16[256,256]{1,0:T(8,128)(2,1)S(1)} collective-permute-done((bf16[256,256]{1,0:T(8,128)(2,1)S(1)}, bf16[256,256]{1,0:T(8,128)(2,1)S(1)}, u32[]{:S(2)}, u32[]{:S(2)}) %collective-permute-start.3) | collective-permute-done | bytes 131104 | tf_op jit(solution)/shard_map/ppermute | solution.py:260
  123.8 3.8 %all-to-all-done.3 = bf16[4,256,512]{2,1,0:T(8,128)(2,1)S(1)} async-done(((bf16[4,256,512]{2,1,0:T(8,128)(2,1)}), bf16[4,256,512]{2,1,0:T(8,128)(2,1)S(1)}, u32[]{:S(2)}, u32[]{:S(2)}) %all-to-all-start.3) | async-done | bytes 1048608 | tf_op jit(solution)/shard_map/all_to_all | solution.py:193
  127.6 0.8 spread.1
  128.4 27.5 %all_to_all.25 = bf16[128,8,128]{2,1,0:T(8,128)(2,1)S(1)} all-to-all(bf16[128,8,128]{2,1,0:T(8,128)(2,1)S(1)} %bitcast.23), channel_id=1, replica_groups=mesh['seq'=64,'h'=2,'x'=4] {'seq','h'}, dimensions={0} | all-to-all | bytes 524288 | tf_op jit(solution)/shard_map/all_to_all | solution.py:193
  156.0 1.1 finish.1
  (3 shorter events, 0.0 us)
Async XLA Ops:
  0.0 0.9 copy-start.4
  0.9 0.9 copy-start.6
  2.8 15.6 %copy-start.16 = (s32[256,3]{0,1:T(4,128)S(1)}, s32[256,3]{0,1:T(4,128)}, u32[]{:S(2)}) copy-start(s32[256,3]{0,1:T(4,128)} %param.12) | copy-start | bytes 9220
  2.8 29.1 %all-to-all-start = ((bf16[64,8,256]{2,1,0:T(8,128)(2,1)}), bf16[64,8,256]{2,1,0:T(8,128)(2,1)S(1)}, u32[]{:S(2)}, u32[]{:S(2)}) async-start(bf16[64,8,256]{2,1,0:T(8,128)(2,1)} %bitcast.3), calls=%async_computation | async-start | bytes 524288 | tf_op jit(solution)/shard_map/all_to_all | solution.py:193
  34.4 33.4 %copy-start.5 = (bf16[256,256]{1,0:T(8,128)(2,1)S(1)}, bf16[256,256]{1,0:T(8,128)(2,1)}, u32[]{:S(2)}) copy-start(bf16[256,256]{1,0:T(8,128)(2,1)} %k_ref.1) | copy-start | bytes 393220
  34.4 33.4 %copy-start.7 = (bf16[256,256]{1,0:T(8,128)(2,1)S(1)}, bf16[256,256]{1,0:T(8,128)(2,1)}, u32[]{:S(2)}) copy-start(bf16[256,256]{1,0:T(8,128)(2,1)} %v_ref.1) | copy-start | bytes 393220
  34.4 33.4 %copy-start.12 = (bf16[256,256]{1,0:T(8,128)(2,1)S(1)}, bf16[256,256]{1,0:T(8,128)(2,1)}, u32[]{:S(2)}) copy-start(bf16[256,256]{1,0:T(8,128)(2,1)} %q_ref.1) | copy-start | bytes 393220
  34.4 33.4 %copy-start.13 = (bf16[256,256]{1,0:T(8,128)(2,1)S(1)}, bf16[256,256]{1,0:T(8,128)(2,1)}, u32[]{:S(2)}) copy-start(bf16[256,256]{1,0:T(8,128)(2,1)} %g_ref.1) | copy-start | bytes 393220
  34.4 33.3 %all-to-all-start.1 = ((bf16[64,16,512]{2,1,0:T(8,128)(2,1)}), bf16[64,16,512]{2,1,0:T(8,128)(2,1)S(1)}, u32[]{:S(2)}, u32[]{:S(2)}) async-start(bf16[64,16,512]{2,1,0:T(8,128)(2,1)} %bitcast.5), calls=%async_computation.1 | async-start | bytes 2097152 | tf_op jit(solution)/shard_map/all_to_all | solution.py:193
  71.2 1.0 copy-start.2
  72.2 6.2 %copy-start = (bf16[2048,256]{1,0:T(8,128)(2,1)S(1)}, bf16[2048,256]{1,0:T(8,128)(2,1)}, u32[]{:S(2)}) copy-start(bf16[2048,256]{1,0:T(8,128)(2,1)} %wk_ref.1) | copy-start | bytes 3145732
  72.2 6.2 %copy-start.1 = (bf16[2048,256]{1,0:T(8,128)(2,1)S(1)}, bf16[2048,256]{1,0:T(8,128)(2,1)}, u32[]{:S(2)}) copy-start(bf16[2048,256]{1,0:T(8,128)(2,1)} %wv_ref.1) | copy-start | bytes 3145732
  72.2 34.7 %all-to-all-start.2 = ((bf16[64,16,512]{2,1,0:T(8,128)(2,1)}), bf16[64,16,512]{2,1,0:T(8,128)(2,1)S(1)}, u32[]{:S(2)}, u32[]{:S(2)}) async-start(bf16[64,16,512]{2,1,0:T(8,128)(2,1)} %bitcast.22), calls=%async_computation.2 | async-start | bytes 2097152 | tf_op jit(solution)/shard_map/all_to_all | solution.py:193
  78.5 1.2 copy-start.3
  82.0 0.7 copy-start.8
  82.7 11.4 %collective-permute-start = (bf16[256,512]{1,0:T(8,128)(2,1)}, bf16[256,512]{1,0:T(8,128)(2,1)S(1)}, u32[]{:S(2)}, u32[]{:S(2)}) collective-permute-start(bf16[256,512]{1,0:T(8,128)(2,1)} %get-tuple-element.20), channel_id=1, source_target_pairs={{0,1},{1,2},{2,3},{3,0},{4,5},{5,6},{6,7},{7,4},{8,9},{9,10},{10,1... | collective-permute-start | bytes 786440 | tf_op jit(solution)/shard_map/ppermute | solution.py:251
  85.8 14.3 %collective-permute-start.1 = (bf16[256,512]{1,0:T(8,128)(2,1)}, bf16[256,512]{1,0:T(8,128)(2,1)}, u32[]{:S(2)}, u32[]{:S(2)}) collective-permute-start(bf16[256,512]{1,0:T(8,128)(2,1)} %get-tuple-element.21), channel_id=1, source_target_pairs={{0,2},{1,3},{2,0},{3,1},{4,6},{5,7},{6,4},{7,5},{8,10},{9,11},{10,... | collective-permute-start | bytes 786440 | tf_op jit(solution)/shard_map/ppermute | solution.py:251
  90.2 11.1 %collective-permute-start.2 = (bf16[256,512]{1,0:T(8,128)(2,1)}, bf16[256,512]{1,0:T(8,128)(2,1)}, u32[]{:S(2)}, u32[]{:S(2)}) collective-permute-start(bf16[256,512]{1,0:T(8,128)(2,1)} %get-tuple-element.22), channel_id=1, source_target_pairs={{0,3},{1,0},{2,1},{3,2},{4,7},{5,4},{6,5},{7,6},{8,11},{9,8},{10,9... | collective-permute-start | bytes 786440 | tf_op jit(solution)/shard_map/ppermute | solution.py:251
  94.1 0.7 copy-start.10
  101.3 1.0 copy-start.9
  102.2 0.9 copy-start.11
  104.4 0.7 copy-start.14
  109.9 4.2 %copy-start.15 = (bf16[256,256]{1,0:T(8,128)(2,1)S(1)}, bf16[256,256]{1,0:T(8,128)(2,1)}, u32[]{:S(2)}) copy-start(bf16[256,256]{1,0:T(8,128)(2,1)} %copy-done.14) | copy-start | bytes 393220
  109.9 17.6 %all-to-all-start.3 = ((bf16[4,256,512]{2,1,0:T(8,128)(2,1)}), bf16[4,256,512]{2,1,0:T(8,128)(2,1)S(1)}, u32[]{:S(2)}, u32[]{:S(2)}) async-start(bf16[4,256,512]{2,1,0:T(8,128)(2,1)} %bitcast.11), calls=%async_computation.3 | async-start | bytes 2097152 | tf_op jit(solution)/shard_map/all_to_all | solution.py:193
  114.1 9.7 %collective-permute-start.3 = (bf16[256,256]{1,0:T(8,128)(2,1)S(1)}, bf16[256,256]{1,0:T(8,128)(2,1)S(1)}, u32[]{:S(2)}, u32[]{:S(2)}) collective-permute-start(bf16[256,256]{1,0:T(8,128)(2,1)S(1)} %copy-done.15), channel_id=1, source_target_pairs={{0,4},{4,0},{1,5},{5,1},{2,6},{6,2},{3,7},{7,3},{8,12},{12,8},{9,1... | collective-permute-start | bytes 393224 | tf_op jit(solution)/shard_map/ppermute | solution.py:260

commit v4 on v3

--- a/solution.py
+++ b/solution.py
@@ -39,23 +39,43 @@
     return [lax.broadcasted_iota(jnp.int32, dims, axis) for axis in range(len(dims))]
 
 
-def pack_kernel(keys_ref, values_ref, out_ref):
+def pack_kernel(keys_hbm, values_hbm, out_ref, keys_ref, values_ref, sems):
+    copies = [
+        pltpu.make_async_copy(src, dst, sems.at[i])
+        for i, (src, dst) in enumerate(((keys_hbm, keys_ref), (values_hbm, values_ref)))
+    ]
+    for copy in copies:
+        copy.start()
     to, row = iotas(512, 256)
-    source = (to & 3) * BLK + (to >> 3)
-    here = row == source
+    here = row == (to & 3) * BLK + (to >> 3)
     is_value = (to & 4) != 0
-    rows = nn(one_hot(here & jnp.logical_not(is_value)), keys_ref[...])
-    rows = rows + nn(one_hot(here & is_value), values_ref[...])
+    from_keys = one_hot(here & jnp.logical_not(is_value))
+    from_values = one_hot(here & is_value)
+    for copy in copies:
+        copy.wait()
+    rows = nn(from_keys, keys_ref[...]) + nn(from_values, values_ref[...])
     out_ref[...] = rows.astype(jnp.bfloat16)
 
 
-def pick_kernel(place_ref, table_ref, out_ref):
-    place = place_ref[...]
-    _, row = iotas(place.shape[0], table_ref.shape[0])
-    table = table_ref[...]
+def pick_kernel(index_ref, stripes_ref, out_hbm, rows_ref, sems):
+    block, row = iotas(256, 512)
+    table = []
     for kind in range(2):
-        hits = one_hot(row == place + 4 * kind)
-        out_ref[:, kind * 256 : (kind + 1) * 256] = nn(hits, table).astype(jnp.bfloat16)
+        source = (block >> 2) * 8 + kind * 4 + (block & 3)
+        table.append(nn(one_hot(row == source), stripes_ref[...]).astype(jnp.bfloat16))
+    chunk = rows_ref.shape[0] // sems.shape[0]
+    _, block = iotas(chunk, 256)
+    copies = []
+    for at in range(sems.shape[0]):
+        rows = slice(at * chunk, (at + 1) * chunk)
+        hits = one_hot(block == index_ref[rows, :])
+        for kind in range(2):
+            lanes = slice(kind * 256, (kind + 1) * 256)
+            rows_ref[rows, lanes] = nn(hits, table[kind]).astype(jnp.bfloat16)
+        copies.append(pltpu.make_async_copy(rows_ref.at[rows], out_hbm.at[rows], sems.at[at]))
+        copies[-1].start()
+    for copy in copies:
+        copy.wait()
 
 
 def attention_kernel(
@@ -138,20 +158,36 @@
     theirs_ref[...] = total(1 - half).astype(jnp.bfloat16)
 
 
-def project_kernel(table_ref, shares_ref, wk_ref, wv_ref, _, out_ref, rows_ref):
-    @pl.when(pl.program_id(0) == 0)
-    def _():
-        block, _ = iotas(256, table_ref.shape[1])
-        rows_ref[...] = nn(one_hot(block == table_ref[...]), shares_ref[...]).astype(jnp.bfloat16)
-
-    for half in range(2):
-        term = nt(rows_ref[:, 0:256], wk_ref[half, 0]) + nt(rows_ref[:, 256:512], wv_ref[half, 0])
-        out_ref[:, half * 256 : (half + 1) * 256] = term.astype(jnp.bfloat16)
+def project_kernel(index_ref, shares_ref, wk_hbm, wv_hbm, _, __, ___, out_hbm, weights_ref, terms_ref, sems):
+    loads = [
+        [
+            pltpu.make_async_copy(w.at[:, x], weights_ref.at[x, kind], sems.at[0, 2 * x + kind])
+            for kind, w in enumerate((wk_hbm, wv_hbm))
+        ]
+        for x in range(X_SIZE)
+    ]
+    for pair in loads:
+        for load in pair:
+            load.start()
+    block, _ = iotas(256, index_ref.shape[1])
+    rows = nn(one_hot(block == index_ref[...]), shares_ref[...]).astype(jnp.bfloat16)
+    stores = []
+    for x in range(X_SIZE):
+        for load in loads[x]:
+            load.wait()
+        for half in range(2):
+            term = nt(rows[:, 0:256], weights_ref[x, 0, half])
+            term = term + nt(rows[:, 256:512], weights_ref[x, 1, half])
+            terms_ref[x, :, half * 256 : (half + 1) * 256] = term.astype(jnp.bfloat16)
+        stores.append(pltpu.make_async_copy(terms_ref.at[x], out_hbm.at[x], sems.at[1, x]))
+        stores[-1].start()
+    for store in stores:
+        store.wait()
 
 
 def spread_kernel(parts_ref, _, out_ref):
     total = functools.reduce(
-        jnp.add, [parts_ref[g * 256 : (g + 1) * 256].astype(jnp.float32) for g in range(X_SIZE)]
+        jnp.add, [parts_ref[g].astype(jnp.float32) for g in range(X_SIZE)]
     ).astype(jnp.bfloat16)
     to, block = iotas(out_ref.shape[0], 256)
     here = block == ((to >> 4) * 4 + (to & 3))
@@ -174,17 +210,17 @@
         out_ref[:, lanes] = (far + near).astype(jnp.bfloat16)
 
 
-def params():
-    return pltpu.CompilerParams(vmem_limit_bytes=VMEM_LIMIT)
+def params(limit):
+    return pltpu.CompilerParams(vmem_limit_bytes=limit)
 
 
 def shape(dims, dtype=jnp.bfloat16):
     return jax.ShapeDtypeStruct(dims, dtype)
 
 
-def call(kernel, name, out_shape, **kwargs):
+def call(kernel, name, out_shape, limit=VMEM_LIMIT, **kwargs):
     return pl.pallas_call(
-        kernel, out_shape=out_shape, name=name, compiler_params=params(), **kwargs
+        kernel, out_shape=out_shape, name=name, compiler_params=params(limit), **kwargs
     )
 
 
@@ -209,29 +245,29 @@
         ],
         axis=1,
     )
-    place = ((table >> 2) * 8 + (table & 3)).reshape(wanted, 1)
     scalars = pl.BlockSpec(memory_space=pltpu.SMEM)
     whole = pl.BlockSpec()
 
-    packed = call(pack_kernel, "pack", shape((shards * 8, width)))(keys, values)
+    in_hbm = pl.BlockSpec(memory_space=pltpu.HBM)
+    packed = call(
+        pack_kernel,
+        "pack",
+        shape((shards * 8, width)),
+        limit=62 * 1024 * 1024,
+        in_specs=[in_hbm, in_hbm],
+        scratch_shapes=[pltpu.VMEM((256, width), jnp.bfloat16)] * 2 + [pltpu.SemaphoreType.DMA((2,))],
+    )(keys, values)
     stripes = swap(packed, shards, "seq")
 
-    chunk = wanted // 4
-    remote = swap(
-        call(
-            pick_kernel,
-            "pick",
-            shape((wanted, 2 * width)),
-            grid=(4,),
-            in_specs=[
-                pl.BlockSpec((chunk, 1), lambda i: (i, 0)),
-                pl.BlockSpec((shards * 8, width), lambda i: (0, 0)),
-            ],
-            out_specs=pl.BlockSpec((chunk, 2 * width), lambda i: (i, 0)),
-        )(place, stripes),
-        shards,
-        "seq",
-    )
+    outside = pl.BlockSpec(memory_space=pl.ANY)
+    picked = call(
+        pick_kernel,
+        "pick",
+        shape((wanted, 2 * width)),
+        out_specs=outside,
+        scratch_shapes=[pltpu.VMEM((wanted, 2 * width), jnp.bfloat16), pltpu.SemaphoreType.DMA((4,))],
+    )(table.reshape(wanted, 1), stripes)
+    remote = swap(picked, shards, "seq")
 
     query_low, own_key, own_value, shares = call(
         attention_kernel,
@@ -259,32 +295,27 @@
     )(where, *near)
     other = lax.ppermute(theirs, "h", [(0, 1), (1, 0)])
 
-    unused = pl.BlockSpec(memory_space=pl.ANY)
-    w_spec = pl.BlockSpec((2, 1, 256, width), lambda i: (0, i, 0, 0))
     terms = call(
         project_kernel,
         "project",
-        shape((X_SIZE * total_blocks, 2 * width)),
-        grid=(X_SIZE,),
-        in_specs=[
-            pl.BlockSpec((1, wanted), lambda i: (0, 0)),
-            pl.BlockSpec((wanted, 2 * width), lambda i: (0, 0)),
-            w_spec,
-            w_spec,
-            unused,
+        shape((X_SIZE, total_blocks, 2 * width)),
+        in_specs=[whole, whole, in_hbm, in_hbm, outside, outside, outside],
+        out_specs=outside,
+        scratch_shapes=[
+            pltpu.VMEM((X_SIZE, 2, 2, 256, width), jnp.bfloat16),
+            pltpu.VMEM((X_SIZE, total_blocks, 2 * width), jnp.bfloat16),
+            pltpu.SemaphoreType.DMA((2, 2 * X_SIZE)),
         ],
-        out_specs=pl.BlockSpec((total_blocks, 2 * width), lambda i: (i, 0)),
-        scratch_shapes=[pltpu.VMEM((total_blocks, 2 * width), jnp.bfloat16)],
     )(
         table.reshape(1, wanted),
         returned,
         w_key.reshape(2, X_SIZE, 256, width),
         w_value.reshape(2, X_SIZE, 256, width),
-        mine,
+        *near[1:],
     )
-    parts = swap(terms, X_SIZE, "x")
+    parts = lax.all_to_all(terms, "x", split_axis=0, concat_axis=0, tiled=True)
     spread = call(
-        spread_kernel, "spread", shape((shards * 16, 128)), in_specs=[whole, unused]
+        spread_kernel, "spread", shape((shards * 16, 128)), in_specs=[whole, outside]
     )(parts, other)
     rows = swap(spread, 2 * shards, ("seq", "h"))
     return call(finish_kernel, "finish", shape((256, width)))(rows, mine, other)

time: 158 us -> 154 us (0.975)
  local copies, waits for them, and re-layouts: 9.37 us -> 4.66 us
  waiting for transfers between devices: 57.9 us -> 61.5 us
  blocking collectives: 27.5 us -> 25.3 us
    unnamed x35 -> x25, local copies, waits for them, and re-layouts: 8.14 us -> 3.43 us
    all_to_all x4 -> x3, starting transfers between devices: 30.6 us -> 26.4 us  [swap(): lax.all_to_all(cut, axis, split_axis=0, concat_axis=0, tiled=True)]
    all_to_all x0 -> x1, starting transfers between devices: none -> 4.16 us  [body(): parts = lax.all_to_all(terms, 'x', split_axis=0, concat_axis=0, tiled=True)]
    all_to_all x1, blocking collectives: 27.5 us -> 25.3 us  [swap(): lax.all_to_all(cut, axis, split_axis=0, concat_axis=0, tiled=True)]
    ppermute x1, waiting for transfers between devices: 4.96 us -> 6.65 us  [body(): other = lax.ppermute(theirs, 'h', [(0, 1), (1, 0)])]
    all_to_all x4 -> x3, waiting for transfers between devices: 46.4 us -> 46.7 us  [swap(): lax.all_to_all(cut, axis, split_axis=0, concat_axis=0, tiled=True)]
where the time goes in v4:
time: 154 us; the launch traced here: 153 us
  waiting for transfers between devices  61.5 us (40%)
  starting transfers between devices  45.8 us (30%)
  blocking collectives  25.3 us (16%)
  Pallas kernels  15.3 us (10%)
  local copies, waits for them, and re-layouts  4.66 us (3%)
    all_to_all x3, waiting for transfers between devices, swap(): lax.all_to_all(cut, axis, split_axis=0, concat_axis=0, tiled=True)  46.7 us
    all_to_all x3, starting transfers between devices, swap(): lax.all_to_all(cut, axis, split_axis=0, concat_axis=0, tiled=True)  26.4 us
    all_to_all x1, blocking collectives, swap(): lax.all_to_all(cut, axis, split_axis=0, concat_axis=0, tiled=True)  25.3 us
    ppermute x3, starting transfers between devices, body(): lax.ppermute(own[shift], 'x', [(i, (i + shift) % X_SIZE) for i in range(X...  10.5 us
    ppermute x3, waiting for transfers between devices, body(): lax.ppermute(own[shift], 'x', [(i, (i + shift) % X_SIZE) for i in range(X...  7.23 us
    ppermute x1, waiting for transfers between devices, body(): other = lax.ppermute(theirs, 'h', [(0, 1), (1, 0)])  6.65 us
    ppermute x1, starting transfers between devices, body(): other = lax.ppermute(theirs, 'h', [(0, 1), (1, 0)])  4.76 us
    all_to_all x1, starting transfers between devices, body(): parts = lax.all_to_all(terms, 'x', split_axis=0, concat_axis=0, tiled=True)  4.16 us
  transfers between devices with their start and end apart: 8, of which 7 were waited for; matrix products, arithmetic and copies ran while one was open for 1% of the time, Pallas kernels for 2%

profile of v4, /device:TPU:1, one launch (start us, length us, event | category | flops | bytes accessed | tf_op | source)
XLA Modules:
  0.0 152.9 jit_solution(13018138225462120505)
XLA Ops:
  0.0 2.0 %pack.1 = bf16[512,256]{1,0:T(8,128)(2,1)} custom-call(bf16[256,256]{1,0:T(8,128)(2,1)} %k_ref.1, bf16[256,256]{1,0:T(8,128)(2,1)} %v_ref.1), custom_call_target="tpu_custom_call" | custom-call | tf_op jit(solution)/shard_map/pack/pallas_call | solution.py:252
  2.0 0.0 copy-start.11
  2.0 15.4 %all-to-all-start = ((bf16[64,8,256]{2,1,0:T(8,128)(2,1)}), bf16[64,8,256]{2,1,0:T(8,128)(2,1)S(1)}, u32[]{:S(2)}, u32[]{:S(2)}) async-start(bf16[64,8,256]{2,1,0:T(8,128)(2,1)} %bitcast.21), calls=%async_computation | async-start | bytes 524288 | tf_op jit(solution)/shard_map/all_to_all | solution.py:229
  17.4 0.0 copy-done.11
  17.4 0.1 copy.16
  17.6 0.1 reshape.133
  17.7 0.1 pad_add_fusion
  17.8 0.0 copy-start.10
  17.8 0.3 reshape.146.index_ref
  18.1 0.3 copy-done.10
  18.4 12.5 %all-to-all-done = bf16[64,8,256]{2,1,0:T(8,128)(2,1)S(1)} async-done(((bf16[64,8,256]{2,1,0:T(8,128)(2,1)}), bf16[64,8,256]{2,1,0:T(8,128)(2,1)S(1)}, u32[]{:S(2)}, u32[]{:S(2)}) %all-to-all-start) | async-done | bytes 262176 | tf_op jit(solution)/shard_map/all_to_all | solution.py:229
  31.0 1.6 %pick.1 = bf16[1024,512]{1,0:T(8,128)(2,1)} custom-call(s32[1024,1]{1,0:T(8,128)S(1)} %reshape.146.index_ref, bf16[512,256]{1,0:T(8,128)(2,1)S(1)} %bitcast.17), custom_call_target="tpu_custom_call" | custom-call | tf_op jit(solution)/shard_map/pick/pallas_call | solution.py:263
  32.5 0.0 copy-start.4
  32.5 0.0 copy-start.5
  32.6 0.0 copy-start.8
  32.6 0.0 copy-start.9
  32.6 4.7 %all-to-all-start.1 = ((bf16[64,16,512]{2,1,0:T(8,128)(2,1)}), bf16[64,16,512]{2,1,0:T(8,128)(2,1)S(1)}, u32[]{:S(2)}, u32[]{:S(2)}) async-start(bf16[64,16,512]{2,1,0:T(8,128)(2,1)} %bitcast.5), calls=%async_computation.1 | async-start | bytes 2097152 | tf_op jit(solution)/shard_map/all_to_all | solution.py:229
  37.3 0.1 pad_add_fusion.1.where_ref
  37.4 28.5 %all-to-all-done.1 = bf16[64,16,512]{2,1,0:T(8,128)(2,1)S(1)} async-done(((bf16[64,16,512]{2,1,0:T(8,128)(2,1)}), bf16[64,16,512]{2,1,0:T(8,128)(2,1)S(1)}, u32[]{:S(2)}, u32[]{:S(2)}) %all-to-all-start.1) | async-done | bytes 1048608 | tf_op jit(solution)/shard_map/all_to_all | solution.py:229
  65.9 0.0 copy-done.4
  65.9 0.0 copy-done.5
  65.9 0.0 copy-done.8
  65.9 0.0 copy-done.9
  66.0 3.5 %attention.1 = (bf16[256,256]{1,0:T(8,128)(2,1)S(1)}, bf16[256,256]{1,0:T(8,128)(2,1)S(1)}, bf16[256,256]{1,0:T(8,128)(2,1)S(1)}, bf16[1024,512]{1,0:T(8,128)(2,1)S(1)}) custom-call(s32[3]{0:T(128)S(1)} %pad_add_fusion.1.where_ref, bf16[256,256]{1,0:T(8,128)(2,1)S(1)} %copy-done.8, bf16[256,256]{1,0:T(8,128)(2,1)S(1)} %copy-done.4, ...), custom_call_target="tpu_custom_call" | custom-call | tf_op jit(solution)/shard_map/attention/pallas_call | solution.py:272
  69.5 0.0 copy-start.2
  69.5 1.0 copy-done.2
  70.5 0.0 copy-start
  70.5 0.0 copy-start.1
  70.5 6.2 %all-to-all-start.2 = ((bf16[64,16,512]{2,1,0:T(8,128)(2,1)}), bf16[64,16,512]{2,1,0:T(8,128)(2,1)S(1)}, u32[]{:S(2)}, u32[]{:S(2)}) async-start(bf16[64,16,512]{2,1,0:T(8,128)(2,1)} %bitcast.19), calls=%async_computation.2 | async-start | bytes 2097152 | tf_op jit(solution)/shard_map/all_to_all | solution.py:229
  76.7 0.0 copy-done
  76.7 0.0 copy-done.1
  76.7 0.0 copy-start.3
  76.7 1.2 copy-done.3
  78.0 2.3 %own.1 = (bf16[256,512]{1,0:T(8,128)(2,1)S(1)}, bf16[256,512]{1,0:T(8,128)(2,1)}, bf16[256,512]{1,0:T(8,128)(2,1)}, bf16[256,512]{1,0:T(8,128)(2,1)}) custom-call(s32[3]{0:T(128)S(1)} %pad_add_fusion.1.where_ref, bf16[256,256]{1,0:T(8,128)(2,1)S(1)} %get-tuple-element.16.dq_ref, bf16[256,256]{1,0:T(8,128)(2,1)S(1)} %get-tuple-element.17.dk_ref, ...), custom_call_target="tpu_custom_call" | custom-call | tf_op jit(solution)/shard_map/own/pallas_call | solution.py:280
  80.2 0.0 copy-start.6
  80.2 0.7 copy-done.6
  80.9 3.1 %collective-permute-start = (bf16[256,512]{1,0:T(8,128)(2,1)}, bf16[256,512]{1,0:T(8,128)(2,1)S(1)}, u32[]{:S(2)}, u32[]{:S(2)}) collective-permute-start(bf16[256,512]{1,0:T(8,128)(2,1)} %get-tuple-element.19), channel_id=1, source_target_pairs={{0,1},{1,2},{2,3},{3,0},{4,5},{5,6},{6,7},{7,4},{8,9},{9,10},{10,1... | collective-permute-start | bytes 786440 | tf_op jit(solution)/shard_map/ppermute | solution.py:287
  84.1 4.3 %collective-permute-start.1 = (bf16[256,512]{1,0:T(8,128)(2,1)}, bf16[256,512]{1,0:T(8,128)(2,1)}, u32[]{:S(2)}, u32[]{:S(2)}) collective-permute-start(bf16[256,512]{1,0:T(8,128)(2,1)} %get-tuple-element.20), channel_id=1, source_target_pairs={{0,2},{1,3},{2,0},{3,1},{4,6},{5,7},{6,4},{7,5},{8,10},{9,11},{10,... | collective-permute-start | bytes 786440 | tf_op jit(solution)/shard_map/ppermute | solution.py:287
  88.4 3.1 %collective-permute-start.2 = (bf16[256,512]{1,0:T(8,128)(2,1)}, bf16[256,512]{1,0:T(8,128)(2,1)}, u32[]{:S(2)}, u32[]{:S(2)}) collective-permute-start(bf16[256,512]{1,0:T(8,128)(2,1)} %get-tuple-element.21), channel_id=1, source_target_pairs={{0,3},{1,0},{2,1},{3,2},{4,7},{5,4},{6,5},{7,6},{8,11},{9,8},{10,9... | collective-permute-start | bytes 786440 | tf_op jit(solution)/shard_map/ppermute | solution.py:287
  91.5 0.8 reshape.134.index_ref
  92.3 0.0 collective-permute-done._.refs_1_
  92.3 6.0 %collective-permute-done.1.__.refs_2_ = bf16[256,512]{1,0:T(8,128)(2,1)} collective-permute-done((bf16[256,512]{1,0:T(8,128)(2,1)}, bf16[256,512]{1,0:T(8,128)(2,1)}, u32[]{:S(2)}, u32[]{:S(2)}) %collective-permute-start.1) | collective-permute-done | bytes 262176 | tf_op jit(solution)/shard_map/ppermute | solution.py:287
  98.4 1.2 collective-permute-done.2.___.refs_3_
  99.6 5.6 %all-to-all-done.2 = bf16[64,16,512]{2,1,0:T(8,128)(2,1)S(1)} async-done(((bf16[64,16,512]{2,1,0:T(8,128)(2,1)}), bf16[64,16,512]{2,1,0:T(8,128)(2,1)S(1)}, u32[]{:S(2)}, u32[]{:S(2)}) %all-to-all-start.2) | async-done | bytes 1048608 | tf_op jit(solution)/shard_map/all_to_all | solution.py:229
  105.2 2.8 %project.1 = bf16[4,256,512]{2,1,0:T(8,128)(2,1)} custom-call(s32[1,1024]{1,0:T(1,128)S(1)} %reshape.134.index_ref, bf16[1024,512]{1,0:T(8,128)(2,1)S(1)} %bitcast.14, bf16[2,4,256,256]{3,2,1,0:T(8,128)(2,1)S(1)} %bitcast.15, bf16[2,4,256,256]{3,2,1,0:T(8,128)(2,1)S(1)} %bitcast.16, bf16[256,512]{1,0:T(8,128)(2,1)S(1)} %collective-permute-done._.refs_1_, ...), custom_call_target="tpu_custom_call" | custom-call | tf_op jit(solution)/shard_map/project/pallas_call | solution.py:298
  108.0 0.0 copy-start.7
  108.0 4.2 %all-to-all-start.3 = ((bf16[4,256,512]{2,1,0:T(8,128)(2,1)}), bf16[4,256,512]{2,1,0:T(8,128)(2,1)S(1)}, u32[]{:S(2)}, u32[]{:S(2)}) async-start(bf16[4,256,512]{2,1,0:T(8,128)(2,1)} %project.1), calls=%async_computation.3 | async-start | bytes 2097152 | tf_op jit(solution)/shard_map/all_to_all | solution.py:316
  112.2 0.0 copy-done.7
  112.2 1.2 own_sum.1
  113.3 4.8 %collective-permute-start.3 = (bf16[256,256]{1,0:T(8,128)(2,1)S(1)}, bf16[256,256]{1,0:T(8,128)(2,1)S(1)}, u32[]{:S(2)}, u32[]{:S(2)}) collective-permute-start(bf16[256,256]{1,0:T(8,128)(2,1)S(1)} %get-tuple-element.23), channel_id=1, source_target_pairs={{0,4},{4,0},{1,5},{5,1},{2,6},{6,2},{3,7},{7,3},{8,12},{12,8},{9,1... | collective-permute-start | bytes 393224 | tf_op jit(solution)/shard_map/ppermute | solution.py:296
  118.1 6.6 %collective-permute-done.3._.other_ref = bf16[256,256]{1,0:T(8,128)(2,1)S(1)} collective-permute-done((bf16[256,256]{1,0:T(8,128)(2,1)S(1)}, bf16[256,256]{1,0:T(8,128)(2,1)S(1)}, u32[]{:S(2)}, u32[]{:S(2)}) %collective-permute-start.3) | collective-permute-done | bytes 131104 | tf_op jit(solution)/shard_map/ppermute | solution.py:296
  124.7 0.9 all-to-all-done.3.parts_ref
  125.6 0.8 spread.1
  126.5 25.3 %all_to_all.25 = bf16[128,8,128]{2,1,0:T(8,128)(2,1)S(1)} all-to-all(bf16[128,8,128]{2,1,0:T(8,128)(2,1)S(1)} %bitcast.20), channel_id=1, replica_groups=mesh['seq'=64,'h'=2,'x'=4] {'seq','h'}, dimensions={0} | all-to-all | bytes 524288 | tf_op jit(solution)/shard_map/all_to_all | solution.py:229
  151.8 1.2 finish.1
  (2 shorter events, 0.0 us)
Async XLA Ops:
  2.0 15.4 %copy-start.11 = (s32[256,3]{0,1:T(4,128)S(1)}, s32[256,3]{0,1:T(4,128)}, u32[]{:S(2)}) copy-start(s32[256,3]{0,1:T(4,128)} %param.12) | copy-start | bytes 9220
  2.0 29.0 %all-to-all-start = ((bf16[64,8,256]{2,1,0:T(8,128)(2,1)}), bf16[64,8,256]{2,1,0:T(8,128)(2,1)S(1)}, u32[]{:S(2)}, u32[]{:S(2)}) async-start(bf16[64,8,256]{2,1,0:T(8,128)(2,1)} %bitcast.21), calls=%async_computation | async-start | bytes 524288 | tf_op jit(solution)/shard_map/all_to_all | solution.py:229
  17.8 0.6 copy-start.10
  32.5 33.4 %copy-start.4 = (bf16[256,256]{1,0:T(8,128)(2,1)S(1)}, bf16[256,256]{1,0:T(8,128)(2,1)}, u32[]{:S(2)}) copy-start(bf16[256,256]{1,0:T(8,128)(2,1)} %k_ref.1) | copy-start | bytes 393220
  32.5 33.4 %copy-start.5 = (bf16[256,256]{1,0:T(8,128)(2,1)S(1)}, bf16[256,256]{1,0:T(8,128)(2,1)}, u32[]{:S(2)}) copy-start(bf16[256,256]{1,0:T(8,128)(2,1)} %v_ref.1) | copy-start | bytes 393220
  32.6 33.4 %copy-start.8 = (bf16[256,256]{1,0:T(8,128)(2,1)S(1)}, bf16[256,256]{1,0:T(8,128)(2,1)}, u32[]{:S(2)}) copy-start(bf16[256,256]{1,0:T(8,128)(2,1)} %q_ref.1) | copy-start | bytes 393220
  32.6 33.4 %copy-start.9 = (bf16[256,256]{1,0:T(8,128)(2,1)S(1)}, bf16[256,256]{1,0:T(8,128)(2,1)}, u32[]{:S(2)}) copy-start(bf16[256,256]{1,0:T(8,128)(2,1)} %g_ref.1) | copy-start | bytes 393220
  32.6 33.3 %all-to-all-start.1 = ((bf16[64,16,512]{2,1,0:T(8,128)(2,1)}), bf16[64,16,512]{2,1,0:T(8,128)(2,1)S(1)}, u32[]{:S(2)}, u32[]{:S(2)}) async-start(bf16[64,16,512]{2,1,0:T(8,128)(2,1)} %bitcast.5), calls=%async_computation.1 | async-start | bytes 2097152 | tf_op jit(solution)/shard_map/all_to_all | solution.py:229
  69.5 1.0 copy-start.2
  70.5 6.2 %copy-start = (bf16[2048,256]{1,0:T(8,128)(2,1)S(1)}, bf16[2048,256]{1,0:T(8,128)(2,1)}, u32[]{:S(2)}) copy-start(bf16[2048,256]{1,0:T(8,128)(2,1)} %wk_ref.1) | copy-start | bytes 3145732
  70.5 6.2 %copy-start.1 = (bf16[2048,256]{1,0:T(8,128)(2,1)S(1)}, bf16[2048,256]{1,0:T(8,128)(2,1)}, u32[]{:S(2)}) copy-start(bf16[2048,256]{1,0:T(8,128)(2,1)} %wv_ref.1) | copy-start | bytes 3145732
  70.5 34.7 %all-to-all-start.2 = ((bf16[64,16,512]{2,1,0:T(8,128)(2,1)}), bf16[64,16,512]{2,1,0:T(8,128)(2,1)S(1)}, u32[]{:S(2)}, u32[]{:S(2)}) async-start(bf16[64,16,512]{2,1,0:T(8,128)(2,1)} %bitcast.19), calls=%async_computation.2 | async-start | bytes 2097152 | tf_op jit(solution)/shard_map/all_to_all | solution.py:229
  76.7 1.2 copy-start.3
  80.2 0.7 copy-start.6
  80.9 11.4 %collective-permute-start = (bf16[256,512]{1,0:T(8,128)(2,1)}, bf16[256,512]{1,0:T(8,128)(2,1)S(1)}, u32[]{:S(2)}, u32[]{:S(2)}) collective-permute-start(bf16[256,512]{1,0:T(8,128)(2,1)} %get-tuple-element.19), channel_id=1, source_target_pairs={{0,1},{1,2},{2,3},{3,0},{4,5},{5,6},{6,7},{7,4},{8,9},{9,10},{10,1... | collective-permute-start | bytes 786440 | tf_op jit(solution)/shard_map/ppermute | solution.py:287
  84.1 14.3 %collective-permute-start.1 = (bf16[256,512]{1,0:T(8,128)(2,1)}, bf16[256,512]{1,0:T(8,128)(2,1)}, u32[]{:S(2)}, u32[]{:S(2)}) collective-permute-start(bf16[256,512]{1,0:T(8,128)(2,1)} %get-tuple-element.20), channel_id=1, source_target_pairs={{0,2},{1,3},{2,0},{3,1},{4,6},{5,7},{6,4},{7,5},{8,10},{9,11},{10,... | collective-permute-start | bytes 786440 | tf_op jit(solution)/shard_map/ppermute | solution.py:287
  88.4 11.1 %collective-permute-start.2 = (bf16[256,512]{1,0:T(8,128)(2,1)}, bf16[256,512]{1,0:T(8,128)(2,1)}, u32[]{:S(2)}, u32[]{:S(2)}) collective-permute-start(bf16[256,512]{1,0:T(8,128)(2,1)} %get-tuple-element.21), channel_id=1, source_target_pairs={{0,3},{1,0},{2,1},{3,2},{4,7},{5,4},{6,5},{7,6},{8,11},{9,8},{10,9... | collective-permute-start | bytes 786440 | tf_op jit(solution)/shard_map/ppermute | solution.py:287
  108.0 4.2 %copy-start.7 = (bf16[256,512]{1,0:T(8,128)(2,1)S(1)}, bf16[256,512]{1,0:T(8,128)(2,1)}, u32[]{:S(2)}) copy-start(bf16[256,512]{1,0:T(8,128)(2,1)} %copy-done.6) | copy-start | bytes 786436
  108.0 17.7 %all-to-all-start.3 = ((bf16[4,256,512]{2,1,0:T(8,128)(2,1)}), bf16[4,256,512]{2,1,0:T(8,128)(2,1)S(1)}, u32[]{:S(2)}, u32[]{:S(2)}) async-start(bf16[4,256,512]{2,1,0:T(8,128)(2,1)} %project.1), calls=%async_computation.3 | async-start | bytes 2097152 | tf_op jit(solution)/shard_map/all_to_all | solution.py:316
  113.3 11.4 %collective-permute-start.3 = (bf16[256,256]{1,0:T(8,128)(2,1)S(1)}, bf16[256,256]{1,0:T(8,128)(2,1)S(1)}, u32[]{:S(2)}, u32[]{:S(2)}) collective-permute-start(bf16[256,256]{1,0:T(8,128)(2,1)S(1)} %get-tuple-element.23), channel_id=1, source_target_pairs={{0,4},{4,0},{1,5},{5,1},{2,6},{6,2},{3,7},{7,3},{8,12},{12,8},{9,1... | collective-permute-start | bytes 393224 | tf_op jit(solution)/shard_map/ppermute | solution.py:296

commit v5 on v4

--- a/solution.py
+++ b/solution.py
@@ -14,7 +14,7 @@
 GLOB = 2
 RAND = 3
 PER = 4
-SLOTS = GLOB + 2 + PER * RAND
+FOLDED = 6
 X_SIZE = 4
 VMEM_LIMIT = 40 * 1024 * 1024
 
@@ -57,54 +57,110 @@
     out_ref[...] = rows.astype(jnp.bfloat16)
 
 
-def pick_kernel(index_ref, stripes_ref, out_hbm, rows_ref, sems):
+def fold(rows, quarter):
+    to, source = iotas(*rows)
+    return (to >> 3 == source >> 1) & ((to >> 1) & 3 == quarter) & (to & 1 == source & 1)
+
+
+def fold_turned(rows, quarter):
+    source, to = iotas(*rows)
+    return (to >> 3 == source >> 1) & ((to >> 1) & 3 == quarter) & (to & 1 == source & 1)
+
+
+def pick_kernel(
+    index_ref, stripes_ref, keys_hbm, values_hbm, out_hbm, first_hbm, last_hbm, rows_ref, sems, rim_sems
+):
+    copies = []
+    for at, (rim_hbm, row) in enumerate(((first_hbm, 0), (last_hbm, (PER - 1) * BLK))):
+        for kind, source in enumerate((keys_hbm, values_hbm)):
+            copies.append(
+                pltpu.make_async_copy(source.at[pl.ds(row, BLK)], rim_hbm.at[kind], rim_sems.at[at, kind])
+            )
+            copies[-1].start()
     block, row = iotas(256, 512)
     table = []
     for kind in range(2):
         source = (block >> 2) * 8 + kind * 4 + (block & 3)
         table.append(nn(one_hot(row == source), stripes_ref[...]).astype(jnp.bfloat16))
-    chunk = rows_ref.shape[0] // sems.shape[0]
-    _, block = iotas(chunk, 256)
-    copies = []
-    for at in range(sems.shape[0]):
-        rows = slice(at * chunk, (at + 1) * chunk)
+    _, block = iotas(256, 256)
+    for at in range(0, 512, 256):
+        rows = slice(at, at + 256)
         hits = one_hot(block == index_ref[rows, :])
         for kind in range(2):
             lanes = slice(kind * 256, (kind + 1) * 256)
             rows_ref[rows, lanes] = nn(hits, table[kind]).astype(jnp.bfloat16)
-        copies.append(pltpu.make_async_copy(rows_ref.at[rows], out_hbm.at[rows], sems.at[at]))
+        copies.append(
+            pltpu.make_async_copy(
+                rows_ref.at[rows, 0:512], out_hbm.at[rows, 0:512], sems.at[at // 256]
+            )
+        )
         copies[-1].start()
+    _, block = iotas(128, 256)
+    pairs = []
+    for pair in range(FOLDED // 2):
+        hits = one_hot(block == index_ref[512 + pair * 128 : 640 + pair * 128, :])
+        pairs.append([nn(hits, table[kind]).astype(jnp.bfloat16) for kind in range(2)])
+    folded = None
+    for quarter in range(4):
+        lanes = slice((quarter & 1) * HD, (quarter & 1) * HD + HD)
+        rows = jnp.concatenate([pair[quarter >> 1][:, lanes] for pair in pairs], axis=1)
+        part = nn(one_hot(fold((512, 128), quarter)), rows)
+        folded = part if folded is None else folded + part
+    rows_ref[:, 512:] = folded.astype(jnp.bfloat16)
+    copies.append(pltpu.make_async_copy(rows_ref.at[:, 512:], out_hbm.at[:, 512:], sems.at[2]))
+    copies[-1].start()
     for copy in copies:
         copy.wait()
 
 
 def attention_kernel(
-    where_ref, q_ref, k_ref, v_ref, g_ref, remote_ref, dq_ref, dk_ref, dv_ref, shares_ref
+    where_ref, q_ref, k_ref, v_ref, g_ref, far_ref, left_ref, right_ref, dq_ref, dk_ref, dv_ref, shares_ref, part_ref
 ):
     scale = 1.0 / math.sqrt(HD)
     first_block = where_ref[0] * PER
     key_row, q_row = iotas(256, 256)
     q_block = q_row >> 6
     own_gap = (key_row >> 6) - q_block
-    own_mask = (own_gap >= -1) & (own_gap <= 1)
-    slot = key_row & (SLOTS - 1)
-    offset = slot - (GLOB + 2) - RAND * q_block
-    in_window = ((first_block + q_block - slot + 1) & 255) <= 2
-    far_mask = (
-        ((slot < GLOB) & jnp.logical_not(in_window))
-        | ((slot == GLOB) & (q_block == 0))
-        | ((slot == GLOB + 1) & (q_block == PER - 1))
-        | ((slot >= GLOB + 2) & (offset >= 0) & (offset < RAND))
-    )
+
+    def listed(draw):
+        offset = draw - RAND * q_block
+        return (offset >= 0) & (offset < RAND)
+
+    in_window = ((first_block + q_block - (key_row & 1) + 1) & 255) <= 2
+    masks = [
+        (own_gap >= -1) & (own_gap <= 1),
+        listed(key_row & 7),
+        listed(key_row & 7),
+        listed(8 + 2 * (key_row >> 7) + (key_row & 1)),
+        ((key_row < 128) & jnp.logical_not(in_window))
+        | ((key_row >= 128) & (key_row < 192) & (q_block == 0))
+        | ((key_row >= 192) & (q_block == PER - 1)),
+    ]
+    unfold = [
+        nn(one_hot(fold_turned((128, 512), quarter)), far_ref[:, 512:]).astype(jnp.bfloat16)
+        for quarter in range(4)
+    ]
     for head in range(2):
         lanes = slice(head * HD, (head + 1) * HD)
-        value_lanes = slice(256 + head * HD, 256 + (head + 1) * HD)
         q = q_ref[:, lanes]
         g = g_ref[:, lanes]
-        far_rows = [slice(at, at + 256) for at in range(0, remote_ref.shape[0], 256)]
-        key_parts = [k_ref[:, lanes]] + [remote_ref[rows, lanes] for rows in far_rows]
-        value_parts = [v_ref[:, lanes]] + [remote_ref[rows, value_lanes] for rows in far_rows]
-        masks = [own_mask] + [far_mask] * len(far_rows)
+
+        def parts(own_ref, kind):
+            far_lanes = slice(kind * 256 + head * HD, kind * 256 + (head + 1) * HD)
+            folded = [
+                unfold[2 * kind + head][:, pair * HD : (pair + 1) * HD] for pair in range(FOLDED // 2)
+            ]
+            rims = [left_ref[kind, :, lanes], right_ref[kind, :, lanes]]
+            return [
+                own_ref[:, lanes],
+                far_ref[0:256, far_lanes],
+                far_ref[256:512, far_lanes],
+                jnp.concatenate(folded[:2], axis=0),
+                jnp.concatenate(folded[2:] + rims, axis=0),
+            ]
+
+        key_parts = parts(k_ref, 0)
+        value_parts = parts(v_ref, 1)
         weighted = [
             jnp.where(mask, jnp.exp(nt(k, q) * scale), 0.0) for k, mask in zip(key_parts, masks)
         ]
@@ -123,6 +179,7 @@
         grad_low = [(p * (d - delta)).astype(jnp.bfloat16) for p, d in zip(probs, grad_probs)]
         dq = functools.reduce(jnp.add, [tn(k, w) for k, w in zip(key_parts, grad_low)])
         dq_ref[:, lanes] = (scale * dq).T.astype(jnp.bfloat16)
+        value_lanes = slice(256 + head * HD, 256 + (head + 1) * HD)
         for part in range(len(masks)):
             dk = (scale * nn(grad_low[part], q)).astype(jnp.bfloat16)
             dv = nn(probs_low[part], g).astype(jnp.bfloat16)
@@ -130,8 +187,18 @@
                 dk_ref[:, lanes] = dk
                 dv_ref[:, lanes] = dv
             else:
-                shares_ref[far_rows[part - 1], lanes] = dk
-                shares_ref[far_rows[part - 1], value_lanes] = dv
+                rows = slice(((part - 1) & 1) * 256, ((part - 1) & 1) * 256 + 256)
+                to = shares_ref if part < 3 else part_ref
+                to[rows, lanes] = dk
+                to[rows, value_lanes] = dv
+    to, source = iotas(512, 512)
+    slot = to & 7
+    wanted = jnp.where(
+        slot < FOLDED,
+        (slot >> 1) * 128 + (to >> 3) * 2 + (slot & 1),
+        384 + (slot - FOLDED) * BLK + (to >> 3),
+    )
+    shares_ref[:, 512:] = nn(one_hot(source == wanted), part_ref[...]).astype(jnp.bfloat16)
 
 
 def own_kernel(where_ref, dq_ref, dk_ref, dv_ref, wq_ref, wk_ref, wv_ref, *outs):
@@ -170,7 +237,13 @@
         for load in pair:
             load.start()
     block, _ = iotas(256, index_ref.shape[1])
-    rows = nn(one_hot(block == index_ref[...]), shares_ref[...]).astype(jnp.bfloat16)
+    rows = None
+    for half in range(2):
+        part = nn(
+            one_hot(block == index_ref[half : half + 1, :]), shares_ref[:, half * 512 : (half + 1) * 512]
+        )
+        rows = part if rows is None else rows + part
+    rows = rows.astype(jnp.bfloat16)
     stores = []
     for x in range(X_SIZE):
         for load in loads[x]:
@@ -232,19 +305,17 @@
 def body(queries, keys, values, out_grad, random_blocks, w_query, w_key, w_value):
     shards = lax.axis_size("seq")
     total_blocks = shards * PER
-    wanted = shards * SLOTS
     width = 2 * HD
     where = jnp.stack([lax.axis_index(name) for name in ("seq", "h", "x")]).astype(jnp.int32)
     first = jnp.arange(shards, dtype=jnp.int32)[:, None] * PER
-    table = jnp.concatenate(
-        [
-            jnp.broadcast_to(jnp.arange(GLOB, dtype=jnp.int32)[None], (shards, GLOB)),
-            (first - 1) % total_blocks,
-            (first + PER) % total_blocks,
-            random_blocks.reshape(shards, PER * RAND),
-        ],
-        axis=1,
+    draws = random_blocks.reshape(shards, PER * RAND)
+    fixed = jnp.broadcast_to(jnp.arange(GLOB, dtype=jnp.int32)[None], (shards, GLOB))
+    plain = draws[:, :8].reshape(-1)
+    ahead = jnp.concatenate(
+        [plain, draws[:, 8:10].reshape(-1), draws[:, 10:].reshape(-1), fixed.reshape(-1)]
     )
+    rims = [(first - 1) % total_blocks, (first + PER) % total_blocks]
+    behind = jnp.stack([plain, jnp.concatenate([draws[:, 8:], fixed] + rims, axis=1).reshape(-1)])
     scalars = pl.BlockSpec(memory_space=pltpu.SMEM)
     whole = pl.BlockSpec()
 
@@ -260,21 +331,31 @@
     stripes = swap(packed, shards, "seq")
 
     outside = pl.BlockSpec(memory_space=pl.ANY)
-    picked = call(
+    lanes = 4 * HD + FOLDED * HD // 2
+    rim = shape((2, BLK, width))
+    picked, first_block, last_block = call(
         pick_kernel,
         "pick",
-        shape((wanted, 2 * width)),
-        out_specs=outside,
-        scratch_shapes=[pltpu.VMEM((wanted, 2 * width), jnp.bfloat16), pltpu.SemaphoreType.DMA((4,))],
-    )(table.reshape(wanted, 1), stripes)
+        [shape((shards * 8, lanes)), rim, rim],
+        in_specs=[whole, whole, in_hbm, in_hbm],
+        out_specs=[outside] * 3,
+        scratch_shapes=[
+            pltpu.VMEM((shards * 8, lanes), jnp.bfloat16),
+            pltpu.SemaphoreType.DMA((3,)),
+            pltpu.SemaphoreType.DMA((2, 2)),
+        ],
+    )(ahead.reshape(-1, 1), stripes, keys, values)
     remote = swap(picked, shards, "seq")
+    left = lax.ppermute(last_block, "seq", [(i, (i + 1) % shards) for i in range(shards)])
+    right = lax.ppermute(first_block, "seq", [(i, (i - 1) % shards) for i in range(shards)])
 
     query_low, own_key, own_value, shares = call(
         attention_kernel,
         "attention",
-        [shape((256, width))] * 3 + [shape((wanted, 2 * width))],
-        in_specs=[scalars] + [whole] * 5,
-    )(where, queries, keys, values, out_grad, remote)
+        [shape((256, width))] * 3 + [shape((shards * 8, 4 * width))],
+        in_specs=[scalars] + [whole] * 7,
+        scratch_shapes=[pltpu.VMEM((512, 2 * width), jnp.bfloat16)],
+    )(where, queries, keys, values, out_grad, remote, left, right)
     returned = swap(shares, shards, "seq")
 
     own = call(
@@ -307,7 +388,7 @@
             pltpu.SemaphoreType.DMA((2, 2 * X_SIZE)),
         ],
     )(
-        table.reshape(1, wanted),
+        behind,
         returned,
         w_key.reshape(2, X_SIZE, 256, width),
         w_value.reshape(2, X_SIZE, 256, width),

time: 154 us -> 153 us (level)
  waiting for transfers between devices: 61.5 us -> 53.3 us
  starting transfers between devices: 45.8 us -> 51.2 us
    all_to_all x3, waiting for transfers between devices: 46.7 us -> 27.9 us  [swap(): lax.all_to_all(cut, axis, split_axis=0, concat_axis=0, tiled=True)]
    ppermute x0 -> x2, waiting for transfers between devices: none -> 10.4 us  [the longest x1 10.4 us: body(): lax.ppermute(last_block, 'seq', [(i, (i + 1) % shards) for i in range(sha...]
    ppermute x0 -> x2, starting transfers between devices: none -> 5.47 us  [the longest x1 3.55 us: body(): lax.ppermute(last_block, 'seq', [(i, (i + 1) % shards) for i in range(sha...]
    unnamed x25 -> x27, local copies, waits for them, and re-layouts: 3.43 us -> 4.09 us
  transfers between devices with their start and end apart: 8 -> 10, of which waited for: 7 -> 8; matrix products, arithmetic and copies ran while one was open for 1% -> 1% of each run, Pallas kernels for 2% -> 2%
where the time goes in v5:
time: 153 us; the launch traced here: 152 us
  waiting for transfers between devices  53.3 us (35%)
  starting transfers between devices  51.2 us (33%)
  blocking collectives  25.3 us (17%)
  Pallas kernels  16.6 us (11%)
  local copies, waits for them, and re-layouts  5.19 us (3%)
    all_to_all x3, waiting for transfers between devices, swap(): lax.all_to_all(cut, axis, split_axis=0, concat_axis=0, tiled=True)  27.9 us
    all_to_all x3, starting transfers between devices, swap(): lax.all_to_all(cut, axis, split_axis=0, concat_axis=0, tiled=True)  26.1 us
    all_to_all x1, blocking collectives, swap(): lax.all_to_all(cut, axis, split_axis=0, concat_axis=0, tiled=True)  25.3 us
    ppermute x3, starting transfers between devices, body(): lax.ppermute(own[shift], 'x', [(i, (i + shift) % X_SIZE) for i in range(X...  10.5 us
    ppermute x1, waiting for transfers between devices, body(): lax.ppermute(last_block, 'seq', [(i, (i + 1) % shards) for i in range(sha...  10.4 us
    ppermute x3, waiting for transfers between devices, body(): lax.ppermute(own[shift], 'x', [(i, (i + shift) % X_SIZE) for i in range(X...  7.64 us
    ppermute x1, waiting for transfers between devices, body(): other = lax.ppermute(theirs, 'h', [(0, 1), (1, 0)])  6.45 us
    ppermute x1, starting transfers between devices, body(): other = lax.ppermute(theirs, 'h', [(0, 1), (1, 0)])  4.94 us
  transfers between devices with their start and end apart: 10, of which 8 were waited for; matrix products, arithmetic and copies ran while one was open for 1% of the time, Pallas kernels for 2%

profile of v5, /device:TPU:1, one launch (start us, length us, event | category | flops | bytes accessed | tf_op | source)
XLA Modules:
  0.0 152.1 jit_solution(12367882538457591254)
XLA Ops:
  0.0 2.0 %pack.1 = bf16[512,256]{1,0:T(8,128)(2,1)} custom-call(bf16[256,256]{1,0:T(8,128)(2,1)} %k_ref.1, bf16[256,256]{1,0:T(8,128)(2,1)} %v_ref.1), custom_call_target="tpu_custom_call" | custom-call | tf_op jit(solution)/shard_map/pack/pallas_call | solution.py:323
  2.0 15.4 %all-to-all-start = ((bf16[64,8,256]{2,1,0:T(8,128)(2,1)}), bf16[64,8,256]{2,1,0:T(8,128)(2,1)S(1)}, u32[]{:S(2)}, u32[]{:S(2)}) async-start(bf16[64,8,256]{2,1,0:T(8,128)(2,1)} %bitcast.24), calls=%async_computation | async-start | bytes 524288 | tf_op jit(solution)/shard_map/all_to_all | solution.py:302
  17.4 0.0 copy-start.12
  17.4 0.1 reshape.146
  17.6 0.5 copy-done.12
  18.1 0.1 copy.15
  18.3 0.1 reshape.142
  18.4 0.0 copy-start.10
  18.4 0.1 reshape.143
  18.5 0.1 fusion.2
  18.5 0.4 copy-done.10
  19.0 0.1 reshape.144
  19.1 0.1 reshape.145
  19.3 0.0 copy-start.2
  19.3 0.0 copy-start.3
  19.3 0.2 reshape.158.index_ref
  19.5 11.5 %all-to-all-done = bf16[64,8,256]{2,1,0:T(8,128)(2,1)S(1)} async-done(((bf16[64,8,256]{2,1,0:T(8,128)(2,1)}), bf16[64,8,256]{2,1,0:T(8,128)(2,1)S(1)}, u32[]{:S(2)}, u32[]{:S(2)}) %all-to-all-start) | async-done | bytes 262176 | tf_op jit(solution)/shard_map/all_to_all | solution.py:302
  31.0 0.0 copy-done.2
  31.0 0.0 copy-done.3
  31.0 2.2 %pick.1 = (bf16[512,896]{1,0:T(8,128)(2,1)}, bf16[2,64,256]{2,1,0:T(8,128)(2,1)S(1)}, bf16[2,64,256]{2,1,0:T(8,128)(2,1)S(1)}) custom-call(s32[896,1]{1,0:T(8,128)S(1)} %reshape.158.index_ref, bf16[512,256]{1,0:T(8,128)(2,1)S(1)} %bitcast.20, bf16[256,256]{1,0:T(8,128)(2,1)S(1)} %copy-done.2, bf16[256,256]{1,0:T(8,128)(2,1)S(1)} %copy-done.3), custom_call_target="tpu_custom_call" | custom-call | tf_op jit(solution)/shard_map/pick/pallas_call | solution.py:336
  33.2 0.0 copy-start.8
  33.2 0.0 copy-start.9
  33.2 4.7 %all-to-all-start.1 = ((bf16[64,8,896]{2,1,0:T(8,128)(2,1)}), bf16[64,8,896]{2,1,0:T(8,128)(2,1)S(1)}, u32[]{:S(2)}, u32[]{:S(2)}) async-start(bf16[64,8,896]{2,1,0:T(8,128)(2,1)} %bitcast.5), calls=%async_computation.1 | async-start | bytes 1835008 | tf_op jit(solution)/shard_map/all_to_all | solution.py:302
  38.0 3.5 %collective-permute-start = (bf16[2,64,256]{2,1,0:T(8,128)(2,1)S(1)}, bf16[2,64,256]{2,1,0:T(8,128)(2,1)S(1)}, u32[]{:S(2)}, u32[]{:S(2)}) collective-permute-start(bf16[2,64,256]{2,1,0:T(8,128)(2,1)S(1)} %get-tuple-element.19), channel_id=1, source_target_pairs={{0,8},{8,16},{16,24},{24,32},{32,40},{40,48},{48,56},{56,64},{64,7... | collective-permute-start | bytes 196616 | tf_op jit(solution)/shard_map/ppermute | solution.py:349
  41.5 1.9 %collective-permute-start.1 = (bf16[2,64,256]{2,1,0:T(8,128)(2,1)S(1)}, bf16[2,64,256]{2,1,0:T(8,128)(2,1)S(1)}, u32[]{:S(2)}, u32[]{:S(2)}) collective-permute-start(bf16[2,64,256]{2,1,0:T(8,128)(2,1)S(1)} %get-tuple-element.20), channel_id=1, source_target_pairs={{0,504},{8,0},{16,8},{24,16},{32,24},{40,32},{48,40},{56,48},{64,5... | collective-permute-start | bytes 196616 | tf_op jit(solution)/shard_map/ppermute | solution.py:350
  43.5 0.1 pad_add_fusion.3.where_ref
  43.5 10.4 %collective-permute-done.left_ref = bf16[2,64,256]{2,1,0:T(8,128)(2,1)S(1)} collective-permute-done((bf16[2,64,256]{2,1,0:T(8,128)(2,1)S(1)}, bf16[2,64,256]{2,1,0:T(8,128)(2,1)S(1)}, u32[]{:S(2)}, u32[]{:S(2)}) %collective-permute-start) | collective-permute-done | bytes 65568 | tf_op jit(solution)/shard_map/ppermute | solution.py:349
  53.9 0.0 collective-permute-done.1.right_ref
  53.9 10.9 %all-to-all-done.1 = bf16[64,8,896]{2,1,0:T(8,128)(2,1)S(1)} async-done(((bf16[64,8,896]{2,1,0:T(8,128)(2,1)}), bf16[64,8,896]{2,1,0:T(8,128)(2,1)S(1)}, u32[]{:S(2)}, u32[]{:S(2)}) %all-to-all-start.1) | async-done | bytes 917536 | tf_op jit(solution)/shard_map/all_to_all | solution.py:302
  64.8 0.0 copy-done.8
  64.8 0.0 copy-done.9
  64.8 4.1 %attention.1 = (bf16[256,256]{1,0:T(8,128)(2,1)S(1)}, bf16[256,256]{1,0:T(8,128)(2,1)S(1)}, bf16[256,256]{1,0:T(8,128)(2,1)S(1)}, bf16[512,1024]{1,0:T(8,128)(2,1)S(1)}) custom-call(s32[3]{0:T(128)S(1)} %pad_add_fusion.3.where_ref, bf16[256,256]{1,0:T(8,128)(2,1)S(1)} %copy-done.8, bf16[256,256]{1,0:T(8,128)(2,1)S(1)} %copy-done.2, ...), custom_call_target="tpu_custom_call" | custom-call | tf_op jit(solution)/shard_map/attention/pallas_call | solution.py:352
  68.9 0.0 copy-start.4
  68.9 1.0 copy-done.4
  69.9 5.9 %all-to-all-start.2 = ((bf16[64,8,1024]{2,1,0:T(8,128)(2,1)}), bf16[64,8,1024]{2,1,0:T(8,128)(2,1)S(1)}, u32[]{:S(2)}, u32[]{:S(2)}) async-start(bf16[64,8,1024]{2,1,0:T(8,128)(2,1)} %bitcast.19), calls=%async_computation.2 | async-start | bytes 2097152 | tf_op jit(solution)/shard_map/all_to_all | solution.py:302
  75.9 0.0 copy-done
  75.9 0.0 copy-done.1
  75.9 0.0 copy-start.5
  75.9 1.2 copy-done.5
  77.1 2.3 %own.1 = (bf16[256,512]{1,0:T(8,128)(2,1)S(1)}, bf16[256,512]{1,0:T(8,128)(2,1)}, bf16[256,512]{1,0:T(8,128)(2,1)}, bf16[256,512]{1,0:T(8,128)(2,1)}) custom-call(s32[3]{0:T(128)S(1)} %pad_add_fusion.3.where_ref, bf16[256,256]{1,0:T(8,128)(2,1)S(1)} %get-tuple-element.22.dq_ref, bf16[256,256]{1,0:T(8,128)(2,1)S(1)} %get-tuple-element.23.dk_ref, ...), custom_call_target="tpu_custom_call" | custom-call | tf_op jit(solution)/shard_map/own/pallas_call | solution.py:361
  79.4 0.7 copy-done.6
  80.1 3.1 %collective-permute-start.2 = (bf16[256,512]{1,0:T(8,128)(2,1)}, bf16[256,512]{1,0:T(8,128)(2,1)S(1)}, u32[]{:S(2)}, u32[]{:S(2)}) collective-permute-start(bf16[256,512]{1,0:T(8,128)(2,1)} %get-tuple-element.25), channel_id=1, source_target_pairs={{0,1},{1,2},{2,3},{3,0},{4,5},{5,6},{6,7},{7,4},{8,9},{9,10},{10,1... | collective-permute-start | bytes 786440 | tf_op jit(solution)/shard_map/ppermute | solution.py:368
  83.3 4.4 %collective-permute-start.3 = (bf16[256,512]{1,0:T(8,128)(2,1)}, bf16[256,512]{1,0:T(8,128)(2,1)}, u32[]{:S(2)}, u32[]{:S(2)}) collective-permute-start(bf16[256,512]{1,0:T(8,128)(2,1)} %get-tuple-element.26), channel_id=1, source_target_pairs={{0,2},{1,3},{2,0},{3,1},{4,6},{5,7},{6,4},{7,5},{8,10},{9,11},{10,... | collective-permute-start | bytes 786440 | tf_op jit(solution)/shard_map/ppermute | solution.py:368
  87.6 0.0 copy-start.11
  87.6 3.0 %collective-permute-start.4 = (bf16[256,512]{1,0:T(8,128)(2,1)}, bf16[256,512]{1,0:T(8,128)(2,1)}, u32[]{:S(2)}, u32[]{:S(2)}) collective-permute-start(bf16[256,512]{1,0:T(8,128)(2,1)} %get-tuple-element.27), channel_id=1, source_target_pairs={{0,3},{1,0},{2,1},{3,2},{4,7},{5,4},{6,5},{7,6},{8,11},{9,8},{10,9... | collective-permute-start | bytes 786440 | tf_op jit(solution)/shard_map/ppermute | solution.py:368
  90.7 0.0 copy-done.11
  90.7 0.1 stack_reshape.6
  90.8 0.1 slice.17
  90.9 0.1 pad_add_fusion
  91.0 0.1 stack_reshape.7
  91.1 0.0 collective-permute-done.2._.refs_1_
  91.1 6.4 %collective-permute-done.3.__.refs_2_ = bf16[256,512]{1,0:T(8,128)(2,1)} collective-permute-done((bf16[256,512]{1,0:T(8,128)(2,1)}, bf16[256,512]{1,0:T(8,128)(2,1)}, u32[]{:S(2)}, u32[]{:S(2)}) %collective-permute-start.3) | collective-permute-done | bytes 262176 | tf_op jit(solution)/shard_map/ppermute | solution.py:368
  97.6 1.2 collective-permute-done.4.___.refs_3_
  98.8 5.6 %all-to-all-done.2 = bf16[64,8,1024]{2,1,0:T(8,128)(2,1)S(1)} async-done(((bf16[64,8,1024]{2,1,0:T(8,128)(2,1)}), bf16[64,8,1024]{2,1,0:T(8,128)(2,1)S(1)}, u32[]{:S(2)}, u32[]{:S(2)}) %all-to-all-start.2) | async-done | bytes 1048608 | tf_op jit(solution)/shard_map/all_to_all | solution.py:302
  104.4 2.8 %project.1 = bf16[4,256,512]{2,1,0:T(8,128)(2,1)} custom-call(s32[2,512]{1,0:T(2,128)S(1)} %pad_add_fusion.1.index_ref, bf16[512,1024]{1,0:T(8,128)(2,1)S(1)} %bitcast.14, bf16[2,4,256,256]{3,2,1,0:T(8,128)(2,1)S(1)} %bitcast.15, bf16[2,4,256,256]{3,2,1,0:T(8,128)(2,1)S(1)} %bitcast.16, bf16[256,512]{1,0:T(8,128)(2,1)S(1)} %collective-permute-done.2._.refs_1_, ...), custom_call_target="tpu_custom_call" | custom-call | tf_op jit(solution)/shard_map/project/pallas_call | solution.py:379
  107.2 0.0 copy-start.7
  107.2 4.1 %all-to-all-start.3 = ((bf16[4,256,512]{2,1,0:T(8,128)(2,1)}), bf16[4,256,512]{2,1,0:T(8,128)(2,1)S(1)}, u32[]{:S(2)}, u32[]{:S(2)}) async-start(bf16[4,256,512]{2,1,0:T(8,128)(2,1)} %project.1), calls=%async_computation.3 | async-start | bytes 2097152 | tf_op jit(solution)/shard_map/all_to_all | solution.py:397
  111.3 1.2 own_sum.1
  112.5 4.9 %collective-permute-start.5 = (bf16[256,256]{1,0:T(8,128)(2,1)S(1)}, bf16[256,256]{1,0:T(8,128)(2,1)S(1)}, u32[]{:S(2)}, u32[]{:S(2)}) collective-permute-start(bf16[256,256]{1,0:T(8,128)(2,1)S(1)} %get-tuple-element.29), channel_id=1, source_target_pairs={{0,4},{4,0},{1,5},{5,1},{2,6},{6,2},{3,7},{7,3},{8,12},{12,8},{9,1... | collective-permute-start | bytes 393224 | tf_op jit(solution)/shard_map/ppermute | solution.py:377
  117.4 6.5 %collective-permute-done.5._.other_ref = bf16[256,256]{1,0:T(8,128)(2,1)S(1)} collective-permute-done((bf16[256,256]{1,0:T(8,128)(2,1)S(1)}, bf16[256,256]{1,0:T(8,128)(2,1)S(1)}, u32[]{:S(2)}, u32[]{:S(2)}) %collective-permute-start.5) | collective-permute-done | bytes 131104 | tf_op jit(solution)/shard_map/ppermute | solution.py:377
  123.9 0.9 all-to-all-done.3.parts_ref
  124.8 0.8 spread.1
  125.7 25.3 %all_to_all.25 = bf16[128,8,128]{2,1,0:T(8,128)(2,1)S(1)} all-to-all(bf16[128,8,128]{2,1,0:T(8,128)(2,1)S(1)} %bitcast.21), channel_id=1, replica_groups=mesh['seq'=64,'h'=2,'x'=4] {'seq','h'}, dimensions={0} | all-to-all | bytes 524288 | tf_op jit(solution)/shard_map/all_to_all | solution.py:302
  151.0 1.1 finish.1
  (9 shorter events, 0.1 us)
Async XLA Ops:
  2.0 29.0 %all-to-all-start = ((bf16[64,8,256]{2,1,0:T(8,128)(2,1)}), bf16[64,8,256]{2,1,0:T(8,128)(2,1)S(1)}, u32[]{:S(2)}, u32[]{:S(2)}) async-start(bf16[64,8,256]{2,1,0:T(8,128)(2,1)} %bitcast.24), calls=%async_computation | async-start | bytes 524288 | tf_op jit(solution)/shard_map/all_to_all | solution.py:302
  17.4 0.7 copy-start.12
  18.4 0.6 copy-start.10
  19.3 11.7 %copy-start.2 = (bf16[256,256]{1,0:T(8,128)(2,1)S(1)}, bf16[256,256]{1,0:T(8,128)(2,1)}, u32[]{:S(2)}) copy-start(bf16[256,256]{1,0:T(8,128)(2,1)} %k_ref.1) | copy-start | bytes 393220
  19.3 11.7 %copy-start.3 = (bf16[256,256]{1,0:T(8,128)(2,1)S(1)}, bf16[256,256]{1,0:T(8,128)(2,1)}, u32[]{:S(2)}) copy-start(bf16[256,256]{1,0:T(8,128)(2,1)} %v_ref.1) | copy-start | bytes 393220
  33.2 31.6 %copy-start.8 = (bf16[256,256]{1,0:T(8,128)(2,1)S(1)}, bf16[256,256]{1,0:T(8,128)(2,1)}, u32[]{:S(2)}) copy-start(bf16[256,256]{1,0:T(8,128)(2,1)} %q_ref.1) | copy-start | bytes 393220
  33.2 31.6 %copy-start.9 = (bf16[256,256]{1,0:T(8,128)(2,1)S(1)}, bf16[256,256]{1,0:T(8,128)(2,1)}, u32[]{:S(2)}) copy-start(bf16[256,256]{1,0:T(8,128)(2,1)} %g_ref.1) | copy-start | bytes 393220
  33.2 31.5 %all-to-all-start.1 = ((bf16[64,8,896]{2,1,0:T(8,128)(2,1)}), bf16[64,8,896]{2,1,0:T(8,128)(2,1)S(1)}, u32[]{:S(2)}, u32[]{:S(2)}) async-start(bf16[64,8,896]{2,1,0:T(8,128)(2,1)} %bitcast.5), calls=%async_computation.1 | async-start | bytes 1835008 | tf_op jit(solution)/shard_map/all_to_all | solution.py:302
  38.0 15.9 %collective-permute-start = (bf16[2,64,256]{2,1,0:T(8,128)(2,1)S(1)}, bf16[2,64,256]{2,1,0:T(8,128)(2,1)S(1)}, u32[]{:S(2)}, u32[]{:S(2)}) collective-permute-start(bf16[2,64,256]{2,1,0:T(8,128)(2,1)S(1)} %get-tuple-element.19), channel_id=1, source_target_pairs={{0,8},{8,16},{16,24},{24,32},{32,40},{40,48},{48,56},{56,64},{64,7... | collective-permute-start | bytes 196616 | tf_op jit(solution)/shard_map/ppermute | solution.py:349
  41.5 12.4 %collective-permute-start.1 = (bf16[2,64,256]{2,1,0:T(8,128)(2,1)S(1)}, bf16[2,64,256]{2,1,0:T(8,128)(2,1)S(1)}, u32[]{:S(2)}, u32[]{:S(2)}) collective-permute-start(bf16[2,64,256]{2,1,0:T(8,128)(2,1)S(1)} %get-tuple-element.20), channel_id=1, source_target_pairs={{0,504},{8,0},{16,8},{24,16},{32,24},{40,32},{48,40},{56,48},{64,5... | collective-permute-start | bytes 196616 | tf_op jit(solution)/shard_map/ppermute | solution.py:350
  68.9 1.0 copy-start.4
  69.9 6.0 %copy-start = (bf16[2048,256]{1,0:T(8,128)(2,1)S(1)}, bf16[2048,256]{1,0:T(8,128)(2,1)}, u32[]{:S(2)}) copy-start(bf16[2048,256]{1,0:T(8,128)(2,1)} %wk_ref.1) | copy-start | bytes 3145732
  69.9 6.0 %copy-start.1 = (bf16[2048,256]{1,0:T(8,128)(2,1)S(1)}, bf16[2048,256]{1,0:T(8,128)(2,1)}, u32[]{:S(2)}) copy-start(bf16[2048,256]{1,0:T(8,128)(2,1)} %wv_ref.1) | copy-start | bytes 3145732
  69.9 34.4 %all-to-all-start.2 = ((bf16[64,8,1024]{2,1,0:T(8,128)(2,1)}), bf16[64,8,1024]{2,1,0:T(8,128)(2,1)S(1)}, u32[]{:S(2)}, u32[]{:S(2)}) async-start(bf16[64,8,1024]{2,1,0:T(8,128)(2,1)} %bitcast.19), calls=%async_computation.2 | async-start | bytes 2097152 | tf_op jit(solution)/shard_map/all_to_all | solution.py:302
  75.9 1.2 copy-start.5
  79.4 0.7 copy-start.6
  80.1 11.0 %collective-permute-start.2 = (bf16[256,512]{1,0:T(8,128)(2,1)}, bf16[256,512]{1,0:T(8,128)(2,1)S(1)}, u32[]{:S(2)}, u32[]{:S(2)}) collective-permute-start(bf16[256,512]{1,0:T(8,128)(2,1)} %get-tuple-element.25), channel_id=1, source_target_pairs={{0,1},{1,2},{2,3},{3,0},{4,5},{5,6},{6,7},{7,4},{8,9},{9,10},{10,1... | collective-permute-start | bytes 786440 | tf_op jit(solution)/shard_map/ppermute | solution.py:368
  83.3 14.3 %collective-permute-start.3 = (bf16[256,512]{1,0:T(8,128)(2,1)}, bf16[256,512]{1,0:T(8,128)(2,1)}, u32[]{:S(2)}, u32[]{:S(2)}) collective-permute-start(bf16[256,512]{1,0:T(8,128)(2,1)} %get-tuple-element.26), channel_id=1, source_target_pairs={{0,2},{1,3},{2,0},{3,1},{4,6},{5,7},{6,4},{7,5},{8,10},{9,11},{10,... | collective-permute-start | bytes 786440 | tf_op jit(solution)/shard_map/ppermute | solution.py:368
  87.6 3.1 %copy-start.11 = (s32[64,12]{1,0:T(8,128)S(1)}, s32[64,12]{1,0:T(8,128)}, u32[]{:S(2)}) copy-start(s32[64,12]{1,0:T(8,128)} %copy-done.10) | copy-start | bytes 9220
  87.6 11.1 %collective-permute-start.4 = (bf16[256,512]{1,0:T(8,128)(2,1)}, bf16[256,512]{1,0:T(8,128)(2,1)}, u32[]{:S(2)}, u32[]{:S(2)}) collective-permute-start(bf16[256,512]{1,0:T(8,128)(2,1)} %get-tuple-element.27), channel_id=1, source_target_pairs={{0,3},{1,0},{2,1},{3,2},{4,7},{5,4},{6,5},{7,6},{8,11},{9,8},{10,9... | collective-permute-start | bytes 786440 | tf_op jit(solution)/shard_map/ppermute | solution.py:368
  107.2 4.1 %copy-start.7 = (bf16[256,512]{1,0:T(8,128)(2,1)S(1)}, bf16[256,512]{1,0:T(8,128)(2,1)}, u32[]{:S(2)}) copy-start(bf16[256,512]{1,0:T(8,128)(2,1)} %copy-done.6) | copy-start | bytes 786436
  107.2 17.6 %all-to-all-start.3 = ((bf16[4,256,512]{2,1,0:T(8,128)(2,1)}), bf16[4,256,512]{2,1,0:T(8,128)(2,1)S(1)}, u32[]{:S(2)}, u32[]{:S(2)}) async-start(bf16[4,256,512]{2,1,0:T(8,128)(2,1)} %project.1), calls=%async_computation.3 | async-start | bytes 2097152 | tf_op jit(solution)/shard_map/all_to_all | solution.py:397
  112.5 11.4 %collective-permute-start.5 = (bf16[256,256]{1,0:T(8,128)(2,1)S(1)}, bf16[256,256]{1,0:T(8,128)(2,1)S(1)}, u32[]{:S(2)}, u32[]{:S(2)}) collective-permute-start(bf16[256,256]{1,0:T(8,128)(2,1)S(1)} %get-tuple-element.29), channel_id=1, source_target_pairs={{0,4},{4,0},{1,5},{5,1},{2,6},{6,2},{3,7},{7,3},{8,12},{12,8},{9,1... | collective-permute-start | bytes 393224 | tf_op jit(solution)/shard_map/ppermute | solution.py:377

commit v6 on v5

--- a/solution.py
+++ b/solution.py
@@ -57,18 +57,18 @@
     out_ref[...] = rows.astype(jnp.bfloat16)
 
 
-def fold(rows, quarter):
-    to, source = iotas(*rows)
-    return (to >> 3 == source >> 1) & ((to >> 1) & 3 == quarter) & (to & 1 == source & 1)
-
-
-def fold_turned(rows, quarter):
-    source, to = iotas(*rows)
-    return (to >> 3 == source >> 1) & ((to >> 1) & 3 == quarter) & (to & 1 == source & 1)
-
-
 def pick_kernel(
-    index_ref, stripes_ref, keys_hbm, values_hbm, out_hbm, first_hbm, last_hbm, rows_ref, sems, rim_sems
+    index_ref,
+    stripes_ref,
+    keys_hbm,
+    values_hbm,
+    out_hbm,
+    first_hbm,
+    last_hbm,
+    rows_ref,
+    wide_ref,
+    sems,
+    rim_sems,
 ):
     copies = []
     for at, (rim_hbm, row) in enumerate(((first_hbm, 0), (last_hbm, (PER - 1) * BLK))):
@@ -77,11 +77,15 @@
                 pltpu.make_async_copy(source.at[pl.ds(row, BLK)], rim_hbm.at[kind], rim_sems.at[at, kind])
             )
             copies[-1].start()
-    block, row = iotas(256, 512)
+    for half in range(2):
+        wide_ref[half] = stripes_ref[:, half * HD : (half + 1) * HD].astype(jnp.float32)
     table = []
     for kind in range(2):
-        source = (block >> 2) * 8 + kind * 4 + (block & 3)
-        table.append(nn(one_hot(row == source), stripes_ref[...]).astype(jnp.bfloat16))
+        parts = []
+        for half in range(2):
+            rows = [wide_ref[half, pl.ds(kind * PER + b, 64, stride=8), :] for b in range(PER)]
+            parts.append(jnp.concatenate(rows, axis=0).astype(jnp.bfloat16))
+        table.append(jnp.concatenate(parts, axis=1))
     _, block = iotas(256, 256)
     for at in range(0, 512, 256):
         rows = slice(at, at + 256)
@@ -95,18 +99,19 @@
             )
         )
         copies[-1].start()
-    _, block = iotas(128, 256)
-    pairs = []
+    _, block = iotas(64 * FOLDED, 256)
+    hits = one_hot(block == index_ref[512 : 512 + 64 * FOLDED, :])
+    for kind in range(2):
+        rows = nn(hits, table[kind])
+        for slot in range(FOLDED):
+            for head in range(2):
+                to = (2 * kind + head) * 2 + slot % 2
+                wide_ref[slot // 2, pl.ds(to, 64, stride=8), :] = rows[
+                    slot * 64 : (slot + 1) * 64, head * HD : (head + 1) * HD
+                ]
     for pair in range(FOLDED // 2):
-        hits = one_hot(block == index_ref[512 + pair * 128 : 640 + pair * 128, :])
-        pairs.append([nn(hits, table[kind]).astype(jnp.bfloat16) for kind in range(2)])
-    folded = None
-    for quarter in range(4):
-        lanes = slice((quarter & 1) * HD, (quarter & 1) * HD + HD)
-        rows = jnp.concatenate([pair[quarter >> 1][:, lanes] for pair in pairs], axis=1)
-        part = nn(one_hot(fold((512, 128), quarter)), rows)
-        folded = part if folded is None else folded + part
-    rows_ref[:, 512:] = folded.astype(jnp.bfloat16)
+        lanes = slice(512 + pair * HD, 512 + (pair + 1) * HD)
+        rows_ref[:, lanes] = wide_ref[pair].astype(jnp.bfloat16)
     copies.append(pltpu.make_async_copy(rows_ref.at[:, 512:], out_hbm.at[:, 512:], sems.at[2]))
     copies[-1].start()
     for copy in copies:
@@ -114,7 +119,7 @@
 
 
 def attention_kernel(
-    where_ref, q_ref, k_ref, v_ref, g_ref, far_ref, left_ref, right_ref, dq_ref, dk_ref, dv_ref, shares_ref, part_ref
+    where_ref, q_ref, k_ref, v_ref, g_ref, far_ref, left_ref, right_ref, dq_ref, dk_ref, dv_ref, shares_ref, folded_ref, wide_ref
 ):
     scale = 1.0 / math.sqrt(HD)
     first_block = where_ref[0] * PER
@@ -126,20 +131,18 @@
         offset = draw - RAND * q_block
         return (offset >= 0) & (offset < RAND)
 
-    in_window = ((first_block + q_block - (key_row & 1) + 1) & 255) <= 2
+    in_window = ((first_block + q_block - (key_row >> 6) + 1) & 255) <= 2
     masks = [
         (own_gap >= -1) & (own_gap <= 1),
         listed(key_row & 7),
         listed(key_row & 7),
-        listed(8 + 2 * (key_row >> 7) + (key_row & 1)),
+        listed(8 + (key_row >> 6)),
         ((key_row < 128) & jnp.logical_not(in_window))
         | ((key_row >= 128) & (key_row < 192) & (q_block == 0))
         | ((key_row >= 192) & (q_block == PER - 1)),
     ]
-    unfold = [
-        nn(one_hot(fold_turned((128, 512), quarter)), far_ref[:, 512:]).astype(jnp.bfloat16)
-        for quarter in range(4)
-    ]
+    for pair in range(FOLDED // 2):
+        folded_ref[pair] = far_ref[:, 512 + pair * HD : 512 + (pair + 1) * HD].astype(jnp.float32)
     for head in range(2):
         lanes = slice(head * HD, (head + 1) * HD)
         q = q_ref[:, lanes]
@@ -147,16 +150,18 @@
 
         def parts(own_ref, kind):
             far_lanes = slice(kind * 256 + head * HD, kind * 256 + (head + 1) * HD)
+            quarter = 2 * kind + head
             folded = [
-                unfold[2 * kind + head][:, pair * HD : (pair + 1) * HD] for pair in range(FOLDED // 2)
+                folded_ref[slot // 2, pl.ds(2 * quarter + slot % 2, 64, stride=8), :].astype(jnp.bfloat16)
+                for slot in range(FOLDED)
             ]
             rims = [left_ref[kind, :, lanes], right_ref[kind, :, lanes]]
             return [
                 own_ref[:, lanes],
                 far_ref[0:256, far_lanes],
                 far_ref[256:512, far_lanes],
-                jnp.concatenate(folded[:2], axis=0),
-                jnp.concatenate(folded[2:] + rims, axis=0),
+                jnp.concatenate(folded[:4], axis=0),
+                jnp.concatenate(folded[4:] + rims, axis=0),
             ]
 
         key_parts = parts(k_ref, 0)
@@ -181,24 +186,24 @@
         dq_ref[:, lanes] = (scale * dq).T.astype(jnp.bfloat16)
         value_lanes = slice(256 + head * HD, 256 + (head + 1) * HD)
         for part in range(len(masks)):
-            dk = (scale * nn(grad_low[part], q)).astype(jnp.bfloat16)
-            dv = nn(probs_low[part], g).astype(jnp.bfloat16)
+            dk = scale * nn(grad_low[part], q)
+            dv = nn(probs_low[part], g)
             if part == 0:
-                dk_ref[:, lanes] = dk
-                dv_ref[:, lanes] = dv
+                dk_ref[:, lanes] = dk.astype(jnp.bfloat16)
+                dv_ref[:, lanes] = dv.astype(jnp.bfloat16)
+            elif part < 3:
+                rows = slice((part - 1) * 256, part * 256)
+                shares_ref[rows, lanes] = dk.astype(jnp.bfloat16)
+                shares_ref[rows, value_lanes] = dv.astype(jnp.bfloat16)
             else:
-                rows = slice(((part - 1) & 1) * 256, ((part - 1) & 1) * 256 + 256)
-                to = shares_ref if part < 3 else part_ref
-                to[rows, lanes] = dk
-                to[rows, value_lanes] = dv
-    to, source = iotas(512, 512)
-    slot = to & 7
-    wanted = jnp.where(
-        slot < FOLDED,
-        (slot >> 1) * 128 + (to >> 3) * 2 + (slot & 1),
-        384 + (slot - FOLDED) * BLK + (to >> 3),
-    )
-    shares_ref[:, 512:] = nn(one_hot(source == wanted), part_ref[...]).astype(jnp.bfloat16)
+                for slot in range(4):
+                    rows = slice(slot * 64, (slot + 1) * 64)
+                    to = pl.ds((part - 3) * 4 + slot, 64, stride=8)
+                    wide_ref[head, to, :] = dk[rows]
+                    wide_ref[2 + head, to, :] = dv[rows]
+    for quarter in range(4):
+        lanes = slice(512 + quarter * HD, 512 + (quarter + 1) * HD)
+        shares_ref[:, lanes] = wide_ref[quarter].astype(jnp.bfloat16)
 
 
 def own_kernel(where_ref, dq_ref, dk_ref, dv_ref, wq_ref, wk_ref, wv_ref, *outs):
@@ -272,15 +277,16 @@
     out_ref[...] = rows.astype(jnp.bfloat16)
 
 
-def finish_kernel(rows_ref, mine_ref, other_ref, out_ref):
-    token, row = iotas(256, rows_ref.shape[0])
-    here = ((row >> 4) == (token & 63)) & ((row & 3) == (token >> 6))
-    rows = rows_ref[...]
+def finish_kernel(rows_ref, mine_ref, other_ref, out_ref, wide_ref):
+    wide_ref[...] = rows_ref[...].astype(jnp.float32)
     for half in range(2):
-        lanes = slice(half * 128, (half + 1) * 128)
-        far = nn(one_hot(here & (((row >> 2) & 1) == half)), rows)
+        lanes = slice(half * HD, (half + 1) * HD)
+        far = []
+        for b in range(PER):
+            senders = [wide_ref[pl.ds(h * 8 + half * PER + b, 64, stride=16), :] for h in range(2)]
+            far.append(senders[0] + senders[1])
         near = mine_ref[:, lanes] + other_ref[:, lanes].astype(jnp.float32)
-        out_ref[:, lanes] = (far + near).astype(jnp.bfloat16)
+        out_ref[:, lanes] = (jnp.concatenate(far, axis=0) + near).astype(jnp.bfloat16)
 
 
 def params(limit):
@@ -311,9 +317,8 @@
     draws = random_blocks.reshape(shards, PER * RAND)
     fixed = jnp.broadcast_to(jnp.arange(GLOB, dtype=jnp.int32)[None], (shards, GLOB))
     plain = draws[:, :8].reshape(-1)
-    ahead = jnp.concatenate(
-        [plain, draws[:, 8:10].reshape(-1), draws[:, 10:].reshape(-1), fixed.reshape(-1)]
-    )
+    ahead = jnp.concatenate([plain, draws[:, 8:].T.reshape(-1), fixed.T.reshape(-1)])
+    ahead = (ahead % PER) * shards + ahead // PER
     rims = [(first - 1) % total_blocks, (first + PER) % total_blocks]
     behind = jnp.stack([plain, jnp.concatenate([draws[:, 8:], fixed] + rims, axis=1).reshape(-1)])
     scalars = pl.BlockSpec(memory_space=pltpu.SMEM)
@@ -341,6 +346,7 @@
         out_specs=[outside] * 3,
         scratch_shapes=[
             pltpu.VMEM((shards * 8, lanes), jnp.bfloat16),
+            pltpu.VMEM((FOLDED // 2, shards * 8, HD), jnp.float32),
             pltpu.SemaphoreType.DMA((3,)),
             pltpu.SemaphoreType.DMA((2, 2)),
         ],
@@ -354,7 +360,10 @@
         "attention",
         [shape((256, width))] * 3 + [shape((shards * 8, 4 * width))],
         in_specs=[scalars] + [whole] * 7,
-        scratch_shapes=[pltpu.VMEM((512, 2 * width), jnp.bfloat16)],
+        scratch_shapes=[
+            pltpu.VMEM((FOLDED // 2, shards * 8, HD), jnp.float32),
+            pltpu.VMEM((4, shards * 8, HD), jnp.float32),
+        ],
     )(where, queries, keys, values, out_grad, remote, left, right)
     returned = swap(shares, shards, "seq")
 
@@ -399,7 +408,12 @@
         spread_kernel, "spread", shape((shards * 16, 128)), in_specs=[whole, outside]
     )(parts, other)
     rows = swap(spread, 2 * shards, ("seq", "h"))
-    return call(finish_kernel, "finish", shape((256, width)))(rows, mine, other)
+    return call(
+        finish_kernel,
+        "finish",
+        shape((256, width)),
+        scratch_shapes=[pltpu.VMEM((shards * 16, HD), jnp.float32)],
+    )(rows, mine, other)
 
 
 def solution(mesh):

time: 153 us -> 152 us (level)
    unnamed x27 -> x29, local copies, waits for them, and re-layouts: 4.09 us -> 3.76 us
  transfers between devices with their start and end apart: 10 -> 10, of which waited for: 8 -> 8; matrix products, arithmetic and copies ran while one was open for 1% -> 2% of each run, Pallas kernels for 2% -> 2%
where the time goes in v6:
time: 152 us; the launch traced here: 151 us
  waiting for transfers between devices  53 us (35%)
  starting transfers between devices  51 us (34%)
  blocking collectives  25.3 us (17%)
  Pallas kernels  15.2 us (10%)
  local copies, waits for them, and re-layouts  5.28 us (3%)
    all_to_all x3, waiting for transfers between devices, swap(): lax.all_to_all(cut, axis, split_axis=0, concat_axis=0, tiled=True)  28 us
    all_to_all x3, starting transfers between devices, swap(): lax.all_to_all(cut, axis, split_axis=0, concat_axis=0, tiled=True)  26.1 us
    all_to_all x1, blocking collectives, swap(): lax.all_to_all(cut, axis, split_axis=0, concat_axis=0, tiled=True)  25.3 us
    ppermute x3, starting transfers between devices, body(): lax.ppermute(own[shift], 'x', [(i, (i + shift) % X_SIZE) for i in range(X...  10.5 us
    ppermute x1, waiting for transfers between devices, body(): lax.ppermute(last_block, 'seq', [(i, (i + 1) % shards) for i in range(sha...  10.4 us
    ppermute x3, waiting for transfers between devices, body(): lax.ppermute(own[shift], 'x', [(i, (i + shift) % X_SIZE) for i in range(X...  7.03 us
    ppermute x1, waiting for transfers between devices, body(): other = lax.ppermute(theirs, 'h', [(0, 1), (1, 0)])  6.65 us
    ppermute x1, starting transfers between devices, body(): other = lax.ppermute(theirs, 'h', [(0, 1), (1, 0)])  4.76 us
  transfers between devices with their start and end apart: 10, of which 8 were waited for; matrix products, arithmetic and copies ran while one was open for 2% of the time, Pallas kernels for 2%

profile of v6, /device:TPU:1, one launch (start us, length us, event | category | flops | bytes accessed | tf_op | source)
XLA Modules:
  0.0 150.7 jit_solution(4628384896463089796)
XLA Ops:
  0.0 2.0 %pack.1 = bf16[512,256]{1,0:T(8,128)(2,1)} custom-call(bf16[256,256]{1,0:T(8,128)(2,1)} %k_ref.1, bf16[256,256]{1,0:T(8,128)(2,1)} %v_ref.1), custom_call_target="tpu_custom_call" | custom-call | tf_op jit(solution)/shard_map/pack/pallas_call | solution.py:328
  2.0 0.0 copy-start.13
  2.0 15.4 %all-to-all-start = ((bf16[64,8,256]{2,1,0:T(8,128)(2,1)}), bf16[64,8,256]{2,1,0:T(8,128)(2,1)S(1)}, u32[]{:S(2)}, u32[]{:S(2)}) async-start(bf16[64,8,256]{2,1,0:T(8,128)(2,1)} %bitcast.24), calls=%async_computation | async-start | bytes 524288 | tf_op jit(solution)/shard_map/all_to_all | solution.py:308
  17.4 0.1 concatenate.46
  17.5 0.0 copy-done.13
  17.5 0.1 copy.24
  17.7 0.1 reshape.387
  17.8 0.0 copy-start.10
  17.8 0.1 concatenate.44
  17.9 0.7 slice_bitcast_fusion
  18.6 0.0 copy-done.10
  18.6 0.1 copy.25
  18.6 0.1 concatenate.45
  18.7 0.2 copy.26
  18.9 0.0 copy-start.2
  19.0 0.0 copy-start.3
  19.0 0.4 fusion.1.index_ref
  19.4 11.6 %all-to-all-done = bf16[64,8,256]{2,1,0:T(8,128)(2,1)S(1)} async-done(((bf16[64,8,256]{2,1,0:T(8,128)(2,1)}), bf16[64,8,256]{2,1,0:T(8,128)(2,1)S(1)}, u32[]{:S(2)}, u32[]{:S(2)}) %all-to-all-start) | async-done | bytes 262176 | tf_op jit(solution)/shard_map/all_to_all | solution.py:308
  30.9 0.0 copy-done.2
  31.0 0.0 copy-done.3
  31.0 1.6 %pick.1 = (bf16[512,896]{1,0:T(8,128)(2,1)}, bf16[2,64,256]{2,1,0:T(8,128)(2,1)S(1)}, bf16[2,64,256]{2,1,0:T(8,128)(2,1)S(1)}) custom-call(s32[896,1]{1,0:T(8,128)S(1)} %fusion.1.index_ref, bf16[512,256]{1,0:T(8,128)(2,1)S(1)} %bitcast.22, bf16[256,256]{1,0:T(8,128)(2,1)S(1)} %copy-done.2, bf16[256,256]{1,0:T(8,128)(2,1)S(1)} %copy-done.3), custom_call_target="tpu_custom_call" | custom-call | tf_op jit(solution)/shard_map/pick/pallas_call | solution.py:341
  32.5 0.0 copy-start.8
  32.5 0.0 copy-start.9
  32.6 4.7 %all-to-all-start.1 = ((bf16[64,8,896]{2,1,0:T(8,128)(2,1)}), bf16[64,8,896]{2,1,0:T(8,128)(2,1)S(1)}, u32[]{:S(2)}, u32[]{:S(2)}) async-start(bf16[64,8,896]{2,1,0:T(8,128)(2,1)} %bitcast.6), calls=%async_computation.1 | async-start | bytes 1835008 | tf_op jit(solution)/shard_map/all_to_all | solution.py:308
  37.3 3.5 %collective-permute-start = (bf16[2,64,256]{2,1,0:T(8,128)(2,1)S(1)}, bf16[2,64,256]{2,1,0:T(8,128)(2,1)S(1)}, u32[]{:S(2)}, u32[]{:S(2)}) collective-permute-start(bf16[2,64,256]{2,1,0:T(8,128)(2,1)S(1)} %get-tuple-element.19), channel_id=1, source_target_pairs={{0,8},{8,16},{16,24},{24,32},{32,40},{40,48},{48,56},{56,64},{64,7... | collective-permute-start | bytes 196616 | tf_op jit(solution)/shard_map/ppermute | solution.py:355
  40.9 1.9 %collective-permute-start.1 = (bf16[2,64,256]{2,1,0:T(8,128)(2,1)S(1)}, bf16[2,64,256]{2,1,0:T(8,128)(2,1)S(1)}, u32[]{:S(2)}, u32[]{:S(2)}) collective-permute-start(bf16[2,64,256]{2,1,0:T(8,128)(2,1)S(1)} %get-tuple-element.20), channel_id=1, source_target_pairs={{0,504},{8,0},{16,8},{24,16},{32,24},{40,32},{48,40},{56,48},{64,5... | collective-permute-start | bytes 196616 | tf_op jit(solution)/shard_map/ppermute | solution.py:356
  42.8 0.1 pad_add_fusion.3.where_ref
  42.9 10.4 %collective-permute-done.left_ref = bf16[2,64,256]{2,1,0:T(8,128)(2,1)S(1)} collective-permute-done((bf16[2,64,256]{2,1,0:T(8,128)(2,1)S(1)}, bf16[2,64,256]{2,1,0:T(8,128)(2,1)S(1)}, u32[]{:S(2)}, u32[]{:S(2)}) %collective-permute-start) | collective-permute-done | bytes 65568 | tf_op jit(solution)/shard_map/ppermute | solution.py:355
  53.2 0.0 collective-permute-done.1.right_ref
  53.2 10.9 %all-to-all-done.1 = bf16[64,8,896]{2,1,0:T(8,128)(2,1)S(1)} async-done(((bf16[64,8,896]{2,1,0:T(8,128)(2,1)}), bf16[64,8,896]{2,1,0:T(8,128)(2,1)S(1)}, u32[]{:S(2)}, u32[]{:S(2)}) %all-to-all-start.1) | async-done | bytes 917536 | tf_op jit(solution)/shard_map/all_to_all | solution.py:308
  64.1 0.0 copy-done.8
  64.1 0.0 copy-done.9
  64.1 3.7 %attention.1 = (bf16[256,256]{1,0:T(8,128)(2,1)S(1)}, bf16[256,256]{1,0:T(8,128)(2,1)S(1)}, bf16[256,256]{1,0:T(8,128)(2,1)S(1)}, bf16[512,1024]{1,0:T(8,128)(2,1)S(1)}) custom-call(s32[3]{0:T(128)S(1)} %pad_add_fusion.3.where_ref, bf16[256,256]{1,0:T(8,128)(2,1)S(1)} %copy-done.8, bf16[256,256]{1,0:T(8,128)(2,1)S(1)} %copy-done.2, ...), custom_call_target="tpu_custom_call" | custom-call | tf_op jit(solution)/shard_map/attention/pallas_call | solution.py:358
  67.8 0.0 copy-start.4
  67.8 1.0 copy-done.4
  68.8 5.9 %all-to-all-start.2 = ((bf16[64,8,1024]{2,1,0:T(8,128)(2,1)}), bf16[64,8,1024]{2,1,0:T(8,128)(2,1)S(1)}, u32[]{:S(2)}, u32[]{:S(2)}) async-start(bf16[64,8,1024]{2,1,0:T(8,128)(2,1)} %bitcast.21), calls=%async_computation.2 | async-start | bytes 2097152 | tf_op jit(solution)/shard_map/all_to_all | solution.py:308
  74.7 0.0 copy-done
  74.7 0.0 copy-done.1
  74.7 0.0 copy-start.5
  74.8 1.2 copy-done.5
  76.0 2.3 %own.1 = (bf16[256,512]{1,0:T(8,128)(2,1)S(1)}, bf16[256,512]{1,0:T(8,128)(2,1)}, bf16[256,512]{1,0:T(8,128)(2,1)}, bf16[256,512]{1,0:T(8,128)(2,1)}) custom-call(s32[3]{0:T(128)S(1)} %pad_add_fusion.3.where_ref, bf16[256,256]{1,0:T(8,128)(2,1)S(1)} %get-tuple-element.22.dq_ref, bf16[256,256]{1,0:T(8,128)(2,1)S(1)} %get-tuple-element.23.dk_ref, ...), custom_call_target="tpu_custom_call" | custom-call | tf_op jit(solution)/shard_map/own/pallas_call | solution.py:370
  78.3 0.7 copy-done.6
  79.0 3.1 %collective-permute-start.2 = (bf16[256,512]{1,0:T(8,128)(2,1)}, bf16[256,512]{1,0:T(8,128)(2,1)S(1)}, u32[]{:S(2)}, u32[]{:S(2)}) collective-permute-start(bf16[256,512]{1,0:T(8,128)(2,1)} %get-tuple-element.25), channel_id=1, source_target_pairs={{0,1},{1,2},{2,3},{3,0},{4,5},{5,6},{6,7},{7,4},{8,9},{9,10},{10,1... | collective-permute-start | bytes 786440 | tf_op jit(solution)/shard_map/ppermute | solution.py:377
  82.1 4.4 %collective-permute-start.3 = (bf16[256,512]{1,0:T(8,128)(2,1)}, bf16[256,512]{1,0:T(8,128)(2,1)}, u32[]{:S(2)}, u32[]{:S(2)}) collective-permute-start(bf16[256,512]{1,0:T(8,128)(2,1)} %get-tuple-element.26), channel_id=1, source_target_pairs={{0,2},{1,3},{2,0},{3,1},{4,6},{5,7},{6,4},{7,5},{8,10},{9,11},{10,... | collective-permute-start | bytes 786440 | tf_op jit(solution)/shard_map/ppermute | solution.py:377
  86.5 3.1 %collective-permute-start.4 = (bf16[256,512]{1,0:T(8,128)(2,1)}, bf16[256,512]{1,0:T(8,128)(2,1)}, u32[]{:S(2)}, u32[]{:S(2)}) collective-permute-start(bf16[256,512]{1,0:T(8,128)(2,1)} %get-tuple-element.27), channel_id=1, source_target_pairs={{0,3},{1,0},{2,1},{3,2},{4,7},{5,4},{6,5},{7,6},{8,11},{9,8},{10,9... | collective-permute-start | bytes 786440 | tf_op jit(solution)/shard_map/ppermute | solution.py:377
  89.6 0.0 copy-done.11
  89.6 0.0 copy-start.12
  89.6 0.1 stack_reshape.6
  89.7 0.6 copy-done.12
  90.4 0.1 pad_add_fusion
  90.5 0.1 stack_reshape.7
  90.6 0.0 collective-permute-done.2._.refs_1_
  90.6 5.9 %collective-permute-done.3.__.refs_2_ = bf16[256,512]{1,0:T(8,128)(2,1)} collective-permute-done((bf16[256,512]{1,0:T(8,128)(2,1)}, bf16[256,512]{1,0:T(8,128)(2,1)}, u32[]{:S(2)}, u32[]{:S(2)}) %collective-permute-start.3) | collective-permute-done | bytes 262176 | tf_op jit(solution)/shard_map/ppermute | solution.py:377
  96.4 1.2 collective-permute-done.4.___.refs_3_
  97.6 5.6 %all-to-all-done.2 = bf16[64,8,1024]{2,1,0:T(8,128)(2,1)S(1)} async-done(((bf16[64,8,1024]{2,1,0:T(8,128)(2,1)}), bf16[64,8,1024]{2,1,0:T(8,128)(2,1)S(1)}, u32[]{:S(2)}, u32[]{:S(2)}) %all-to-all-start.2) | async-done | bytes 1048608 | tf_op jit(solution)/shard_map/all_to_all | solution.py:308
  103.2 2.8 %project.1 = bf16[4,256,512]{2,1,0:T(8,128)(2,1)} custom-call(s32[2,512]{1,0:T(2,128)S(1)} %pad_add_fusion.1.index_ref, bf16[512,1024]{1,0:T(8,128)(2,1)S(1)} %bitcast.16, bf16[2,4,256,256]{3,2,1,0:T(8,128)(2,1)S(1)} %bitcast.17, bf16[2,4,256,256]{3,2,1,0:T(8,128)(2,1)S(1)} %bitcast.18, bf16[256,512]{1,0:T(8,128)(2,1)S(1)} %collective-permute-done.2._.refs_1_, ...), custom_call_target="tpu_custom_call" | custom-call | tf_op jit(solution)/shard_map/project/pallas_call | solution.py:388
  106.0 4.2 %all-to-all-start.3 = ((bf16[4,256,512]{2,1,0:T(8,128)(2,1)}), bf16[4,256,512]{2,1,0:T(8,128)(2,1)S(1)}, u32[]{:S(2)}, u32[]{:S(2)}) async-start(bf16[4,256,512]{2,1,0:T(8,128)(2,1)} %project.1), calls=%async_computation.3 | async-start | bytes 2097152 | tf_op jit(solution)/shard_map/all_to_all | solution.py:406
  110.2 1.2 own_sum.1
  111.4 4.8 %collective-permute-start.5 = (bf16[256,256]{1,0:T(8,128)(2,1)S(1)}, bf16[256,256]{1,0:T(8,128)(2,1)S(1)}, u32[]{:S(2)}, u32[]{:S(2)}) collective-permute-start(bf16[256,256]{1,0:T(8,128)(2,1)S(1)} %get-tuple-element.29), channel_id=1, source_target_pairs={{0,4},{4,0},{1,5},{5,1},{2,6},{6,2},{3,7},{7,3},{8,12},{12,8},{9,1... | collective-permute-start | bytes 393224 | tf_op jit(solution)/shard_map/ppermute | solution.py:386
  116.1 6.6 %collective-permute-done.5._.other_ref = bf16[256,256]{1,0:T(8,128)(2,1)S(1)} collective-permute-done((bf16[256,256]{1,0:T(8,128)(2,1)S(1)}, bf16[256,256]{1,0:T(8,128)(2,1)S(1)}, u32[]{:S(2)}, u32[]{:S(2)}) %collective-permute-start.5) | collective-permute-done | bytes 131104 | tf_op jit(solution)/shard_map/ppermute | solution.py:386
  122.8 0.9 all-to-all-done.3.parts_ref
  123.7 0.8 spread.1
  124.5 25.3 %all_to_all.25 = bf16[128,8,128]{2,1,0:T(8,128)(2,1)S(1)} all-to-all(bf16[128,8,128]{2,1,0:T(8,128)(2,1)S(1)} %bitcast.23), channel_id=1, replica_groups=mesh['seq'=64,'h'=2,'x'=4] {'seq','h'}, dimensions={0} | all-to-all | bytes 524288 | tf_op jit(solution)/shard_map/all_to_all | solution.py:308
  149.8 0.9 finish.1
  (11 shorter events, 0.1 us)
Async XLA Ops:
  2.0 15.5 %copy-start.13 = (s32[256,3]{0,1:T(4,128)S(1)}, s32[256,3]{0,1:T(4,128)}, u32[]{:S(2)}) copy-start(s32[256,3]{0,1:T(4,128)} %param.12) | copy-start | bytes 9220
  2.0 29.0 %all-to-all-start = ((bf16[64,8,256]{2,1,0:T(8,128)(2,1)}), bf16[64,8,256]{2,1,0:T(8,128)(2,1)S(1)}, u32[]{:S(2)}, u32[]{:S(2)}) async-start(bf16[64,8,256]{2,1,0:T(8,128)(2,1)} %bitcast.24), calls=%async_computation | async-start | bytes 524288 | tf_op jit(solution)/shard_map/all_to_all | solution.py:308
  17.8 0.8 copy-start.10
  18.9 12.0 %copy-start.2 = (bf16[256,256]{1,0:T(8,128)(2,1)S(1)}, bf16[256,256]{1,0:T(8,128)(2,1)}, u32[]{:S(2)}) copy-start(bf16[256,256]{1,0:T(8,128)(2,1)} %k_ref.1) | copy-start | bytes 393220
  19.0 12.0 %copy-start.3 = (bf16[256,256]{1,0:T(8,128)(2,1)S(1)}, bf16[256,256]{1,0:T(8,128)(2,1)}, u32[]{:S(2)}) copy-start(bf16[256,256]{1,0:T(8,128)(2,1)} %v_ref.1) | copy-start | bytes 393220
  32.5 31.6 %copy-start.8 = (bf16[256,256]{1,0:T(8,128)(2,1)S(1)}, bf16[256,256]{1,0:T(8,128)(2,1)}, u32[]{:S(2)}) copy-start(bf16[256,256]{1,0:T(8,128)(2,1)} %q_ref.1) | copy-start | bytes 393220
  32.5 31.6 %copy-start.9 = (bf16[256,256]{1,0:T(8,128)(2,1)S(1)}, bf16[256,256]{1,0:T(8,128)(2,1)}, u32[]{:S(2)}) copy-start(bf16[256,256]{1,0:T(8,128)(2,1)} %g_ref.1) | copy-start | bytes 393220
  32.6 31.5 %all-to-all-start.1 = ((bf16[64,8,896]{2,1,0:T(8,128)(2,1)}), bf16[64,8,896]{2,1,0:T(8,128)(2,1)S(1)}, u32[]{:S(2)}, u32[]{:S(2)}) async-start(bf16[64,8,896]{2,1,0:T(8,128)(2,1)} %bitcast.6), calls=%async_computation.1 | async-start | bytes 1835008 | tf_op jit(solution)/shard_map/all_to_all | solution.py:308
  37.3 15.9 %collective-permute-start = (bf16[2,64,256]{2,1,0:T(8,128)(2,1)S(1)}, bf16[2,64,256]{2,1,0:T(8,128)(2,1)S(1)}, u32[]{:S(2)}, u32[]{:S(2)}) collective-permute-start(bf16[2,64,256]{2,1,0:T(8,128)(2,1)S(1)} %get-tuple-element.19), channel_id=1, source_target_pairs={{0,8},{8,16},{16,24},{24,32},{32,40},{40,48},{48,56},{56,64},{64,7... | collective-permute-start | bytes 196616 | tf_op jit(solution)/shard_map/ppermute | solution.py:355
  40.9 12.4 %collective-permute-start.1 = (bf16[2,64,256]{2,1,0:T(8,128)(2,1)S(1)}, bf16[2,64,256]{2,1,0:T(8,128)(2,1)S(1)}, u32[]{:S(2)}, u32[]{:S(2)}) collective-permute-start(bf16[2,64,256]{2,1,0:T(8,128)(2,1)S(1)} %get-tuple-element.20), channel_id=1, source_target_pairs={{0,504},{8,0},{16,8},{24,16},{32,24},{40,32},{48,40},{56,48},{64,5... | collective-permute-start | bytes 196616 | tf_op jit(solution)/shard_map/ppermute | solution.py:356
  67.8 1.0 copy-start.4
  68.8 5.9 %copy-start = (bf16[2048,256]{1,0:T(8,128)(2,1)S(1)}, bf16[2048,256]{1,0:T(8,128)(2,1)}, u32[]{:S(2)}) copy-start(bf16[2048,256]{1,0:T(8,128)(2,1)} %wk_ref.1) | copy-start | bytes 3145732
  68.8 6.0 %copy-start.1 = (bf16[2048,256]{1,0:T(8,128)(2,1)S(1)}, bf16[2048,256]{1,0:T(8,128)(2,1)}, u32[]{:S(2)}) copy-start(bf16[2048,256]{1,0:T(8,128)(2,1)} %wv_ref.1) | copy-start | bytes 3145732
  68.8 34.4 %all-to-all-start.2 = ((bf16[64,8,1024]{2,1,0:T(8,128)(2,1)}), bf16[64,8,1024]{2,1,0:T(8,128)(2,1)S(1)}, u32[]{:S(2)}, u32[]{:S(2)}) async-start(bf16[64,8,1024]{2,1,0:T(8,128)(2,1)} %bitcast.21), calls=%async_computation.2 | async-start | bytes 2097152 | tf_op jit(solution)/shard_map/all_to_all | solution.py:308
  74.7 1.2 copy-start.5
  78.3 0.7 copy-start.6
  79.0 11.6 %collective-permute-start.2 = (bf16[256,512]{1,0:T(8,128)(2,1)}, bf16[256,512]{1,0:T(8,128)(2,1)S(1)}, u32[]{:S(2)}, u32[]{:S(2)}) collective-permute-start(bf16[256,512]{1,0:T(8,128)(2,1)} %get-tuple-element.25), channel_id=1, source_target_pairs={{0,1},{1,2},{2,3},{3,0},{4,5},{5,6},{6,7},{7,4},{8,9},{9,10},{10,1... | collective-permute-start | bytes 786440 | tf_op jit(solution)/shard_map/ppermute | solution.py:377
  82.1 14.3 %collective-permute-start.3 = (bf16[256,512]{1,0:T(8,128)(2,1)}, bf16[256,512]{1,0:T(8,128)(2,1)}, u32[]{:S(2)}, u32[]{:S(2)}) collective-permute-start(bf16[256,512]{1,0:T(8,128)(2,1)} %get-tuple-element.26), channel_id=1, source_target_pairs={{0,2},{1,3},{2,0},{3,1},{4,6},{5,7},{6,4},{7,5},{8,10},{9,11},{10,... | collective-permute-start | bytes 786440 | tf_op jit(solution)/shard_map/ppermute | solution.py:377
  86.5 3.1 %copy-start.11 = (s32[64,12]{1,0:T(8,128)S(1)}, s32[64,12]{1,0:T(8,128)}, u32[]{:S(2)}) copy-start(s32[64,12]{1,0:T(8,128)} %copy-done.10) | copy-start | bytes 9220
  86.5 11.1 %collective-permute-start.4 = (bf16[256,512]{1,0:T(8,128)(2,1)}, bf16[256,512]{1,0:T(8,128)(2,1)}, u32[]{:S(2)}, u32[]{:S(2)}) collective-permute-start(bf16[256,512]{1,0:T(8,128)(2,1)} %get-tuple-element.27), channel_id=1, source_target_pairs={{0,3},{1,0},{2,1},{3,2},{4,7},{5,4},{6,5},{7,6},{8,11},{9,8},{10,9... | collective-permute-start | bytes 786440 | tf_op jit(solution)/shard_map/ppermute | solution.py:377
  89.6 0.8 copy-start.12
  106.0 4.2 %copy-start.7 = (bf16[256,512]{1,0:T(8,128)(2,1)S(1)}, bf16[256,512]{1,0:T(8,128)(2,1)}, u32[]{:S(2)}) copy-start(bf16[256,512]{1,0:T(8,128)(2,1)} %copy-done.6) | copy-start | bytes 786436
  106.0 17.7 %all-to-all-start.3 = ((bf16[4,256,512]{2,1,0:T(8,128)(2,1)}), bf16[4,256,512]{2,1,0:T(8,128)(2,1)S(1)}, u32[]{:S(2)}, u32[]{:S(2)}) async-start(bf16[4,256,512]{2,1,0:T(8,128)(2,1)} %project.1), calls=%async_computation.3 | async-start | bytes 2097152 | tf_op jit(solution)/shard_map/all_to_all | solution.py:406
  111.4 11.4 %collective-permute-start.5 = (bf16[256,256]{1,0:T(8,128)(2,1)S(1)}, bf16[256,256]{1,0:T(8,128)(2,1)S(1)}, u32[]{:S(2)}, u32[]{:S(2)}) collective-permute-start(bf16[256,256]{1,0:T(8,128)(2,1)S(1)} %get-tuple-element.29), channel_id=1, source_target_pairs={{0,4},{4,0},{1,5},{5,1},{2,6},{6,2},{3,7},{7,3},{8,12},{12,8},{9,1... | collective-permute-start | bytes 393224 | tf_op jit(solution)/shard_map/ppermute | solution.py:386

commit v7 on v6

--- a/solution.py
+++ b/solution.py
@@ -78,7 +78,7 @@
             )
             copies[-1].start()
     for half in range(2):
-        wide_ref[half] = stripes_ref[:, half * HD : (half + 1) * HD].astype(jnp.float32)
+        wide_ref[half, 0:512] = stripes_ref[:, half * HD : (half + 1) * HD].astype(jnp.float32)
     table = []
     for kind in range(2):
         parts = []
@@ -111,7 +111,7 @@
                 ]
     for pair in range(FOLDED // 2):
         lanes = slice(512 + pair * HD, 512 + (pair + 1) * HD)
-        rows_ref[:, lanes] = wide_ref[pair].astype(jnp.bfloat16)
+        rows_ref[:, lanes] = wide_ref[pair, 0:512].astype(jnp.bfloat16)
     copies.append(pltpu.make_async_copy(rows_ref.at[:, 512:], out_hbm.at[:, 512:], sems.at[2]))
     copies[-1].start()
     for copy in copies:
@@ -142,7 +142,7 @@
         | ((key_row >= 192) & (q_block == PER - 1)),
     ]
     for pair in range(FOLDED // 2):
-        folded_ref[pair] = far_ref[:, 512 + pair * HD : 512 + (pair + 1) * HD].astype(jnp.float32)
+        folded_ref[pair, 0:512] = far_ref[:, 512 + pair * HD : 512 + (pair + 1) * HD].astype(jnp.float32)
     for head in range(2):
         lanes = slice(head * HD, (head + 1) * HD)
         q = q_ref[:, lanes]
@@ -203,7 +203,7 @@
                     wide_ref[2 + head, to, :] = dv[rows]
     for quarter in range(4):
         lanes = slice(512 + quarter * HD, 512 + (quarter + 1) * HD)
-        shares_ref[:, lanes] = wide_ref[quarter].astype(jnp.bfloat16)
+        shares_ref[:, lanes] = wide_ref[quarter, 0:512].astype(jnp.bfloat16)
 
 
 def own_kernel(where_ref, dq_ref, dk_ref, dv_ref, wq_ref, wk_ref, wv_ref, *outs):
@@ -263,22 +263,20 @@
         store.wait()
 
 
-def spread_kernel(parts_ref, _, out_ref):
-    total = functools.reduce(
-        jnp.add, [parts_ref[g].astype(jnp.float32) for g in range(X_SIZE)]
-    ).astype(jnp.bfloat16)
-    to, block = iotas(out_ref.shape[0], 256)
-    here = block == ((to >> 4) * 4 + (to & 3))
-    rows = None
+def spread_kernel(parts_ref, _, out_ref, wide_ref):
     for quarter in range(4):
-        hits = one_hot(here & (((to >> 2) & 3) == quarter))
-        part = nn(hits, total[:, quarter * 128 : (quarter + 1) * 128])
-        rows = part if rows is None else rows + part
-    out_ref[...] = rows.astype(jnp.bfloat16)
+        lanes = slice(quarter * HD, (quarter + 1) * HD)
+        for b in range(PER):
+            rows = slice(b * 64, (b + 1) * 64)
+            total = functools.reduce(
+                jnp.add, [parts_ref[g, rows, lanes].astype(jnp.float32) for g in range(X_SIZE)]
+            )
+            wide_ref[pl.ds(quarter * PER + b, 64, stride=16), :] = total
+    out_ref[...] = wide_ref[0:1024].astype(jnp.bfloat16)
 
 
 def finish_kernel(rows_ref, mine_ref, other_ref, out_ref, wide_ref):
-    wide_ref[...] = rows_ref[...].astype(jnp.float32)
+    wide_ref[0:1024] = rows_ref[...].astype(jnp.float32)
     for half in range(2):
         lanes = slice(half * HD, (half + 1) * HD)
         far = []
@@ -318,9 +316,9 @@
     fixed = jnp.broadcast_to(jnp.arange(GLOB, dtype=jnp.int32)[None], (shards, GLOB))
     plain = draws[:, :8].reshape(-1)
     ahead = jnp.concatenate([plain, draws[:, 8:].T.reshape(-1), fixed.T.reshape(-1)])
-    ahead = (ahead % PER) * shards + ahead // PER
     rims = [(first - 1) % total_blocks, (first + PER) % total_blocks]
     behind = jnp.stack([plain, jnp.concatenate([draws[:, 8:], fixed] + rims, axis=1).reshape(-1)])
+    ahead, behind = [(blocks % PER) * shards + blocks // PER for blocks in (ahead, behind)]
     scalars = pl.BlockSpec(memory_space=pltpu.SMEM)
     whole = pl.BlockSpec()
 
@@ -346,7 +344,7 @@
         out_specs=[outside] * 3,
         scratch_shapes=[
             pltpu.VMEM((shards * 8, lanes), jnp.bfloat16),
-            pltpu.VMEM((FOLDED // 2, shards * 8, HD), jnp.float32),
+            pltpu.VMEM((FOLDED // 2, shards * 8 + 8, HD), jnp.float32),
             pltpu.SemaphoreType.DMA((3,)),
             pltpu.SemaphoreType.DMA((2, 2)),
         ],
@@ -361,8 +359,8 @@
         [shape((256, width))] * 3 + [shape((shards * 8, 4 * width))],
         in_specs=[scalars] + [whole] * 7,
         scratch_shapes=[
-            pltpu.VMEM((FOLDED // 2, shards * 8, HD), jnp.float32),
-            pltpu.VMEM((4, shards * 8, HD), jnp.float32),
+            pltpu.VMEM((FOLDED // 2, shards * 8 + 8, HD), jnp.float32),
+            pltpu.VMEM((4, shards * 8 + 8, HD), jnp.float32),
         ],
     )(where, queries, keys, values, out_grad, remote, left, right)
     returned = swap(shares, shards, "seq")
@@ -405,14 +403,18 @@
     )
     parts = lax.all_to_all(terms, "x", split_axis=0, concat_axis=0, tiled=True)
     spread = call(
-        spread_kernel, "spread", shape((shards * 16, 128)), in_specs=[whole, outside]
+        spread_kernel,
+        "spread",
+        shape((shards * 16, HD)),
+        in_specs=[whole, outside],
+        scratch_shapes=[pltpu.VMEM((shards * 16 + 16, HD), jnp.float32)],
     )(parts, other)
     rows = swap(spread, 2 * shards, ("seq", "h"))
     return call(
         finish_kernel,
         "finish",
         shape((256, width)),
-        scratch_shapes=[pltpu.VMEM((shards * 16, HD), jnp.float32)],
+        scratch_shapes=[pltpu.VMEM((shards * 16 + 16, HD), jnp.float32)],
     )(rows, mine, other)
 
 

time: 152 us -> 151 us (level)
  no operation moved by 1% of the time
where the time goes in v7:
time: 151 us; the launch traced here: 150 us
  waiting for transfers between devices  53 us (35%)
  starting transfers between devices  51 us (34%)
  blocking collectives  25.3 us (17%)
  Pallas kernels  14.7 us (10%)
  local copies, waits for them, and re-layouts  5.28 us (3%)
    all_to_all x3, waiting for transfers between devices, swap(): lax.all_to_all(cut, axis, split_axis=0, concat_axis=0, tiled=True)  28 us
    all_to_all x3, starting transfers between devices, swap(): lax.all_to_all(cut, axis, split_axis=0, concat_axis=0, tiled=True)  26.1 us
    all_to_all x1, blocking collectives, swap(): lax.all_to_all(cut, axis, split_axis=0, concat_axis=0, tiled=True)  25.3 us
    ppermute x3, starting transfers between devices, body(): lax.ppermute(own[shift], 'x', [(i, (i + shift) % X_SIZE) for i in range(X...  10.5 us
    ppermute x1, waiting for transfers between devices, body(): lax.ppermute(last_block, 'seq', [(i, (i + 1) % shards) for i in range(sha...  10.4 us
    ppermute x3, waiting for transfers between devices, body(): lax.ppermute(own[shift], 'x', [(i, (i + shift) % X_SIZE) for i in range(X...  7.02 us
    ppermute x1, waiting for transfers between devices, body(): other = lax.ppermute(theirs, 'h', [(0, 1), (1, 0)])  6.64 us
    ppermute x1, starting transfers between devices, body(): other = lax.ppermute(theirs, 'h', [(0, 1), (1, 0)])  4.76 us
  transfers between devices with their start and end apart: 10, of which 8 were waited for; matrix products, arithmetic and copies ran while one was open for 2% of the time, Pallas kernels for 2%

profile of v7, /device:TPU:1, one launch (start us, length us, event | category | flops | bytes accessed | tf_op | source)
XLA Modules:
  0.0 150.3 jit_solution(13907382854776161206)
XLA Ops:
  0.0 2.0 %pack.1 = bf16[512,256]{1,0:T(8,128)(2,1)} custom-call(bf16[256,256]{1,0:T(8,128)(2,1)} %k_ref.1, bf16[256,256]{1,0:T(8,128)(2,1)} %v_ref.1), custom_call_target="tpu_custom_call" | custom-call | tf_op jit(solution)/shard_map/pack/pallas_call | solution.py:326
  2.0 0.0 copy-start.13
  2.0 15.4 %all-to-all-start = ((bf16[64,8,256]{2,1,0:T(8,128)(2,1)}), bf16[64,8,256]{2,1,0:T(8,128)(2,1)S(1)}, u32[]{:S(2)}, u32[]{:S(2)}) async-start(bf16[64,8,256]{2,1,0:T(8,128)(2,1)} %bitcast.24), calls=%async_computation | async-start | bytes 524288 | tf_op jit(solution)/shard_map/all_to_all | solution.py:306
  17.4 0.1 concatenate.46
  17.5 0.0 copy-done.13
  17.5 0.1 copy.24
  17.7 0.1 reshape.387
  17.8 0.0 copy-start.10
  17.8 0.1 concatenate.44
  17.9 0.7 slice_bitcast_fusion
  18.6 0.0 copy-done.10
  18.6 0.1 copy.25
  18.6 0.1 concatenate.45
  18.7 0.2 copy.26
  18.9 0.0 copy-start.2
  19.0 0.0 copy-start.3
  19.0 0.4 fusion.1.index_ref
  19.4 11.6 %all-to-all-done = bf16[64,8,256]{2,1,0:T(8,128)(2,1)S(1)} async-done(((bf16[64,8,256]{2,1,0:T(8,128)(2,1)}), bf16[64,8,256]{2,1,0:T(8,128)(2,1)S(1)}, u32[]{:S(2)}, u32[]{:S(2)}) %all-to-all-start) | async-done | bytes 262176 | tf_op jit(solution)/shard_map/all_to_all | solution.py:306
  30.9 0.0 copy-done.2
  31.0 0.0 copy-done.3
  31.0 1.6 %pick.1 = (bf16[512,896]{1,0:T(8,128)(2,1)}, bf16[2,64,256]{2,1,0:T(8,128)(2,1)S(1)}, bf16[2,64,256]{2,1,0:T(8,128)(2,1)S(1)}) custom-call(s32[896,1]{1,0:T(8,128)S(1)} %fusion.1.index_ref, bf16[512,256]{1,0:T(8,128)(2,1)S(1)} %bitcast.22, bf16[256,256]{1,0:T(8,128)(2,1)S(1)} %copy-done.2, bf16[256,256]{1,0:T(8,128)(2,1)S(1)} %copy-done.3), custom_call_target="tpu_custom_call" | custom-call | tf_op jit(solution)/shard_map/pick/pallas_call | solution.py:339
  32.5 0.0 copy-start.8
  32.5 0.0 copy-start.9
  32.6 4.7 %all-to-all-start.1 = ((bf16[64,8,896]{2,1,0:T(8,128)(2,1)}), bf16[64,8,896]{2,1,0:T(8,128)(2,1)S(1)}, u32[]{:S(2)}, u32[]{:S(2)}) async-start(bf16[64,8,896]{2,1,0:T(8,128)(2,1)} %bitcast.6), calls=%async_computation.1 | async-start | bytes 1835008 | tf_op jit(solution)/shard_map/all_to_all | solution.py:306
  37.3 3.5 %collective-permute-start = (bf16[2,64,256]{2,1,0:T(8,128)(2,1)S(1)}, bf16[2,64,256]{2,1,0:T(8,128)(2,1)S(1)}, u32[]{:S(2)}, u32[]{:S(2)}) collective-permute-start(bf16[2,64,256]{2,1,0:T(8,128)(2,1)S(1)} %get-tuple-element.19), channel_id=1, source_target_pairs={{0,8},{8,16},{16,24},{24,32},{32,40},{40,48},{48,56},{56,64},{64,7... | collective-permute-start | bytes 196616 | tf_op jit(solution)/shard_map/ppermute | solution.py:353
  40.9 1.9 %collective-permute-start.1 = (bf16[2,64,256]{2,1,0:T(8,128)(2,1)S(1)}, bf16[2,64,256]{2,1,0:T(8,128)(2,1)S(1)}, u32[]{:S(2)}, u32[]{:S(2)}) collective-permute-start(bf16[2,64,256]{2,1,0:T(8,128)(2,1)S(1)} %get-tuple-element.20), channel_id=1, source_target_pairs={{0,504},{8,0},{16,8},{24,16},{32,24},{40,32},{48,40},{56,48},{64,5... | collective-permute-start | bytes 196616 | tf_op jit(solution)/shard_map/ppermute | solution.py:354
  42.8 0.1 pad_add_fusion.3.where_ref
  42.9 10.4 %collective-permute-done.left_ref = bf16[2,64,256]{2,1,0:T(8,128)(2,1)S(1)} collective-permute-done((bf16[2,64,256]{2,1,0:T(8,128)(2,1)S(1)}, bf16[2,64,256]{2,1,0:T(8,128)(2,1)S(1)}, u32[]{:S(2)}, u32[]{:S(2)}) %collective-permute-start) | collective-permute-done | bytes 65568 | tf_op jit(solution)/shard_map/ppermute | solution.py:353
  53.2 0.0 collective-permute-done.1.right_ref
  53.2 10.9 %all-to-all-done.1 = bf16[64,8,896]{2,1,0:T(8,128)(2,1)S(1)} async-done(((bf16[64,8,896]{2,1,0:T(8,128)(2,1)}), bf16[64,8,896]{2,1,0:T(8,128)(2,1)S(1)}, u32[]{:S(2)}, u32[]{:S(2)}) %all-to-all-start.1) | async-done | bytes 917536 | tf_op jit(solution)/shard_map/all_to_all | solution.py:306
  64.1 0.0 copy-done.8
  64.1 0.0 copy-done.9
  64.1 3.7 %attention.1 = (bf16[256,256]{1,0:T(8,128)(2,1)S(1)}, bf16[256,256]{1,0:T(8,128)(2,1)S(1)}, bf16[256,256]{1,0:T(8,128)(2,1)S(1)}, bf16[512,1024]{1,0:T(8,128)(2,1)S(1)}) custom-call(s32[3]{0:T(128)S(1)} %pad_add_fusion.3.where_ref, bf16[256,256]{1,0:T(8,128)(2,1)S(1)} %copy-done.8, bf16[256,256]{1,0:T(8,128)(2,1)S(1)} %copy-done.2, ...), custom_call_target="tpu_custom_call" | custom-call | tf_op jit(solution)/shard_map/attention/pallas_call | solution.py:356
  67.8 0.0 copy-start.4
  67.8 1.0 copy-done.4
  68.8 5.9 %all-to-all-start.2 = ((bf16[64,8,1024]{2,1,0:T(8,128)(2,1)}), bf16[64,8,1024]{2,1,0:T(8,128)(2,1)S(1)}, u32[]{:S(2)}, u32[]{:S(2)}) async-start(bf16[64,8,1024]{2,1,0:T(8,128)(2,1)} %bitcast.21), calls=%async_computation.2 | async-start | bytes 2097152 | tf_op jit(solution)/shard_map/all_to_all | solution.py:306
  74.7 0.0 copy-done
  74.7 0.0 copy-done.1
  74.7 0.0 copy-start.5
  74.8 1.2 copy-done.5
  76.0 2.3 %own.1 = (bf16[256,512]{1,0:T(8,128)(2,1)S(1)}, bf16[256,512]{1,0:T(8,128)(2,1)}, bf16[256,512]{1,0:T(8,128)(2,1)}, bf16[256,512]{1,0:T(8,128)(2,1)}) custom-call(s32[3]{0:T(128)S(1)} %pad_add_fusion.3.where_ref, bf16[256,256]{1,0:T(8,128)(2,1)S(1)} %get-tuple-element.22.dq_ref, bf16[256,256]{1,0:T(8,128)(2,1)S(1)} %get-tuple-element.23.dk_ref, ...), custom_call_target="tpu_custom_call" | custom-call | tf_op jit(solution)/shard_map/own/pallas_call | solution.py:368
  78.3 0.7 copy-done.6
  79.0 3.1 %collective-permute-start.2 = (bf16[256,512]{1,0:T(8,128)(2,1)}, bf16[256,512]{1,0:T(8,128)(2,1)S(1)}, u32[]{:S(2)}, u32[]{:S(2)}) collective-permute-start(bf16[256,512]{1,0:T(8,128)(2,1)} %get-tuple-element.25), channel_id=1, source_target_pairs={{0,1},{1,2},{2,3},{3,0},{4,5},{5,6},{6,7},{7,4},{8,9},{9,10},{10,1... | collective-permute-start | bytes 786440 | tf_op jit(solution)/shard_map/ppermute | solution.py:375
  82.1 4.4 %collective-permute-start.3 = (bf16[256,512]{1,0:T(8,128)(2,1)}, bf16[256,512]{1,0:T(8,128)(2,1)}, u32[]{:S(2)}, u32[]{:S(2)}) collective-permute-start(bf16[256,512]{1,0:T(8,128)(2,1)} %get-tuple-element.26), channel_id=1, source_target_pairs={{0,2},{1,3},{2,0},{3,1},{4,6},{5,7},{6,4},{7,5},{8,10},{9,11},{10,... | collective-permute-start | bytes 786440 | tf_op jit(solution)/shard_map/ppermute | solution.py:375
  86.5 0.0 copy-start.11
  86.5 3.1 %collective-permute-start.4 = (bf16[256,512]{1,0:T(8,128)(2,1)}, bf16[256,512]{1,0:T(8,128)(2,1)}, u32[]{:S(2)}, u32[]{:S(2)}) collective-permute-start(bf16[256,512]{1,0:T(8,128)(2,1)} %get-tuple-element.27), channel_id=1, source_target_pairs={{0,3},{1,0},{2,1},{3,2},{4,7},{5,4},{6,5},{7,6},{8,11},{9,8},{10,9... | collective-permute-start | bytes 786440 | tf_op jit(solution)/shard_map/ppermute | solution.py:375
  89.6 0.0 copy-start.12
  89.6 0.1 stack_reshape.6
  89.7 0.6 copy-done.12
  90.4 0.1 pad_add_fusion
  90.5 0.1 stack_reshape.7
  90.6 0.0 collective-permute-done.2._.refs_1_
  90.6 5.8 %collective-permute-done.3.__.refs_2_ = bf16[256,512]{1,0:T(8,128)(2,1)} collective-permute-done((bf16[256,512]{1,0:T(8,128)(2,1)}, bf16[256,512]{1,0:T(8,128)(2,1)}, u32[]{:S(2)}, u32[]{:S(2)}) %collective-permute-start.3) | collective-permute-done | bytes 262176 | tf_op jit(solution)/shard_map/ppermute | solution.py:375
  96.4 1.2 collective-permute-done.4.___.refs_3_
  97.6 5.6 %all-to-all-done.2 = bf16[64,8,1024]{2,1,0:T(8,128)(2,1)S(1)} async-done(((bf16[64,8,1024]{2,1,0:T(8,128)(2,1)}), bf16[64,8,1024]{2,1,0:T(8,128)(2,1)S(1)}, u32[]{:S(2)}, u32[]{:S(2)}) %all-to-all-start.2) | async-done | bytes 1048608 | tf_op jit(solution)/shard_map/all_to_all | solution.py:306
  103.2 2.8 %project.1 = bf16[4,256,512]{2,1,0:T(8,128)(2,1)} custom-call(s32[2,512]{1,0:T(2,128)S(1)} %fusion.9.index_ref, bf16[512,1024]{1,0:T(8,128)(2,1)S(1)} %bitcast.16, bf16[2,4,256,256]{3,2,1,0:T(8,128)(2,1)S(1)} %bitcast.17, bf16[2,4,256,256]{3,2,1,0:T(8,128)(2,1)S(1)} %bitcast.18, bf16[256,512]{1,0:T(8,128)(2,1)S(1)} %collective-permute-done.2._.refs_1_, ...), custom_call_target="tpu_custom_call" | custom-call | tf_op jit(solution)/shard_map/project/pallas_call | solution.py:386
  106.0 4.2 %all-to-all-start.3 = ((bf16[4,256,512]{2,1,0:T(8,128)(2,1)}), bf16[4,256,512]{2,1,0:T(8,128)(2,1)S(1)}, u32[]{:S(2)}, u32[]{:S(2)}) async-start(bf16[4,256,512]{2,1,0:T(8,128)(2,1)} %project.1), calls=%async_computation.3 | async-start | bytes 2097152 | tf_op jit(solution)/shard_map/all_to_all | solution.py:404
  110.2 1.2 own_sum.1
  111.4 4.8 %collective-permute-start.5 = (bf16[256,256]{1,0:T(8,128)(2,1)S(1)}, bf16[256,256]{1,0:T(8,128)(2,1)S(1)}, u32[]{:S(2)}, u32[]{:S(2)}) collective-permute-start(bf16[256,256]{1,0:T(8,128)(2,1)S(1)} %get-tuple-element.29), channel_id=1, source_target_pairs={{0,4},{4,0},{1,5},{5,1},{2,6},{6,2},{3,7},{7,3},{8,12},{12,8},{9,1... | collective-permute-start | bytes 393224 | tf_op jit(solution)/shard_map/ppermute | solution.py:384
  116.1 6.6 %collective-permute-done.5._.other_ref = bf16[256,256]{1,0:T(8,128)(2,1)S(1)} collective-permute-done((bf16[256,256]{1,0:T(8,128)(2,1)S(1)}, bf16[256,256]{1,0:T(8,128)(2,1)S(1)}, u32[]{:S(2)}, u32[]{:S(2)}) %collective-permute-start.5) | collective-permute-done | bytes 131104 | tf_op jit(solution)/shard_map/ppermute | solution.py:384
  122.8 0.9 all-to-all-done.3.parts_ref
  123.7 0.4 spread.1
  124.0 25.3 %all_to_all.25 = bf16[128,8,128]{2,1,0:T(8,128)(2,1)S(1)} all-to-all(bf16[128,8,128]{2,1,0:T(8,128)(2,1)S(1)} %bitcast.23), channel_id=1, replica_groups=mesh['seq'=64,'h'=2,'x'=4] {'seq','h'}, dimensions={0} | all-to-all | bytes 524288 | tf_op jit(solution)/shard_map/all_to_all | solution.py:306
  149.4 0.9 finish.1
  (11 shorter events, 0.1 us)
Async XLA Ops:
  2.0 15.5 %copy-start.13 = (s32[256,3]{0,1:T(4,128)S(1)}, s32[256,3]{0,1:T(4,128)}, u32[]{:S(2)}) copy-start(s32[256,3]{0,1:T(4,128)} %param.12) | copy-start | bytes 9220
  2.0 29.0 %all-to-all-start = ((bf16[64,8,256]{2,1,0:T(8,128)(2,1)}), bf16[64,8,256]{2,1,0:T(8,128)(2,1)S(1)}, u32[]{:S(2)}, u32[]{:S(2)}) async-start(bf16[64,8,256]{2,1,0:T(8,128)(2,1)} %bitcast.24), calls=%async_computation | async-start | bytes 524288 | tf_op jit(solution)/shard_map/all_to_all | solution.py:306
  17.8 0.8 copy-start.10
  18.9 12.0 %copy-start.2 = (bf16[256,256]{1,0:T(8,128)(2,1)S(1)}, bf16[256,256]{1,0:T(8,128)(2,1)}, u32[]{:S(2)}) copy-start(bf16[256,256]{1,0:T(8,128)(2,1)} %k_ref.1) | copy-start | bytes 393220
  19.0 12.0 %copy-start.3 = (bf16[256,256]{1,0:T(8,128)(2,1)S(1)}, bf16[256,256]{1,0:T(8,128)(2,1)}, u32[]{:S(2)}) copy-start(bf16[256,256]{1,0:T(8,128)(2,1)} %v_ref.1) | copy-start | bytes 393220
  32.5 31.6 %copy-start.8 = (bf16[256,256]{1,0:T(8,128)(2,1)S(1)}, bf16[256,256]{1,0:T(8,128)(2,1)}, u32[]{:S(2)}) copy-start(bf16[256,256]{1,0:T(8,128)(2,1)} %q_ref.1) | copy-start | bytes 393220
  32.5 31.6 %copy-start.9 = (bf16[256,256]{1,0:T(8,128)(2,1)S(1)}, bf16[256,256]{1,0:T(8,128)(2,1)}, u32[]{:S(2)}) copy-start(bf16[256,256]{1,0:T(8,128)(2,1)} %g_ref.1) | copy-start | bytes 393220
  32.6 31.5 %all-to-all-start.1 = ((bf16[64,8,896]{2,1,0:T(8,128)(2,1)}), bf16[64,8,896]{2,1,0:T(8,128)(2,1)S(1)}, u32[]{:S(2)}, u32[]{:S(2)}) async-start(bf16[64,8,896]{2,1,0:T(8,128)(2,1)} %bitcast.6), calls=%async_computation.1 | async-start | bytes 1835008 | tf_op jit(solution)/shard_map/all_to_all | solution.py:306
  37.3 15.9 %collective-permute-start = (bf16[2,64,256]{2,1,0:T(8,128)(2,1)S(1)}, bf16[2,64,256]{2,1,0:T(8,128)(2,1)S(1)}, u32[]{:S(2)}, u32[]{:S(2)}) collective-permute-start(bf16[2,64,256]{2,1,0:T(8,128)(2,1)S(1)} %get-tuple-element.19), channel_id=1, source_target_pairs={{0,8},{8,16},{16,24},{24,32},{32,40},{40,48},{48,56},{56,64},{64,7... | collective-permute-start | bytes 196616 | tf_op jit(solution)/shard_map/ppermute | solution.py:353
  40.9 12.4 %collective-permute-start.1 = (bf16[2,64,256]{2,1,0:T(8,128)(2,1)S(1)}, bf16[2,64,256]{2,1,0:T(8,128)(2,1)S(1)}, u32[]{:S(2)}, u32[]{:S(2)}) collective-permute-start(bf16[2,64,256]{2,1,0:T(8,128)(2,1)S(1)} %get-tuple-element.20), channel_id=1, source_target_pairs={{0,504},{8,0},{16,8},{24,16},{32,24},{40,32},{48,40},{56,48},{64,5... | collective-permute-start | bytes 196616 | tf_op jit(solution)/shard_map/ppermute | solution.py:354
  67.8 1.0 copy-start.4
  68.8 5.9 %copy-start = (bf16[2048,256]{1,0:T(8,128)(2,1)S(1)}, bf16[2048,256]{1,0:T(8,128)(2,1)}, u32[]{:S(2)}) copy-start(bf16[2048,256]{1,0:T(8,128)(2,1)} %wk_ref.1) | copy-start | bytes 3145732
  68.8 6.0 %copy-start.1 = (bf16[2048,256]{1,0:T(8,128)(2,1)S(1)}, bf16[2048,256]{1,0:T(8,128)(2,1)}, u32[]{:S(2)}) copy-start(bf16[2048,256]{1,0:T(8,128)(2,1)} %wv_ref.1) | copy-start | bytes 3145732
  68.8 34.4 %all-to-all-start.2 = ((bf16[64,8,1024]{2,1,0:T(8,128)(2,1)}), bf16[64,8,1024]{2,1,0:T(8,128)(2,1)S(1)}, u32[]{:S(2)}, u32[]{:S(2)}) async-start(bf16[64,8,1024]{2,1,0:T(8,128)(2,1)} %bitcast.21), calls=%async_computation.2 | async-start | bytes 2097152 | tf_op jit(solution)/shard_map/all_to_all | solution.py:306
  74.7 1.2 copy-start.5
  78.3 0.7 copy-start.6
  79.0 11.6 %collective-permute-start.2 = (bf16[256,512]{1,0:T(8,128)(2,1)}, bf16[256,512]{1,0:T(8,128)(2,1)S(1)}, u32[]{:S(2)}, u32[]{:S(2)}) collective-permute-start(bf16[256,512]{1,0:T(8,128)(2,1)} %get-tuple-element.25), channel_id=1, source_target_pairs={{0,1},{1,2},{2,3},{3,0},{4,5},{5,6},{6,7},{7,4},{8,9},{9,10},{10,1... | collective-permute-start | bytes 786440 | tf_op jit(solution)/shard_map/ppermute | solution.py:375
  82.1 14.3 %collective-permute-start.3 = (bf16[256,512]{1,0:T(8,128)(2,1)}, bf16[256,512]{1,0:T(8,128)(2,1)}, u32[]{:S(2)}, u32[]{:S(2)}) collective-permute-start(bf16[256,512]{1,0:T(8,128)(2,1)} %get-tuple-element.26), channel_id=1, source_target_pairs={{0,2},{1,3},{2,0},{3,1},{4,6},{5,7},{6,4},{7,5},{8,10},{9,11},{10,... | collective-permute-start | bytes 786440 | tf_op jit(solution)/shard_map/ppermute | solution.py:375
  86.5 3.1 %copy-start.11 = (s32[64,12]{1,0:T(8,128)S(1)}, s32[64,12]{1,0:T(8,128)}, u32[]{:S(2)}) copy-start(s32[64,12]{1,0:T(8,128)} %copy-done.10) | copy-start | bytes 9220
  86.5 11.1 %collective-permute-start.4 = (bf16[256,512]{1,0:T(8,128)(2,1)}, bf16[256,512]{1,0:T(8,128)(2,1)}, u32[]{:S(2)}, u32[]{:S(2)}) collective-permute-start(bf16[256,512]{1,0:T(8,128)(2,1)} %get-tuple-element.27), channel_id=1, source_target_pairs={{0,3},{1,0},{2,1},{3,2},{4,7},{5,4},{6,5},{7,6},{8,11},{9,8},{10,9... | collective-permute-start | bytes 786440 | tf_op jit(solution)/shard_map/ppermute | solution.py:375
  89.6 0.8 copy-start.12
  106.0 4.2 %copy-start.7 = (bf16[256,512]{1,0:T(8,128)(2,1)S(1)}, bf16[256,512]{1,0:T(8,128)(2,1)}, u32[]{:S(2)}) copy-start(bf16[256,512]{1,0:T(8,128)(2,1)} %copy-done.6) | copy-start | bytes 786436
  106.0 17.6 %all-to-all-start.3 = ((bf16[4,256,512]{2,1,0:T(8,128)(2,1)}), bf16[4,256,512]{2,1,0:T(8,128)(2,1)S(1)}, u32[]{:S(2)}, u32[]{:S(2)}) async-start(bf16[4,256,512]{2,1,0:T(8,128)(2,1)} %project.1), calls=%async_computation.3 | async-start | bytes 2097152 | tf_op jit(solution)/shard_map/all_to_all | solution.py:404
  111.4 11.4 %collective-permute-start.5 = (bf16[256,256]{1,0:T(8,128)(2,1)S(1)}, bf16[256,256]{1,0:T(8,128)(2,1)S(1)}, u32[]{:S(2)}, u32[]{:S(2)}) collective-permute-start(bf16[256,256]{1,0:T(8,128)(2,1)S(1)} %get-tuple-element.29), channel_id=1, source_target_pairs={{0,4},{4,0},{1,5},{5,1},{2,6},{6,2},{3,7},{7,3},{8,12},{12,8},{9,1... | collective-permute-start | bytes 393224 | tf_op jit(solution)/shard_map/ppermute | solution.py:384

commit v8 on v7

--- a/solution.py
+++ b/solution.py
@@ -271,7 +271,7 @@
             total = functools.reduce(
                 jnp.add, [parts_ref[g, rows, lanes].astype(jnp.float32) for g in range(X_SIZE)]
             )
-            wide_ref[pl.ds(quarter * PER + b, 64, stride=16), :] = total
+            wide_ref[pl.ds((quarter >> 1) * 512 + (quarter & 1) * PER + b, 64, stride=8), :] = total
     out_ref[...] = wide_ref[0:1024].astype(jnp.bfloat16)
 
 
@@ -281,7 +281,7 @@
         lanes = slice(half * HD, (half + 1) * HD)
         far = []
         for b in range(PER):
-            senders = [wide_ref[pl.ds(h * 8 + half * PER + b, 64, stride=16), :] for h in range(2)]
+            senders = [wide_ref[pl.ds(h * 512 + half * PER + b, 64, stride=8), :] for h in range(2)]
             far.append(senders[0] + senders[1])
         near = mine_ref[:, lanes] + other_ref[:, lanes].astype(jnp.float32)
         out_ref[:, lanes] = (jnp.concatenate(far, axis=0) + near).astype(jnp.bfloat16)
@@ -409,7 +409,7 @@
         in_specs=[whole, outside],
         scratch_shapes=[pltpu.VMEM((shards * 16 + 16, HD), jnp.float32)],
     )(parts, other)
-    rows = swap(spread, 2 * shards, ("seq", "h"))
+    rows = swap(spread, 2 * shards, ("h", "seq"))
     return call(
         finish_kernel,
         "finish",

time: 151 us -> 150 us (level)
  no operation moved by 1% of the time
where the time goes in v8:
time: 150 us; the launch traced here: 149 us
  waiting for transfers between devices  53 us (35%)
  starting transfers between devices  51 us (34%)
  blocking collectives  24.1 us (16%)
  Pallas kernels  14.5 us (10%)
  local copies, waits for them, and re-layouts  5.28 us (4%)
    all_to_all x3, waiting for transfers between devices, swap(): lax.all_to_all(cut, axis, split_axis=0, concat_axis=0, tiled=True)  28 us
    all_to_all x3, starting transfers between devices, swap(): lax.all_to_all(cut, axis, split_axis=0, concat_axis=0, tiled=True)  26.1 us
    all_to_all x1, blocking collectives, swap(): lax.all_to_all(cut, axis, split_axis=0, concat_axis=0, tiled=True)  24.1 us
    ppermute x3, starting transfers between devices, body(): lax.ppermute(own[shift], 'x', [(i, (i + shift) % X_SIZE) for i in range(X...  10.5 us
    ppermute x1, waiting for transfers between devices, body(): lax.ppermute(last_block, 'seq', [(i, (i + 1) % shards) for i in range(sha...  10.4 us
    ppermute x3, waiting for transfers between devices, body(): lax.ppermute(own[shift], 'x', [(i, (i + shift) % X_SIZE) for i in range(X...  7.02 us
    ppermute x1, waiting for transfers between devices, body(): other = lax.ppermute(theirs, 'h', [(0, 1), (1, 0)])  6.64 us
    ppermute x1, starting transfers between devices, body(): other = lax.ppermute(theirs, 'h', [(0, 1), (1, 0)])  4.76 us
  transfers between devices with their start and end apart: 10, of which 8 were waited for; matrix products, arithmetic and copies ran while one was open for 2% of the time, Pallas kernels for 2%

profile of v8, /device:TPU:1, one launch (start us, length us, event | category | flops | bytes accessed | tf_op | source)
XLA Modules:
  0.0 148.8 jit_solution(15981205223999641735)
XLA Ops:
  0.0 2.0 %pack.1 = bf16[512,256]{1,0:T(8,128)(2,1)} custom-call(bf16[256,256]{1,0:T(8,128)(2,1)} %k_ref.1, bf16[256,256]{1,0:T(8,128)(2,1)} %v_ref.1), custom_call_target="tpu_custom_call" | custom-call | tf_op jit(solution)/shard_map/pack/pallas_call | solution.py:326
  2.0 0.0 copy-start.13
  2.0 15.4 %all-to-all-start = ((bf16[64,8,256]{2,1,0:T(8,128)(2,1)}), bf16[64,8,256]{2,1,0:T(8,128)(2,1)S(1)}, u32[]{:S(2)}, u32[]{:S(2)}) async-start(bf16[64,8,256]{2,1,0:T(8,128)(2,1)} %bitcast.24), calls=%async_computation | async-start | bytes 524288 | tf_op jit(solution)/shard_map/all_to_all | solution.py:306
  17.4 0.1 concatenate.46
  17.5 0.0 copy-done.13
  17.5 0.1 copy.24
  17.7 0.1 reshape.387
  17.8 0.0 copy-start.10
  17.8 0.1 concatenate.44
  17.9 0.7 slice_bitcast_fusion
  18.6 0.0 copy-done.10
  18.6 0.1 copy.25
  18.6 0.1 concatenate.45
  18.7 0.2 copy.26
  18.9 0.0 copy-start.2
  19.0 0.0 copy-start.3
  19.0 0.4 fusion.1.index_ref
  19.4 11.6 %all-to-all-done = bf16[64,8,256]{2,1,0:T(8,128)(2,1)S(1)} async-done(((bf16[64,8,256]{2,1,0:T(8,128)(2,1)}), bf16[64,8,256]{2,1,0:T(8,128)(2,1)S(1)}, u32[]{:S(2)}, u32[]{:S(2)}) %all-to-all-start) | async-done | bytes 262176 | tf_op jit(solution)/shard_map/all_to_all | solution.py:306
  30.9 0.0 copy-done.2
  31.0 0.0 copy-done.3
  31.0 1.6 %pick.1 = (bf16[512,896]{1,0:T(8,128)(2,1)}, bf16[2,64,256]{2,1,0:T(8,128)(2,1)S(1)}, bf16[2,64,256]{2,1,0:T(8,128)(2,1)S(1)}) custom-call(s32[896,1]{1,0:T(8,128)S(1)} %fusion.1.index_ref, bf16[512,256]{1,0:T(8,128)(2,1)S(1)} %bitcast.22, bf16[256,256]{1,0:T(8,128)(2,1)S(1)} %copy-done.2, bf16[256,256]{1,0:T(8,128)(2,1)S(1)} %copy-done.3), custom_call_target="tpu_custom_call" | custom-call | tf_op jit(solution)/shard_map/pick/pallas_call | solution.py:339
  32.5 0.0 copy-start.8
  32.5 0.0 copy-start.9
  32.6 4.7 %all-to-all-start.1 = ((bf16[64,8,896]{2,1,0:T(8,128)(2,1)}), bf16[64,8,896]{2,1,0:T(8,128)(2,1)S(1)}, u32[]{:S(2)}, u32[]{:S(2)}) async-start(bf16[64,8,896]{2,1,0:T(8,128)(2,1)} %bitcast.6), calls=%async_computation.1 | async-start | bytes 1835008 | tf_op jit(solution)/shard_map/all_to_all | solution.py:306
  37.3 3.5 %collective-permute-start = (bf16[2,64,256]{2,1,0:T(8,128)(2,1)S(1)}, bf16[2,64,256]{2,1,0:T(8,128)(2,1)S(1)}, u32[]{:S(2)}, u32[]{:S(2)}) collective-permute-start(bf16[2,64,256]{2,1,0:T(8,128)(2,1)S(1)} %get-tuple-element.19), channel_id=1, source_target_pairs={{0,8},{8,16},{16,24},{24,32},{32,40},{40,48},{48,56},{56,64},{64,7... | collective-permute-start | bytes 196616 | tf_op jit(solution)/shard_map/ppermute | solution.py:353
  40.9 1.9 %collective-permute-start.1 = (bf16[2,64,256]{2,1,0:T(8,128)(2,1)S(1)}, bf16[2,64,256]{2,1,0:T(8,128)(2,1)S(1)}, u32[]{:S(2)}, u32[]{:S(2)}) collective-permute-start(bf16[2,64,256]{2,1,0:T(8,128)(2,1)S(1)} %get-tuple-element.20), channel_id=1, source_target_pairs={{0,504},{8,0},{16,8},{24,16},{32,24},{40,32},{48,40},{56,48},{64,5... | collective-permute-start | bytes 196616 | tf_op jit(solution)/shard_map/ppermute | solution.py:354
  42.8 0.1 pad_add_fusion.3.where_ref
  42.9 10.4 %collective-permute-done.left_ref = bf16[2,64,256]{2,1,0:T(8,128)(2,1)S(1)} collective-permute-done((bf16[2,64,256]{2,1,0:T(8,128)(2,1)S(1)}, bf16[2,64,256]{2,1,0:T(8,128)(2,1)S(1)}, u32[]{:S(2)}, u32[]{:S(2)}) %collective-permute-start) | collective-permute-done | bytes 65568 | tf_op jit(solution)/shard_map/ppermute | solution.py:353
  53.2 0.0 collective-permute-done.1.right_ref
  53.2 10.9 %all-to-all-done.1 = bf16[64,8,896]{2,1,0:T(8,128)(2,1)S(1)} async-done(((bf16[64,8,896]{2,1,0:T(8,128)(2,1)}), bf16[64,8,896]{2,1,0:T(8,128)(2,1)S(1)}, u32[]{:S(2)}, u32[]{:S(2)}) %all-to-all-start.1) | async-done | bytes 917536 | tf_op jit(solution)/shard_map/all_to_all | solution.py:306
  64.1 0.0 copy-done.8
  64.1 0.0 copy-done.9
  64.1 3.7 %attention.1 = (bf16[256,256]{1,0:T(8,128)(2,1)S(1)}, bf16[256,256]{1,0:T(8,128)(2,1)S(1)}, bf16[256,256]{1,0:T(8,128)(2,1)S(1)}, bf16[512,1024]{1,0:T(8,128)(2,1)S(1)}) custom-call(s32[3]{0:T(128)S(1)} %pad_add_fusion.3.where_ref, bf16[256,256]{1,0:T(8,128)(2,1)S(1)} %copy-done.8, bf16[256,256]{1,0:T(8,128)(2,1)S(1)} %copy-done.2, ...), custom_call_target="tpu_custom_call" | custom-call | tf_op jit(solution)/shard_map/attention/pallas_call | solution.py:356
  67.8 0.0 copy-start.4
  67.8 1.0 copy-done.4
  68.8 5.9 %all-to-all-start.2 = ((bf16[64,8,1024]{2,1,0:T(8,128)(2,1)}), bf16[64,8,1024]{2,1,0:T(8,128)(2,1)S(1)}, u32[]{:S(2)}, u32[]{:S(2)}) async-start(bf16[64,8,1024]{2,1,0:T(8,128)(2,1)} %bitcast.21), calls=%async_computation.2 | async-start | bytes 2097152 | tf_op jit(solution)/shard_map/all_to_all | solution.py:306
  74.7 0.0 copy-done
  74.7 0.0 copy-done.1
  74.7 0.0 copy-start.5
  74.8 1.2 copy-done.5
  76.0 2.3 %own.1 = (bf16[256,512]{1,0:T(8,128)(2,1)S(1)}, bf16[256,512]{1,0:T(8,128)(2,1)}, bf16[256,512]{1,0:T(8,128)(2,1)}, bf16[256,512]{1,0:T(8,128)(2,1)}) custom-call(s32[3]{0:T(128)S(1)} %pad_add_fusion.3.where_ref, bf16[256,256]{1,0:T(8,128)(2,1)S(1)} %get-tuple-element.22.dq_ref, bf16[256,256]{1,0:T(8,128)(2,1)S(1)} %get-tuple-element.23.dk_ref, ...), custom_call_target="tpu_custom_call" | custom-call | tf_op jit(solution)/shard_map/own/pallas_call | solution.py:368
  78.3 0.7 copy-done.6
  79.0 3.1 %collective-permute-start.2 = (bf16[256,512]{1,0:T(8,128)(2,1)}, bf16[256,512]{1,0:T(8,128)(2,1)S(1)}, u32[]{:S(2)}, u32[]{:S(2)}) collective-permute-start(bf16[256,512]{1,0:T(8,128)(2,1)} %get-tuple-element.25), channel_id=1, source_target_pairs={{0,1},{1,2},{2,3},{3,0},{4,5},{5,6},{6,7},{7,4},{8,9},{9,10},{10,1... | collective-permute-start | bytes 786440 | tf_op jit(solution)/shard_map/ppermute | solution.py:375
  82.1 4.4 %collective-permute-start.3 = (bf16[256,512]{1,0:T(8,128)(2,1)}, bf16[256,512]{1,0:T(8,128)(2,1)}, u32[]{:S(2)}, u32[]{:S(2)}) collective-permute-start(bf16[256,512]{1,0:T(8,128)(2,1)} %get-tuple-element.26), channel_id=1, source_target_pairs={{0,2},{1,3},{2,0},{3,1},{4,6},{5,7},{6,4},{7,5},{8,10},{9,11},{10,... | collective-permute-start | bytes 786440 | tf_op jit(solution)/shard_map/ppermute | solution.py:375
  86.5 0.0 copy-start.11
  86.5 3.1 %collective-permute-start.4 = (bf16[256,512]{1,0:T(8,128)(2,1)}, bf16[256,512]{1,0:T(8,128)(2,1)}, u32[]{:S(2)}, u32[]{:S(2)}) collective-permute-start(bf16[256,512]{1,0:T(8,128)(2,1)} %get-tuple-element.27), channel_id=1, source_target_pairs={{0,3},{1,0},{2,1},{3,2},{4,7},{5,4},{6,5},{7,6},{8,11},{9,8},{10,9... | collective-permute-start | bytes 786440 | tf_op jit(solution)/shard_map/ppermute | solution.py:375
  89.6 0.0 copy-start.12
  89.6 0.1 stack_reshape.6
  89.7 0.6 copy-done.12
  90.4 0.1 pad_add_fusion
  90.5 0.1 stack_reshape.7
  90.6 0.0 collective-permute-done.2._.refs_1_
  90.6 5.8 %collective-permute-done.3.__.refs_2_ = bf16[256,512]{1,0:T(8,128)(2,1)} collective-permute-done((bf16[256,512]{1,0:T(8,128)(2,1)}, bf16[256,512]{1,0:T(8,128)(2,1)}, u32[]{:S(2)}, u32[]{:S(2)}) %collective-permute-start.3) | collective-permute-done | bytes 262176 | tf_op jit(solution)/shard_map/ppermute | solution.py:375
  96.4 1.2 collective-permute-done.4.___.refs_3_
  97.6 5.6 %all-to-all-done.2 = bf16[64,8,1024]{2,1,0:T(8,128)(2,1)S(1)} async-done(((bf16[64,8,1024]{2,1,0:T(8,128)(2,1)}), bf16[64,8,1024]{2,1,0:T(8,128)(2,1)S(1)}, u32[]{:S(2)}, u32[]{:S(2)}) %all-to-all-start.2) | async-done | bytes 1048608 | tf_op jit(solution)/shard_map/all_to_all | solution.py:306
  103.2 2.8 %project.1 = bf16[4,256,512]{2,1,0:T(8,128)(2,1)} custom-call(s32[2,512]{1,0:T(2,128)S(1)} %fusion.9.index_ref, bf16[512,1024]{1,0:T(8,128)(2,1)S(1)} %bitcast.16, bf16[2,4,256,256]{3,2,1,0:T(8,128)(2,1)S(1)} %bitcast.17, bf16[2,4,256,256]{3,2,1,0:T(8,128)(2,1)S(1)} %bitcast.18, bf16[256,512]{1,0:T(8,128)(2,1)S(1)} %collective-permute-done.2._.refs_1_, ...), custom_call_target="tpu_custom_call" | custom-call | tf_op jit(solution)/shard_map/project/pallas_call | solution.py:386
  106.0 4.2 %all-to-all-start.3 = ((bf16[4,256,512]{2,1,0:T(8,128)(2,1)}), bf16[4,256,512]{2,1,0:T(8,128)(2,1)S(1)}, u32[]{:S(2)}, u32[]{:S(2)}) async-start(bf16[4,256,512]{2,1,0:T(8,128)(2,1)} %project.1), calls=%async_computation.3 | async-start | bytes 2097152 | tf_op jit(solution)/shard_map/all_to_all | solution.py:404
  110.2 1.2 own_sum.1
  111.4 4.8 %collective-permute-start.5 = (bf16[256,256]{1,0:T(8,128)(2,1)S(1)}, bf16[256,256]{1,0:T(8,128)(2,1)S(1)}, u32[]{:S(2)}, u32[]{:S(2)}) collective-permute-start(bf16[256,256]{1,0:T(8,128)(2,1)S(1)} %get-tuple-element.29), channel_id=1, source_target_pairs={{0,4},{4,0},{1,5},{5,1},{2,6},{6,2},{3,7},{7,3},{8,12},{12,8},{9,1... | collective-permute-start | bytes 393224 | tf_op jit(solution)/shard_map/ppermute | solution.py:384
  116.1 6.6 %collective-permute-done.5._.other_ref = bf16[256,256]{1,0:T(8,128)(2,1)S(1)} collective-permute-done((bf16[256,256]{1,0:T(8,128)(2,1)S(1)}, bf16[256,256]{1,0:T(8,128)(2,1)S(1)}, u32[]{:S(2)}, u32[]{:S(2)}) %collective-permute-start.5) | collective-permute-done | bytes 131104 | tf_op jit(solution)/shard_map/ppermute | solution.py:384
  122.8 0.9 all-to-all-done.3.parts_ref
  123.7 0.2 spread.1
  123.9 24.1 %all_to_all.25 = bf16[128,8,128]{2,1,0:T(8,128)(2,1)S(1)} all-to-all(bf16[128,8,128]{2,1,0:T(8,128)(2,1)S(1)} %bitcast.23), channel_id=1, replica_groups=mesh['seq'=64,'h'=2,'x'=4] {'h','seq'}, dimensions={0} | all-to-all | bytes 524288 | tf_op jit(solution)/shard_map/all_to_all | solution.py:306
  148.0 0.8 finish.1
  (11 shorter events, 0.1 us)
Async XLA Ops:
  2.0 15.5 %copy-start.13 = (s32[256,3]{0,1:T(4,128)S(1)}, s32[256,3]{0,1:T(4,128)}, u32[]{:S(2)}) copy-start(s32[256,3]{0,1:T(4,128)} %param.12) | copy-start | bytes 9220
  2.0 29.0 %all-to-all-start = ((bf16[64,8,256]{2,1,0:T(8,128)(2,1)}), bf16[64,8,256]{2,1,0:T(8,128)(2,1)S(1)}, u32[]{:S(2)}, u32[]{:S(2)}) async-start(bf16[64,8,256]{2,1,0:T(8,128)(2,1)} %bitcast.24), calls=%async_computation | async-start | bytes 524288 | tf_op jit(solution)/shard_map/all_to_all | solution.py:306
  17.8 0.8 copy-start.10
  18.9 12.0 %copy-start.2 = (bf16[256,256]{1,0:T(8,128)(2,1)S(1)}, bf16[256,256]{1,0:T(8,128)(2,1)}, u32[]{:S(2)}) copy-start(bf16[256,256]{1,0:T(8,128)(2,1)} %k_ref.1) | copy-start | bytes 393220
  19.0 12.0 %copy-start.3 = (bf16[256,256]{1,0:T(8,128)(2,1)S(1)}, bf16[256,256]{1,0:T(8,128)(2,1)}, u32[]{:S(2)}) copy-start(bf16[256,256]{1,0:T(8,128)(2,1)} %v_ref.1) | copy-start | bytes 393220
  32.5 31.6 %copy-start.8 = (bf16[256,256]{1,0:T(8,128)(2,1)S(1)}, bf16[256,256]{1,0:T(8,128)(2,1)}, u32[]{:S(2)}) copy-start(bf16[256,256]{1,0:T(8,128)(2,1)} %q_ref.1) | copy-start | bytes 393220
  32.5 31.6 %copy-start.9 = (bf16[256,256]{1,0:T(8,128)(2,1)S(1)}, bf16[256,256]{1,0:T(8,128)(2,1)}, u32[]{:S(2)}) copy-start(bf16[256,256]{1,0:T(8,128)(2,1)} %g_ref.1) | copy-start | bytes 393220
  32.6 31.5 %all-to-all-start.1 = ((bf16[64,8,896]{2,1,0:T(8,128)(2,1)}), bf16[64,8,896]{2,1,0:T(8,128)(2,1)S(1)}, u32[]{:S(2)}, u32[]{:S(2)}) async-start(bf16[64,8,896]{2,1,0:T(8,128)(2,1)} %bitcast.6), calls=%async_computation.1 | async-start | bytes 1835008 | tf_op jit(solution)/shard_map/all_to_all | solution.py:306
  37.3 15.9 %collective-permute-start = (bf16[2,64,256]{2,1,0:T(8,128)(2,1)S(1)}, bf16[2,64,256]{2,1,0:T(8,128)(2,1)S(1)}, u32[]{:S(2)}, u32[]{:S(2)}) collective-permute-start(bf16[2,64,256]{2,1,0:T(8,128)(2,1)S(1)} %get-tuple-element.19), channel_id=1, source_target_pairs={{0,8},{8,16},{16,24},{24,32},{32,40},{40,48},{48,56},{56,64},{64,7... | collective-permute-start | bytes 196616 | tf_op jit(solution)/shard_map/ppermute | solution.py:353
  40.9 12.4 %collective-permute-start.1 = (bf16[2,64,256]{2,1,0:T(8,128)(2,1)S(1)}, bf16[2,64,256]{2,1,0:T(8,128)(2,1)S(1)}, u32[]{:S(2)}, u32[]{:S(2)}) collective-permute-start(bf16[2,64,256]{2,1,0:T(8,128)(2,1)S(1)} %get-tuple-element.20), channel_id=1, source_target_pairs={{0,504},{8,0},{16,8},{24,16},{32,24},{40,32},{48,40},{56,48},{64,5... | collective-permute-start | bytes 196616 | tf_op jit(solution)/shard_map/ppermute | solution.py:354
  67.8 1.0 copy-start.4
  68.8 5.9 %copy-start = (bf16[2048,256]{1,0:T(8,128)(2,1)S(1)}, bf16[2048,256]{1,0:T(8,128)(2,1)}, u32[]{:S(2)}) copy-start(bf16[2048,256]{1,0:T(8,128)(2,1)} %wk_ref.1) | copy-start | bytes 3145732
  68.8 6.0 %copy-start.1 = (bf16[2048,256]{1,0:T(8,128)(2,1)S(1)}, bf16[2048,256]{1,0:T(8,128)(2,1)}, u32[]{:S(2)}) copy-start(bf16[2048,256]{1,0:T(8,128)(2,1)} %wv_ref.1) | copy-start | bytes 3145732
  68.8 34.4 %all-to-all-start.2 = ((bf16[64,8,1024]{2,1,0:T(8,128)(2,1)}), bf16[64,8,1024]{2,1,0:T(8,128)(2,1)S(1)}, u32[]{:S(2)}, u32[]{:S(2)}) async-start(bf16[64,8,1024]{2,1,0:T(8,128)(2,1)} %bitcast.21), calls=%async_computation.2 | async-start | bytes 2097152 | tf_op jit(solution)/shard_map/all_to_all | solution.py:306
  74.7 1.2 copy-start.5
  78.3 0.7 copy-start.6
  79.0 11.6 %collective-permute-start.2 = (bf16[256,512]{1,0:T(8,128)(2,1)}, bf16[256,512]{1,0:T(8,128)(2,1)S(1)}, u32[]{:S(2)}, u32[]{:S(2)}) collective-permute-start(bf16[256,512]{1,0:T(8,128)(2,1)} %get-tuple-element.25), channel_id=1, source_target_pairs={{0,1},{1,2},{2,3},{3,0},{4,5},{5,6},{6,7},{7,4},{8,9},{9,10},{10,1... | collective-permute-start | bytes 786440 | tf_op jit(solution)/shard_map/ppermute | solution.py:375
  82.1 14.3 %collective-permute-start.3 = (bf16[256,512]{1,0:T(8,128)(2,1)}, bf16[256,512]{1,0:T(8,128)(2,1)}, u32[]{:S(2)}, u32[]{:S(2)}) collective-permute-start(bf16[256,512]{1,0:T(8,128)(2,1)} %get-tuple-element.26), channel_id=1, source_target_pairs={{0,2},{1,3},{2,0},{3,1},{4,6},{5,7},{6,4},{7,5},{8,10},{9,11},{10,... | collective-permute-start | bytes 786440 | tf_op jit(solution)/shard_map/ppermute | solution.py:375
  86.5 3.1 %copy-start.11 = (s32[64,12]{1,0:T(8,128)S(1)}, s32[64,12]{1,0:T(8,128)}, u32[]{:S(2)}) copy-start(s32[64,12]{1,0:T(8,128)} %copy-done.10) | copy-start | bytes 9220
  86.5 11.1 %collective-permute-start.4 = (bf16[256,512]{1,0:T(8,128)(2,1)}, bf16[256,512]{1,0:T(8,128)(2,1)}, u32[]{:S(2)}, u32[]{:S(2)}) collective-permute-start(bf16[256,512]{1,0:T(8,128)(2,1)} %get-tuple-element.27), channel_id=1, source_target_pairs={{0,3},{1,0},{2,1},{3,2},{4,7},{5,4},{6,5},{7,6},{8,11},{9,8},{10,9... | collective-permute-start | bytes 786440 | tf_op jit(solution)/shard_map/ppermute | solution.py:375
  89.6 0.8 copy-start.12
  106.0 4.2 %copy-start.7 = (bf16[256,512]{1,0:T(8,128)(2,1)S(1)}, bf16[256,512]{1,0:T(8,128)(2,1)}, u32[]{:S(2)}) copy-start(bf16[256,512]{1,0:T(8,128)(2,1)} %copy-done.6) | copy-start | bytes 786436
  106.0 17.6 %all-to-all-start.3 = ((bf16[4,256,512]{2,1,0:T(8,128)(2,1)}), bf16[4,256,512]{2,1,0:T(8,128)(2,1)S(1)}, u32[]{:S(2)}, u32[]{:S(2)}) async-start(bf16[4,256,512]{2,1,0:T(8,128)(2,1)} %project.1), calls=%async_computation.3 | async-start | bytes 2097152 | tf_op jit(solution)/shard_map/all_to_all | solution.py:404
  111.4 11.4 %collective-permute-start.5 = (bf16[256,256]{1,0:T(8,128)(2,1)S(1)}, bf16[256,256]{1,0:T(8,128)(2,1)S(1)}, u32[]{:S(2)}, u32[]{:S(2)}) collective-permute-start(bf16[256,256]{1,0:T(8,128)(2,1)S(1)} %get-tuple-element.29), channel_id=1, source_target_pairs={{0,4},{4,0},{1,5},{5,1},{2,6},{6,2},{3,7},{7,3},{8,12},{12,8},{9,1... | collective-permute-start | bytes 393224 | tf_op jit(solution)/shard_map/ppermute | solution.py:384

commit v9 on v8

--- a/solution.py
+++ b/solution.py
@@ -65,6 +65,7 @@
     out_hbm,
     first_hbm,
     last_hbm,
+    _,
     rows_ref,
     wide_ref,
     sems,
@@ -119,7 +120,7 @@
 
 
 def attention_kernel(
-    where_ref, q_ref, k_ref, v_ref, g_ref, far_ref, left_ref, right_ref, dq_ref, dk_ref, dv_ref, shares_ref, folded_ref, wide_ref
+    where_ref, q_ref, k_ref, v_ref, g_ref, far_ref, left_ref, right_ref, _, dq_ref, dk_ref, dv_ref, shares_hbm, folded_ref, wide_ref, shares_ref, sems
 ):
     scale = 1.0 / math.sqrt(HD)
     first_block = where_ref[0] * PER
@@ -143,6 +144,15 @@
     ]
     for pair in range(FOLDED // 2):
         folded_ref[pair, 0:512] = far_ref[:, 512 + pair * HD : 512 + (pair + 1) * HD].astype(jnp.float32)
+    copies = []
+
+    def send(lanes):
+        part = (slice(None), lanes)
+        copies.append(
+            pltpu.make_async_copy(shares_ref.at[part], shares_hbm.at[part], sems.at[len(copies)])
+        )
+        copies[-1].start()
+
     for head in range(2):
         lanes = slice(head * HD, (head + 1) * HD)
         q = q_ref[:, lanes]
@@ -201,9 +211,14 @@
                     to = pl.ds((part - 3) * 4 + slot, 64, stride=8)
                     wide_ref[head, to, :] = dk[rows]
                     wide_ref[2 + head, to, :] = dv[rows]
-    for quarter in range(4):
-        lanes = slice(512 + quarter * HD, 512 + (quarter + 1) * HD)
-        shares_ref[:, lanes] = wide_ref[quarter, 0:512].astype(jnp.bfloat16)
+        send(lanes)
+        send(value_lanes)
+        for quarter in (head, 2 + head):
+            to = slice(512 + quarter * HD, 512 + (quarter + 1) * HD)
+            shares_ref[:, to] = wide_ref[quarter, 0:512].astype(jnp.bfloat16)
+            send(to)
+    for copy in copies:
+        copy.wait()
 
 
 def own_kernel(where_ref, dq_ref, dk_ref, dv_ref, wq_ref, wk_ref, wv_ref, *outs):
@@ -336,12 +351,12 @@
     outside = pl.BlockSpec(memory_space=pl.ANY)
     lanes = 4 * HD + FOLDED * HD // 2
     rim = shape((2, BLK, width))
-    picked, first_block, last_block = call(
+    picked, first_block, last_block, room = call(
         pick_kernel,
         "pick",
-        [shape((shards * 8, lanes)), rim, rim],
+        [shape((shards * 8, lanes)), rim, rim, shape((shards * 8, 4 * width))],
         in_specs=[whole, whole, in_hbm, in_hbm],
-        out_specs=[outside] * 3,
+        out_specs=[outside] * 4,
         scratch_shapes=[
             pltpu.VMEM((shards * 8, lanes), jnp.bfloat16),
             pltpu.VMEM((FOLDED // 2, shards * 8 + 8, HD), jnp.float32),
@@ -357,12 +372,16 @@
         attention_kernel,
         "attention",
         [shape((256, width))] * 3 + [shape((shards * 8, 4 * width))],
-        in_specs=[scalars] + [whole] * 7,
+        in_specs=[scalars] + [whole] * 7 + [outside],
+        out_specs=[whole] * 3 + [outside],
+        input_output_aliases={8: 3},
         scratch_shapes=[
             pltpu.VMEM((FOLDED // 2, shards * 8 + 8, HD), jnp.float32),
             pltpu.VMEM((4, shards * 8 + 8, HD), jnp.float32),
+            pltpu.VMEM((shards * 8, 4 * width), jnp.bfloat16),
+            pltpu.SemaphoreType.DMA((8,)),
         ],
-    )(where, queries, keys, values, out_grad, remote, left, right)
+    )(where, queries, keys, values, out_grad, remote, left, right, room)
     returned = swap(shares, shards, "seq")
 
     own = call(

time: 150 us -> 149 us (level)
    unnamed x29 -> x27, local copies, waits for them, and re-layouts: 3.76 us -> 2.8 us
where the time goes in v9:
time: 149 us
  waiting for transfers between devices  52.9 us (36%)
  starting transfers between devices  51 us (34%)
  blocking collectives  24.1 us (16%)
  Pallas kernels  15.3 us (10%)
  local copies, waits for them, and re-layouts  4.32 us (3%)
    all_to_all x3, waiting for transfers between devices, swap(): lax.all_to_all(cut, axis, split_axis=0, concat_axis=0, tiled=True)  28 us
    all_to_all x3, starting transfers between devices, swap(): lax.all_to_all(cut, axis, split_axis=0, concat_axis=0, tiled=True)  26.1 us
    all_to_all x1, blocking collectives, swap(): lax.all_to_all(cut, axis, split_axis=0, concat_axis=0, tiled=True)  24.1 us
    ppermute x3, starting transfers between devices, body(): lax.ppermute(own[shift], 'x', [(i, (i + shift) % X_SIZE) for i in range(X...  10.5 us
    ppermute x1, waiting for transfers between devices, body(): lax.ppermute(last_block, 'seq', [(i, (i + 1) % shards) for i in range(sha...  10.4 us
    ppermute x3, waiting for transfers between devices, body(): lax.ppermute(own[shift], 'x', [(i, (i + shift) % X_SIZE) for i in range(X...  7.01 us
    ppermute x1, waiting for transfers between devices, body(): other = lax.ppermute(theirs, 'h', [(0, 1), (1, 0)])  6.65 us
    ppermute x1, starting transfers between devices, body(): other = lax.ppermute(theirs, 'h', [(0, 1), (1, 0)])  4.76 us
  transfers between devices with their start and end apart: 10, of which 8 were waited for; matrix products, arithmetic and copies ran while one was open for 2% of the time, Pallas kernels for 2%

profile of v9, /device:TPU:1, one launch (start us, length us, event | category | flops | bytes accessed | tf_op | source)
XLA Modules:
  0.0 148.6 jit_solution(14274735892426270944)
XLA Ops:
  0.0 2.0 %pack.1 = bf16[512,256]{1,0:T(8,128)(2,1)} custom-call(bf16[256,256]{1,0:T(8,128)(2,1)} %k_ref.1, bf16[256,256]{1,0:T(8,128)(2,1)} %v_ref.1), custom_call_target="tpu_custom_call" | custom-call | tf_op jit(solution)/shard_map/pack/pallas_call | solution.py:341
  2.0 0.0 copy-start.12
  2.0 15.4 %all-to-all-start = ((bf16[64,8,256]{2,1,0:T(8,128)(2,1)}), bf16[64,8,256]{2,1,0:T(8,128)(2,1)S(1)}, u32[]{:S(2)}, u32[]{:S(2)}) async-start(bf16[64,8,256]{2,1,0:T(8,128)(2,1)} %bitcast.23), calls=%async_computation | async-start | bytes 524288 | tf_op jit(solution)/shard_map/all_to_all | solution.py:321
  17.4 0.1 concatenate.46
  17.5 0.0 copy-done.12
  17.5 0.1 copy.25
  17.7 0.1 reshape.387
  17.8 0.0 copy-start.9
  17.8 0.1 concatenate.44
  17.9 0.7 slice_bitcast_fusion
  18.6 0.0 copy-done.9
  18.6 0.1 copy.26
  18.6 0.1 concatenate.45
  18.7 0.2 copy.27
  18.9 0.0 copy-start.2
  19.0 0.0 copy-start.3
  19.0 0.4 fusion.1.index_ref
  19.4 11.6 %all-to-all-done = bf16[64,8,256]{2,1,0:T(8,128)(2,1)S(1)} async-done(((bf16[64,8,256]{2,1,0:T(8,128)(2,1)}), bf16[64,8,256]{2,1,0:T(8,128)(2,1)S(1)}, u32[]{:S(2)}, u32[]{:S(2)}) %all-to-all-start) | async-done | bytes 262176 | tf_op jit(solution)/shard_map/all_to_all | solution.py:321
  31.0 0.0 copy-done.2
  31.0 0.0 copy-done.3
  31.0 1.6 %pick.1 = (bf16[512,896]{1,0:T(8,128)(2,1)}, bf16[2,64,256]{2,1,0:T(8,128)(2,1)S(1)}, bf16[2,64,256]{2,1,0:T(8,128)(2,1)S(1)}, bf16[512,1024]{1,0:T(8,128)(2,1)}) custom-call(s32[896,1]{1,0:T(8,128)S(1)} %fusion.1.index_ref, bf16[512,256]{1,0:T(8,128)(2,1)S(1)} %bitcast.21, bf16[256,256]{1,0:T(8,128)(2,1)S(1)} %copy-done.2, bf16[256,256]{1,0:T(8,128)(2,1)S(1)} %copy-done.3), custom_call_target="tpu_custom_call" | custom-call | tf_op jit(solution)/shard_map/pick/pallas_call | solution.py:354
  32.5 0.0 copy-start.7
  32.6 0.0 copy-start.8
  32.6 4.7 %all-to-all-start.1 = ((bf16[64,8,896]{2,1,0:T(8,128)(2,1)}), bf16[64,8,896]{2,1,0:T(8,128)(2,1)S(1)}, u32[]{:S(2)}, u32[]{:S(2)}) async-start(bf16[64,8,896]{2,1,0:T(8,128)(2,1)} %bitcast.6), calls=%async_computation.1 | async-start | bytes 1835008 | tf_op jit(solution)/shard_map/all_to_all | solution.py:321
  37.3 3.5 %collective-permute-start = (bf16[2,64,256]{2,1,0:T(8,128)(2,1)S(1)}, bf16[2,64,256]{2,1,0:T(8,128)(2,1)S(1)}, u32[]{:S(2)}, u32[]{:S(2)}) collective-permute-start(bf16[2,64,256]{2,1,0:T(8,128)(2,1)S(1)} %get-tuple-element.20), channel_id=1, source_target_pairs={{0,8},{8,16},{16,24},{24,32},{32,40},{40,48},{48,56},{56,64},{64,7... | collective-permute-start | bytes 196616 | tf_op jit(solution)/shard_map/ppermute | solution.py:368
  40.9 1.9 %collective-permute-start.1 = (bf16[2,64,256]{2,1,0:T(8,128)(2,1)S(1)}, bf16[2,64,256]{2,1,0:T(8,128)(2,1)S(1)}, u32[]{:S(2)}, u32[]{:S(2)}) collective-permute-start(bf16[2,64,256]{2,1,0:T(8,128)(2,1)S(1)} %get-tuple-element.21), channel_id=1, source_target_pairs={{0,504},{8,0},{16,8},{24,16},{32,24},{40,32},{48,40},{56,48},{64,5... | collective-permute-start | bytes 196616 | tf_op jit(solution)/shard_map/ppermute | solution.py:369
  42.8 0.1 pad_add_fusion.3.where_ref
  42.9 10.4 %collective-permute-done.left_ref = bf16[2,64,256]{2,1,0:T(8,128)(2,1)S(1)} collective-permute-done((bf16[2,64,256]{2,1,0:T(8,128)(2,1)S(1)}, bf16[2,64,256]{2,1,0:T(8,128)(2,1)S(1)}, u32[]{:S(2)}, u32[]{:S(2)}) %collective-permute-start) | collective-permute-done | bytes 65568 | tf_op jit(solution)/shard_map/ppermute | solution.py:368
  53.2 0.0 collective-permute-done.1.right_ref
  53.2 10.9 %all-to-all-done.1 = bf16[64,8,896]{2,1,0:T(8,128)(2,1)S(1)} async-done(((bf16[64,8,896]{2,1,0:T(8,128)(2,1)}), bf16[64,8,896]{2,1,0:T(8,128)(2,1)S(1)}, u32[]{:S(2)}, u32[]{:S(2)}) %all-to-all-start.1) | async-done | bytes 917536 | tf_op jit(solution)/shard_map/all_to_all | solution.py:321
  64.1 0.0 copy-done.7
  64.1 0.0 copy-done.8
  64.1 4.4 %attention.1 = (bf16[256,256]{1,0:T(8,128)(2,1)S(1)}, bf16[256,256]{1,0:T(8,128)(2,1)S(1)}, bf16[256,256]{1,0:T(8,128)(2,1)S(1)}, bf16[512,1024]{1,0:T(8,128)(2,1)}) custom-call(s32[3]{0:T(128)S(1)} %pad_add_fusion.3.where_ref, bf16[256,256]{1,0:T(8,128)(2,1)S(1)} %copy-done.7, bf16[256,256]{1,0:T(8,128)(2,1)S(1)} %copy-done.2, ...), custom_call_target="tpu_custom_call", output_to_operand_aliasing={{3}: (8, {})} | custom-call | tf_op jit(solution)/shard_map/attention/pallas_call | solution.py:371
  68.5 0.0 copy-start
  68.6 0.0 copy-start.1
  68.6 5.9 %all-to-all-start.2 = ((bf16[64,8,1024]{2,1,0:T(8,128)(2,1)}), bf16[64,8,1024]{2,1,0:T(8,128)(2,1)S(1)}, u32[]{:S(2)}, u32[]{:S(2)}) async-start(bf16[64,8,1024]{2,1,0:T(8,128)(2,1)} %bitcast.8), calls=%async_computation.2 | async-start | bytes 2097152 | tf_op jit(solution)/shard_map/all_to_all | solution.py:321
  74.5 0.0 copy-start.4
  74.6 1.2 copy-done.4
  75.8 2.3 %own.1 = (bf16[256,512]{1,0:T(8,128)(2,1)S(1)}, bf16[256,512]{1,0:T(8,128)(2,1)}, bf16[256,512]{1,0:T(8,128)(2,1)}, bf16[256,512]{1,0:T(8,128)(2,1)}) custom-call(s32[3]{0:T(128)S(1)} %pad_add_fusion.3.where_ref, bf16[256,256]{1,0:T(8,128)(2,1)S(1)} %get-tuple-element.24.dq_ref, bf16[256,256]{1,0:T(8,128)(2,1)S(1)} %get-tuple-element.25.dk_ref, ...), custom_call_target="tpu_custom_call" | custom-call | tf_op jit(solution)/shard_map/own/pallas_call | solution.py:387
  78.1 0.7 copy-done.5
  78.8 3.1 %collective-permute-start.2 = (bf16[256,512]{1,0:T(8,128)(2,1)}, bf16[256,512]{1,0:T(8,128)(2,1)S(1)}, u32[]{:S(2)}, u32[]{:S(2)}) collective-permute-start(bf16[256,512]{1,0:T(8,128)(2,1)} %get-tuple-element.27), channel_id=1, source_target_pairs={{0,1},{1,2},{2,3},{3,0},{4,5},{5,6},{6,7},{7,4},{8,9},{9,10},{10,1... | collective-permute-start | bytes 786440 | tf_op jit(solution)/shard_map/ppermute | solution.py:394
  81.9 4.3 %collective-permute-start.3 = (bf16[256,512]{1,0:T(8,128)(2,1)}, bf16[256,512]{1,0:T(8,128)(2,1)}, u32[]{:S(2)}, u32[]{:S(2)}) collective-permute-start(bf16[256,512]{1,0:T(8,128)(2,1)} %get-tuple-element.28), channel_id=1, source_target_pairs={{0,2},{1,3},{2,0},{3,1},{4,6},{5,7},{6,4},{7,5},{8,10},{9,11},{10,... | collective-permute-start | bytes 786440 | tf_op jit(solution)/shard_map/ppermute | solution.py:394
  86.3 0.0 copy-start.10
  86.3 3.1 %collective-permute-start.4 = (bf16[256,512]{1,0:T(8,128)(2,1)}, bf16[256,512]{1,0:T(8,128)(2,1)}, u32[]{:S(2)}, u32[]{:S(2)}) collective-permute-start(bf16[256,512]{1,0:T(8,128)(2,1)} %get-tuple-element.29), channel_id=1, source_target_pairs={{0,3},{1,0},{2,1},{3,2},{4,7},{5,4},{6,5},{7,6},{8,11},{9,8},{10,9... | collective-permute-start | bytes 786440 | tf_op jit(solution)/shard_map/ppermute | solution.py:394
  89.4 0.0 copy-done.10
  89.4 0.0 copy-start.11
  89.4 0.1 stack_reshape.6
  89.5 0.6 copy-done.11
  90.2 0.1 pad_add_fusion
  90.3 0.1 stack_reshape.7
  90.4 0.0 collective-permute-done.2._.refs_1_
  90.4 5.8 %collective-permute-done.3.__.refs_2_ = bf16[256,512]{1,0:T(8,128)(2,1)} collective-permute-done((bf16[256,512]{1,0:T(8,128)(2,1)}, bf16[256,512]{1,0:T(8,128)(2,1)}, u32[]{:S(2)}, u32[]{:S(2)}) %collective-permute-start.3) | collective-permute-done | bytes 262176 | tf_op jit(solution)/shard_map/ppermute | solution.py:394
  96.2 1.2 collective-permute-done.4.___.refs_3_
  97.4 5.6 %all-to-all-done.2 = bf16[64,8,1024]{2,1,0:T(8,128)(2,1)S(1)} async-done(((bf16[64,8,1024]{2,1,0:T(8,128)(2,1)}), bf16[64,8,1024]{2,1,0:T(8,128)(2,1)S(1)}, u32[]{:S(2)}, u32[]{:S(2)}) %all-to-all-start.2) | async-done | bytes 1048608 | tf_op jit(solution)/shard_map/all_to_all | solution.py:321
  103.0 2.8 %project.1 = bf16[4,256,512]{2,1,0:T(8,128)(2,1)} custom-call(s32[2,512]{1,0:T(2,128)S(1)} %fusion.9.index_ref, bf16[512,1024]{1,0:T(8,128)(2,1)S(1)} %bitcast.16, bf16[2,4,256,256]{3,2,1,0:T(8,128)(2,1)S(1)} %bitcast.17, bf16[2,4,256,256]{3,2,1,0:T(8,128)(2,1)S(1)} %bitcast.18, bf16[256,512]{1,0:T(8,128)(2,1)S(1)} %collective-permute-done.2._.refs_1_, ...), custom_call_target="tpu_custom_call" | custom-call | tf_op jit(solution)/shard_map/project/pallas_call | solution.py:405
  105.8 4.2 %all-to-all-start.3 = ((bf16[4,256,512]{2,1,0:T(8,128)(2,1)}), bf16[4,256,512]{2,1,0:T(8,128)(2,1)S(1)}, u32[]{:S(2)}, u32[]{:S(2)}) async-start(bf16[4,256,512]{2,1,0:T(8,128)(2,1)} %project.1), calls=%async_computation.3 | async-start | bytes 2097152 | tf_op jit(solution)/shard_map/all_to_all | solution.py:423
  110.0 0.0 copy-done.6
  110.0 1.2 own_sum.1
  111.2 4.8 %collective-permute-start.5 = (bf16[256,256]{1,0:T(8,128)(2,1)S(1)}, bf16[256,256]{1,0:T(8,128)(2,1)S(1)}, u32[]{:S(2)}, u32[]{:S(2)}) collective-permute-start(bf16[256,256]{1,0:T(8,128)(2,1)S(1)} %get-tuple-element.31), channel_id=1, source_target_pairs={{0,4},{4,0},{1,5},{5,1},{2,6},{6,2},{3,7},{7,3},{8,12},{12,8},{9,1... | collective-permute-start | bytes 393224 | tf_op jit(solution)/shard_map/ppermute | solution.py:403
  115.9 6.6 %collective-permute-done.5._.other_ref = bf16[256,256]{1,0:T(8,128)(2,1)S(1)} collective-permute-done((bf16[256,256]{1,0:T(8,128)(2,1)S(1)}, bf16[256,256]{1,0:T(8,128)(2,1)S(1)}, u32[]{:S(2)}, u32[]{:S(2)}) %collective-permute-start.5) | collective-permute-done | bytes 131104 | tf_op jit(solution)/shard_map/ppermute | solution.py:403
  122.6 0.9 all-to-all-done.3.parts_ref
  123.5 0.2 spread.1
  123.7 24.1 %all_to_all.25 = bf16[128,8,128]{2,1,0:T(8,128)(2,1)S(1)} all-to-all(bf16[128,8,128]{2,1,0:T(8,128)(2,1)S(1)} %bitcast.22), channel_id=1, replica_groups=mesh['seq'=64,'h'=2,'x'=4] {'h','seq'}, dimensions={0} | all-to-all | bytes 524288 | tf_op jit(solution)/shard_map/all_to_all | solution.py:321
  147.8 0.8 finish.1
  (9 shorter events, 0.1 us)
Async XLA Ops:
  2.0 15.5 %copy-start.12 = (s32[256,3]{0,1:T(4,128)S(1)}, s32[256,3]{0,1:T(4,128)}, u32[]{:S(2)}) copy-start(s32[256,3]{0,1:T(4,128)} %param.12) | copy-start | bytes 9220
  2.0 29.0 %all-to-all-start = ((bf16[64,8,256]{2,1,0:T(8,128)(2,1)}), bf16[64,8,256]{2,1,0:T(8,128)(2,1)S(1)}, u32[]{:S(2)}, u32[]{:S(2)}) async-start(bf16[64,8,256]{2,1,0:T(8,128)(2,1)} %bitcast.23), calls=%async_computation | async-start | bytes 524288 | tf_op jit(solution)/shard_map/all_to_all | solution.py:321
  17.8 0.8 copy-start.9
  18.9 12.0 %copy-start.2 = (bf16[256,256]{1,0:T(8,128)(2,1)S(1)}, bf16[256,256]{1,0:T(8,128)(2,1)}, u32[]{:S(2)}) copy-start(bf16[256,256]{1,0:T(8,128)(2,1)} %k_ref.1) | copy-start | bytes 393220
  19.0 12.0 %copy-start.3 = (bf16[256,256]{1,0:T(8,128)(2,1)S(1)}, bf16[256,256]{1,0:T(8,128)(2,1)}, u32[]{:S(2)}) copy-start(bf16[256,256]{1,0:T(8,128)(2,1)} %v_ref.1) | copy-start | bytes 393220
  32.5 31.6 %copy-start.7 = (bf16[256,256]{1,0:T(8,128)(2,1)S(1)}, bf16[256,256]{1,0:T(8,128)(2,1)}, u32[]{:S(2)}) copy-start(bf16[256,256]{1,0:T(8,128)(2,1)} %q_ref.1) | copy-start | bytes 393220
  32.6 31.6 %copy-start.8 = (bf16[256,256]{1,0:T(8,128)(2,1)S(1)}, bf16[256,256]{1,0:T(8,128)(2,1)}, u32[]{:S(2)}) copy-start(bf16[256,256]{1,0:T(8,128)(2,1)} %g_ref.1) | copy-start | bytes 393220
  32.6 31.5 %all-to-all-start.1 = ((bf16[64,8,896]{2,1,0:T(8,128)(2,1)}), bf16[64,8,896]{2,1,0:T(8,128)(2,1)S(1)}, u32[]{:S(2)}, u32[]{:S(2)}) async-start(bf16[64,8,896]{2,1,0:T(8,128)(2,1)} %bitcast.6), calls=%async_computation.1 | async-start | bytes 1835008 | tf_op jit(solution)/shard_map/all_to_all | solution.py:321
  37.3 15.9 %collective-permute-start = (bf16[2,64,256]{2,1,0:T(8,128)(2,1)S(1)}, bf16[2,64,256]{2,1,0:T(8,128)(2,1)S(1)}, u32[]{:S(2)}, u32[]{:S(2)}) collective-permute-start(bf16[2,64,256]{2,1,0:T(8,128)(2,1)S(1)} %get-tuple-element.20), channel_id=1, source_target_pairs={{0,8},{8,16},{16,24},{24,32},{32,40},{40,48},{48,56},{56,64},{64,7... | collective-permute-start | bytes 196616 | tf_op jit(solution)/shard_map/ppermute | solution.py:368
  40.9 12.4 %collective-permute-start.1 = (bf16[2,64,256]{2,1,0:T(8,128)(2,1)S(1)}, bf16[2,64,256]{2,1,0:T(8,128)(2,1)S(1)}, u32[]{:S(2)}, u32[]{:S(2)}) collective-permute-start(bf16[2,64,256]{2,1,0:T(8,128)(2,1)S(1)} %get-tuple-element.21), channel_id=1, source_target_pairs={{0,504},{8,0},{16,8},{24,16},{32,24},{40,32},{48,40},{56,48},{64,5... | collective-permute-start | bytes 196616 | tf_op jit(solution)/shard_map/ppermute | solution.py:369
  68.5 6.0 %copy-start = (bf16[2048,256]{1,0:T(8,128)(2,1)S(1)}, bf16[2048,256]{1,0:T(8,128)(2,1)}, u32[]{:S(2)}) copy-start(bf16[2048,256]{1,0:T(8,128)(2,1)} %wk_ref.1) | copy-start | bytes 3145732
  68.6 6.0 %copy-start.1 = (bf16[2048,256]{1,0:T(8,128)(2,1)S(1)}, bf16[2048,256]{1,0:T(8,128)(2,1)}, u32[]{:S(2)}) copy-start(bf16[2048,256]{1,0:T(8,128)(2,1)} %wv_ref.1) | copy-start | bytes 3145732
  68.6 34.4 %all-to-all-start.2 = ((bf16[64,8,1024]{2,1,0:T(8,128)(2,1)}), bf16[64,8,1024]{2,1,0:T(8,128)(2,1)S(1)}, u32[]{:S(2)}, u32[]{:S(2)}) async-start(bf16[64,8,1024]{2,1,0:T(8,128)(2,1)} %bitcast.8), calls=%async_computation.2 | async-start | bytes 2097152 | tf_op jit(solution)/shard_map/all_to_all | solution.py:321
  74.5 1.2 copy-start.4
  78.1 0.7 copy-start.5
  78.8 11.6 %collective-permute-start.2 = (bf16[256,512]{1,0:T(8,128)(2,1)}, bf16[256,512]{1,0:T(8,128)(2,1)S(1)}, u32[]{:S(2)}, u32[]{:S(2)}) collective-permute-start(bf16[256,512]{1,0:T(8,128)(2,1)} %get-tuple-element.27), channel_id=1, source_target_pairs={{0,1},{1,2},{2,3},{3,0},{4,5},{5,6},{6,7},{7,4},{8,9},{9,10},{10,1... | collective-permute-start | bytes 786440 | tf_op jit(solution)/shard_map/ppermute | solution.py:394
  81.9 14.3 %collective-permute-start.3 = (bf16[256,512]{1,0:T(8,128)(2,1)}, bf16[256,512]{1,0:T(8,128)(2,1)}, u32[]{:S(2)}, u32[]{:S(2)}) collective-permute-start(bf16[256,512]{1,0:T(8,128)(2,1)} %get-tuple-element.28), channel_id=1, source_target_pairs={{0,2},{1,3},{2,0},{3,1},{4,6},{5,7},{6,4},{7,5},{8,10},{9,11},{10,... | collective-permute-start | bytes 786440 | tf_op jit(solution)/shard_map/ppermute | solution.py:394
  86.3 3.1 %copy-start.10 = (s32[64,12]{1,0:T(8,128)S(1)}, s32[64,12]{1,0:T(8,128)}, u32[]{:S(2)}) copy-start(s32[64,12]{1,0:T(8,128)} %copy-done.9) | copy-start | bytes 9220
  86.3 11.1 %collective-permute-start.4 = (bf16[256,512]{1,0:T(8,128)(2,1)}, bf16[256,512]{1,0:T(8,128)(2,1)}, u32[]{:S(2)}, u32[]{:S(2)}) collective-permute-start(bf16[256,512]{1,0:T(8,128)(2,1)} %get-tuple-element.29), channel_id=1, source_target_pairs={{0,3},{1,0},{2,1},{3,2},{4,7},{5,4},{6,5},{7,6},{8,11},{9,8},{10,9... | collective-permute-start | bytes 786440 | tf_op jit(solution)/shard_map/ppermute | solution.py:394
  89.4 0.8 copy-start.11
  105.8 4.2 %copy-start.6 = (bf16[256,512]{1,0:T(8,128)(2,1)S(1)}, bf16[256,512]{1,0:T(8,128)(2,1)}, u32[]{:S(2)}) copy-start(bf16[256,512]{1,0:T(8,128)(2,1)} %copy-done.5) | copy-start | bytes 786436
  105.8 17.6 %all-to-all-start.3 = ((bf16[4,256,512]{2,1,0:T(8,128)(2,1)}), bf16[4,256,512]{2,1,0:T(8,128)(2,1)S(1)}, u32[]{:S(2)}, u32[]{:S(2)}) async-start(bf16[4,256,512]{2,1,0:T(8,128)(2,1)} %project.1), calls=%async_computation.3 | async-start | bytes 2097152 | tf_op jit(solution)/shard_map/all_to_all | solution.py:423
  111.2 11.4 %collective-permute-start.5 = (bf16[256,256]{1,0:T(8,128)(2,1)S(1)}, bf16[256,256]{1,0:T(8,128)(2,1)S(1)}, u32[]{:S(2)}, u32[]{:S(2)}) collective-permute-start(bf16[256,256]{1,0:T(8,128)(2,1)S(1)} %get-tuple-element.31), channel_id=1, source_target_pairs={{0,4},{4,0},{1,5},{5,1},{2,6},{6,2},{3,7},{7,3},{8,12},{12,8},{9,1... | collective-permute-start | bytes 393224 | tf_op jit(solution)/shard_map/ppermute | solution.py:403

commit v10 on v8

--- a/solution.py
+++ b/solution.py
@@ -147,6 +147,7 @@
         lanes = slice(head * HD, (head + 1) * HD)
         q = q_ref[:, lanes]
         g = g_ref[:, lanes]
+        q_turned, g_turned = q.T, g.T
 
         def parts(own_ref, kind):
             far_lanes = slice(kind * 256 + head * HD, kind * 256 + (head + 1) * HD)
@@ -167,13 +168,12 @@
         key_parts = parts(k_ref, 0)
         value_parts = parts(v_ref, 1)
         weighted = [
-            jnp.where(mask, jnp.exp(nt(k, q) * scale), 0.0) for k, mask in zip(key_parts, masks)
+            jnp.where(mask, jnp.exp(nn(k, q_turned) * scale), 0.0) for k, mask in zip(key_parts, masks)
         ]
         total = functools.reduce(jnp.add, [jnp.sum(w, axis=0, keepdims=True) for w in weighted])
         inverse = 1.0 / total
-        grad_probs = [nt(v, g) for v in value_parts]
-        probs = [w * inverse for w in weighted]
-        probs_low = [p.astype(jnp.bfloat16) for p in probs]
+        grad_probs = [nn(v, g_turned) for v in value_parts]
+        probs_low = [(w * inverse).astype(jnp.bfloat16) for w in weighted]
         delta = functools.reduce(
             jnp.add,
             [
@@ -181,8 +181,10 @@
                 for p, d in zip(probs_low, grad_probs)
             ],
         )
-        grad_low = [(p * (d - delta)).astype(jnp.bfloat16) for p, d in zip(probs, grad_probs)]
-        dq = functools.reduce(jnp.add, [tn(k, w) for k, w in zip(key_parts, grad_low)])
+        grad_low = [
+            (w * (inverse * (d - delta))).astype(jnp.bfloat16) for w, d in zip(weighted, grad_probs)
+        ]
+        dq = tn(jnp.concatenate(key_parts, axis=0), jnp.concatenate(grad_low, axis=0))
         dq_ref[:, lanes] = (scale * dq).T.astype(jnp.bfloat16)
         value_lanes = slice(256 + head * HD, 256 + (head + 1) * HD)
         for part in range(len(masks)):

time: 150 us -> 150 us (level)
  no operation moved by 1% of the time
where the time goes in v10:
time: 150 us; the launch traced here: 149 us
  waiting for transfers between devices  53 us (35%)
  starting transfers between devices  51 us (34%)
  blocking collectives  24.1 us (16%)
  Pallas kernels  14.5 us (10%)
  local copies, waits for them, and re-layouts  5.28 us (4%)
    all_to_all x3, waiting for transfers between devices, swap(): lax.all_to_all(cut, axis, split_axis=0, concat_axis=0, tiled=True)  28 us
    all_to_all x3, starting transfers between devices, swap(): lax.all_to_all(cut, axis, split_axis=0, concat_axis=0, tiled=True)  26.1 us
    all_to_all x1, blocking collectives, swap(): lax.all_to_all(cut, axis, split_axis=0, concat_axis=0, tiled=True)  24.1 us
    ppermute x3, starting transfers between devices, body(): lax.ppermute(own[shift], 'x', [(i, (i + shift) % X_SIZE) for i in range(X...  10.5 us
    ppermute x1, waiting for transfers between devices, body(): lax.ppermute(last_block, 'seq', [(i, (i + 1) % shards) for i in range(sha...  10.4 us
    ppermute x3, waiting for transfers between devices, body(): lax.ppermute(own[shift], 'x', [(i, (i + shift) % X_SIZE) for i in range(X...  7.02 us
    ppermute x1, waiting for transfers between devices, body(): other = lax.ppermute(theirs, 'h', [(0, 1), (1, 0)])  6.65 us
    ppermute x1, starting transfers between devices, body(): other = lax.ppermute(theirs, 'h', [(0, 1), (1, 0)])  4.76 us
  transfers between devices with their start and end apart: 10, of which 8 were waited for; matrix products, arithmetic and copies ran while one was open for 2% of the time, Pallas kernels for 2%

profile of v10, /device:TPU:1, one launch (start us, length us, event | category | flops | bytes accessed | tf_op | source)
XLA Modules:
  0.0 148.8 jit_solution(5193076907665479678)
XLA Ops:
  0.0 2.0 %pack.1 = bf16[512,256]{1,0:T(8,128)(2,1)} custom-call(bf16[256,256]{1,0:T(8,128)(2,1)} %k_ref.1, bf16[256,256]{1,0:T(8,128)(2,1)} %v_ref.1), custom_call_target="tpu_custom_call" | custom-call | tf_op jit(solution)/shard_map/pack/pallas_call | solution.py:328
  2.0 0.0 copy-start.13
  2.0 15.4 %all-to-all-start = ((bf16[64,8,256]{2,1,0:T(8,128)(2,1)}), bf16[64,8,256]{2,1,0:T(8,128)(2,1)S(1)}, u32[]{:S(2)}, u32[]{:S(2)}) async-start(bf16[64,8,256]{2,1,0:T(8,128)(2,1)} %bitcast.24), calls=%async_computation | async-start | bytes 524288 | tf_op jit(solution)/shard_map/all_to_all | solution.py:308
  17.4 0.1 concatenate.46
  17.5 0.0 copy-done.13
  17.5 0.1 copy.24
  17.7 0.1 reshape.387
  17.8 0.0 copy-start.10
  17.8 0.1 concatenate.44
  17.9 0.7 slice_bitcast_fusion
  18.6 0.0 copy-done.10
  18.6 0.1 copy.25
  18.6 0.1 concatenate.45
  18.7 0.2 copy.26
  18.9 0.0 copy-start.2
  19.0 0.0 copy-start.3
  19.0 0.4 fusion.1.index_ref
  19.4 11.6 %all-to-all-done = bf16[64,8,256]{2,1,0:T(8,128)(2,1)S(1)} async-done(((bf16[64,8,256]{2,1,0:T(8,128)(2,1)}), bf16[64,8,256]{2,1,0:T(8,128)(2,1)S(1)}, u32[]{:S(2)}, u32[]{:S(2)}) %all-to-all-start) | async-done | bytes 262176 | tf_op jit(solution)/shard_map/all_to_all | solution.py:308
  30.9 0.0 copy-done.2
  31.0 0.0 copy-done.3
  31.0 1.6 %pick.1 = (bf16[512,896]{1,0:T(8,128)(2,1)}, bf16[2,64,256]{2,1,0:T(8,128)(2,1)S(1)}, bf16[2,64,256]{2,1,0:T(8,128)(2,1)S(1)}) custom-call(s32[896,1]{1,0:T(8,128)S(1)} %fusion.1.index_ref, bf16[512,256]{1,0:T(8,128)(2,1)S(1)} %bitcast.22, bf16[256,256]{1,0:T(8,128)(2,1)S(1)} %copy-done.2, bf16[256,256]{1,0:T(8,128)(2,1)S(1)} %copy-done.3), custom_call_target="tpu_custom_call" | custom-call | tf_op jit(solution)/shard_map/pick/pallas_call | solution.py:341
  32.5 0.0 copy-start.8
  32.5 0.0 copy-start.9
  32.6 4.7 %all-to-all-start.1 = ((bf16[64,8,896]{2,1,0:T(8,128)(2,1)}), bf16[64,8,896]{2,1,0:T(8,128)(2,1)S(1)}, u32[]{:S(2)}, u32[]{:S(2)}) async-start(bf16[64,8,896]{2,1,0:T(8,128)(2,1)} %bitcast.6), calls=%async_computation.1 | async-start | bytes 1835008 | tf_op jit(solution)/shard_map/all_to_all | solution.py:308
  37.3 3.5 %collective-permute-start = (bf16[2,64,256]{2,1,0:T(8,128)(2,1)S(1)}, bf16[2,64,256]{2,1,0:T(8,128)(2,1)S(1)}, u32[]{:S(2)}, u32[]{:S(2)}) collective-permute-start(bf16[2,64,256]{2,1,0:T(8,128)(2,1)S(1)} %get-tuple-element.19), channel_id=1, source_target_pairs={{0,8},{8,16},{16,24},{24,32},{32,40},{40,48},{48,56},{56,64},{64,7... | collective-permute-start | bytes 196616 | tf_op jit(solution)/shard_map/ppermute | solution.py:355
  40.9 1.9 %collective-permute-start.1 = (bf16[2,64,256]{2,1,0:T(8,128)(2,1)S(1)}, bf16[2,64,256]{2,1,0:T(8,128)(2,1)S(1)}, u32[]{:S(2)}, u32[]{:S(2)}) collective-permute-start(bf16[2,64,256]{2,1,0:T(8,128)(2,1)S(1)} %get-tuple-element.20), channel_id=1, source_target_pairs={{0,504},{8,0},{16,8},{24,16},{32,24},{40,32},{48,40},{56,48},{64,5... | collective-permute-start | bytes 196616 | tf_op jit(solution)/shard_map/ppermute | solution.py:356
  42.8 0.1 pad_add_fusion.3.where_ref
  42.9 10.4 %collective-permute-done.left_ref = bf16[2,64,256]{2,1,0:T(8,128)(2,1)S(1)} collective-permute-done((bf16[2,64,256]{2,1,0:T(8,128)(2,1)S(1)}, bf16[2,64,256]{2,1,0:T(8,128)(2,1)S(1)}, u32[]{:S(2)}, u32[]{:S(2)}) %collective-permute-start) | collective-permute-done | bytes 65568 | tf_op jit(solution)/shard_map/ppermute | solution.py:355
  53.2 0.0 collective-permute-done.1.right_ref
  53.2 10.9 %all-to-all-done.1 = bf16[64,8,896]{2,1,0:T(8,128)(2,1)S(1)} async-done(((bf16[64,8,896]{2,1,0:T(8,128)(2,1)}), bf16[64,8,896]{2,1,0:T(8,128)(2,1)S(1)}, u32[]{:S(2)}, u32[]{:S(2)}) %all-to-all-start.1) | async-done | bytes 917536 | tf_op jit(solution)/shard_map/all_to_all | solution.py:308
  64.1 0.0 copy-done.8
  64.1 3.7 %attention.1 = (bf16[256,256]{1,0:T(8,128)(2,1)S(1)}, bf16[256,256]{1,0:T(8,128)(2,1)S(1)}, bf16[256,256]{1,0:T(8,128)(2,1)S(1)}, bf16[512,1024]{1,0:T(8,128)(2,1)S(1)}) custom-call(s32[3]{0:T(128)S(1)} %pad_add_fusion.3.where_ref, bf16[256,256]{1,0:T(8,128)(2,1)S(1)} %copy-done.8, bf16[256,256]{1,0:T(8,128)(2,1)S(1)} %copy-done.2, ...), custom_call_target="tpu_custom_call" | custom-call | tf_op jit(solution)/shard_map/attention/pallas_call | solution.py:358
  67.8 1.0 copy-done.4
  68.8 5.9 %all-to-all-start.2 = ((bf16[64,8,1024]{2,1,0:T(8,128)(2,1)}), bf16[64,8,1024]{2,1,0:T(8,128)(2,1)S(1)}, u32[]{:S(2)}, u32[]{:S(2)}) async-start(bf16[64,8,1024]{2,1,0:T(8,128)(2,1)} %bitcast.21), calls=%async_computation.2 | async-start | bytes 2097152 | tf_op jit(solution)/shard_map/all_to_all | solution.py:308
  74.7 0.0 copy-done
  74.7 0.0 copy-done.1
  74.7 0.0 copy-start.5
  74.7 1.2 copy-done.5
  76.0 2.3 %own.1 = (bf16[256,512]{1,0:T(8,128)(2,1)S(1)}, bf16[256,512]{1,0:T(8,128)(2,1)}, bf16[256,512]{1,0:T(8,128)(2,1)}, bf16[256,512]{1,0:T(8,128)(2,1)}) custom-call(s32[3]{0:T(128)S(1)} %pad_add_fusion.3.where_ref, bf16[256,256]{1,0:T(8,128)(2,1)S(1)} %get-tuple-element.22.dq_ref, bf16[256,256]{1,0:T(8,128)(2,1)S(1)} %get-tuple-element.23.dk_ref, ...), custom_call_target="tpu_custom_call" | custom-call | tf_op jit(solution)/shard_map/own/pallas_call | solution.py:370
  78.3 0.7 copy-done.6
  79.0 3.1 %collective-permute-start.2 = (bf16[256,512]{1,0:T(8,128)(2,1)}, bf16[256,512]{1,0:T(8,128)(2,1)S(1)}, u32[]{:S(2)}, u32[]{:S(2)}) collective-permute-start(bf16[256,512]{1,0:T(8,128)(2,1)} %get-tuple-element.25), channel_id=1, source_target_pairs={{0,1},{1,2},{2,3},{3,0},{4,5},{5,6},{6,7},{7,4},{8,9},{9,10},{10,1... | collective-permute-start | bytes 786440 | tf_op jit(solution)/shard_map/ppermute | solution.py:377
  82.1 4.4 %collective-permute-start.3 = (bf16[256,512]{1,0:T(8,128)(2,1)}, bf16[256,512]{1,0:T(8,128)(2,1)}, u32[]{:S(2)}, u32[]{:S(2)}) collective-permute-start(bf16[256,512]{1,0:T(8,128)(2,1)} %get-tuple-element.26), channel_id=1, source_target_pairs={{0,2},{1,3},{2,0},{3,1},{4,6},{5,7},{6,4},{7,5},{8,10},{9,11},{10,... | collective-permute-start | bytes 786440 | tf_op jit(solution)/shard_map/ppermute | solution.py:377
  86.5 3.0 %collective-permute-start.4 = (bf16[256,512]{1,0:T(8,128)(2,1)}, bf16[256,512]{1,0:T(8,128)(2,1)}, u32[]{:S(2)}, u32[]{:S(2)}) collective-permute-start(bf16[256,512]{1,0:T(8,128)(2,1)} %get-tuple-element.27), channel_id=1, source_target_pairs={{0,3},{1,0},{2,1},{3,2},{4,7},{5,4},{6,5},{7,6},{8,11},{9,8},{10,9... | collective-permute-start | bytes 786440 | tf_op jit(solution)/shard_map/ppermute | solution.py:377
  89.6 0.0 copy-done.11
  89.6 0.0 copy-start.12
  89.6 0.1 stack_reshape.6
  89.7 0.6 copy-done.12
  90.4 0.1 pad_add_fusion
  90.4 0.1 stack_reshape.7
  90.6 0.0 collective-permute-done.2._.refs_1_
  90.6 5.8 %collective-permute-done.3.__.refs_2_ = bf16[256,512]{1,0:T(8,128)(2,1)} collective-permute-done((bf16[256,512]{1,0:T(8,128)(2,1)}, bf16[256,512]{1,0:T(8,128)(2,1)}, u32[]{:S(2)}, u32[]{:S(2)}) %collective-permute-start.3) | collective-permute-done | bytes 262176 | tf_op jit(solution)/shard_map/ppermute | solution.py:377
  96.4 1.2 collective-permute-done.4.___.refs_3_
  97.6 5.6 %all-to-all-done.2 = bf16[64,8,1024]{2,1,0:T(8,128)(2,1)S(1)} async-done(((bf16[64,8,1024]{2,1,0:T(8,128)(2,1)}), bf16[64,8,1024]{2,1,0:T(8,128)(2,1)S(1)}, u32[]{:S(2)}, u32[]{:S(2)}) %all-to-all-start.2) | async-done | bytes 1048608 | tf_op jit(solution)/shard_map/all_to_all | solution.py:308
  103.2 2.8 %project.1 = bf16[4,256,512]{2,1,0:T(8,128)(2,1)} custom-call(s32[2,512]{1,0:T(2,128)S(1)} %fusion.9.index_ref, bf16[512,1024]{1,0:T(8,128)(2,1)S(1)} %bitcast.16, bf16[2,4,256,256]{3,2,1,0:T(8,128)(2,1)S(1)} %bitcast.17, bf16[2,4,256,256]{3,2,1,0:T(8,128)(2,1)S(1)} %bitcast.18, bf16[256,512]{1,0:T(8,128)(2,1)S(1)} %collective-permute-done.2._.refs_1_, ...), custom_call_target="tpu_custom_call" | custom-call | tf_op jit(solution)/shard_map/project/pallas_call | solution.py:388
  106.0 0.0 copy-start.7
  106.0 4.2 %all-to-all-start.3 = ((bf16[4,256,512]{2,1,0:T(8,128)(2,1)}), bf16[4,256,512]{2,1,0:T(8,128)(2,1)S(1)}, u32[]{:S(2)}, u32[]{:S(2)}) async-start(bf16[4,256,512]{2,1,0:T(8,128)(2,1)} %project.1), calls=%async_computation.3 | async-start | bytes 2097152 | tf_op jit(solution)/shard_map/all_to_all | solution.py:406
  110.2 0.0 copy-done.7
  110.2 1.2 own_sum.1
  111.4 4.8 %collective-permute-start.5 = (bf16[256,256]{1,0:T(8,128)(2,1)S(1)}, bf16[256,256]{1,0:T(8,128)(2,1)S(1)}, u32[]{:S(2)}, u32[]{:S(2)}) collective-permute-start(bf16[256,256]{1,0:T(8,128)(2,1)S(1)} %get-tuple-element.29), channel_id=1, source_target_pairs={{0,4},{4,0},{1,5},{5,1},{2,6},{6,2},{3,7},{7,3},{8,12},{12,8},{9,1... | collective-permute-start | bytes 393224 | tf_op jit(solution)/shard_map/ppermute | solution.py:386
  116.1 6.6 %collective-permute-done.5._.other_ref = bf16[256,256]{1,0:T(8,128)(2,1)S(1)} collective-permute-done((bf16[256,256]{1,0:T(8,128)(2,1)S(1)}, bf16[256,256]{1,0:T(8,128)(2,1)S(1)}, u32[]{:S(2)}, u32[]{:S(2)}) %collective-permute-start.5) | collective-permute-done | bytes 131104 | tf_op jit(solution)/shard_map/ppermute | solution.py:386
  122.8 0.9 all-to-all-done.3.parts_ref
  123.7 0.2 spread.1
  123.9 24.1 %all_to_all.25 = bf16[128,8,128]{2,1,0:T(8,128)(2,1)S(1)} all-to-all(bf16[128,8,128]{2,1,0:T(8,128)(2,1)S(1)} %bitcast.23), channel_id=1, replica_groups=mesh['seq'=64,'h'=2,'x'=4] {'h','seq'}, dimensions={0} | all-to-all | bytes 524288 | tf_op jit(solution)/shard_map/all_to_all | solution.py:308
  148.0 0.8 finish.1
  (11 shorter events, 0.1 us)
Async XLA Ops:
  2.0 15.5 %copy-start.13 = (s32[256,3]{0,1:T(4,128)S(1)}, s32[256,3]{0,1:T(4,128)}, u32[]{:S(2)}) copy-start(s32[256,3]{0,1:T(4,128)} %param.12) | copy-start | bytes 9220
  2.0 29.0 %all-to-all-start = ((bf16[64,8,256]{2,1,0:T(8,128)(2,1)}), bf16[64,8,256]{2,1,0:T(8,128)(2,1)S(1)}, u32[]{:S(2)}, u32[]{:S(2)}) async-start(bf16[64,8,256]{2,1,0:T(8,128)(2,1)} %bitcast.24), calls=%async_computation | async-start | bytes 524288 | tf_op jit(solution)/shard_map/all_to_all | solution.py:308
  17.8 0.8 copy-start.10
  18.9 12.0 %copy-start.2 = (bf16[256,256]{1,0:T(8,128)(2,1)S(1)}, bf16[256,256]{1,0:T(8,128)(2,1)}, u32[]{:S(2)}) copy-start(bf16[256,256]{1,0:T(8,128)(2,1)} %k_ref.1) | copy-start | bytes 393220
  19.0 12.0 %copy-start.3 = (bf16[256,256]{1,0:T(8,128)(2,1)S(1)}, bf16[256,256]{1,0:T(8,128)(2,1)}, u32[]{:S(2)}) copy-start(bf16[256,256]{1,0:T(8,128)(2,1)} %v_ref.1) | copy-start | bytes 393220
  32.5 31.6 %copy-start.8 = (bf16[256,256]{1,0:T(8,128)(2,1)S(1)}, bf16[256,256]{1,0:T(8,128)(2,1)}, u32[]{:S(2)}) copy-start(bf16[256,256]{1,0:T(8,128)(2,1)} %q_ref.1) | copy-start | bytes 393220
  32.5 31.6 %copy-start.9 = (bf16[256,256]{1,0:T(8,128)(2,1)S(1)}, bf16[256,256]{1,0:T(8,128)(2,1)}, u32[]{:S(2)}) copy-start(bf16[256,256]{1,0:T(8,128)(2,1)} %g_ref.1) | copy-start | bytes 393220
  32.6 31.5 %all-to-all-start.1 = ((bf16[64,8,896]{2,1,0:T(8,128)(2,1)}), bf16[64,8,896]{2,1,0:T(8,128)(2,1)S(1)}, u32[]{:S(2)}, u32[]{:S(2)}) async-start(bf16[64,8,896]{2,1,0:T(8,128)(2,1)} %bitcast.6), calls=%async_computation.1 | async-start | bytes 1835008 | tf_op jit(solution)/shard_map/all_to_all | solution.py:308
  37.3 15.9 %collective-permute-start = (bf16[2,64,256]{2,1,0:T(8,128)(2,1)S(1)}, bf16[2,64,256]{2,1,0:T(8,128)(2,1)S(1)}, u32[]{:S(2)}, u32[]{:S(2)}) collective-permute-start(bf16[2,64,256]{2,1,0:T(8,128)(2,1)S(1)} %get-tuple-element.19), channel_id=1, source_target_pairs={{0,8},{8,16},{16,24},{24,32},{32,40},{40,48},{48,56},{56,64},{64,7... | collective-permute-start | bytes 196616 | tf_op jit(solution)/shard_map/ppermute | solution.py:355
  40.9 12.4 %collective-permute-start.1 = (bf16[2,64,256]{2,1,0:T(8,128)(2,1)S(1)}, bf16[2,64,256]{2,1,0:T(8,128)(2,1)S(1)}, u32[]{:S(2)}, u32[]{:S(2)}) collective-permute-start(bf16[2,64,256]{2,1,0:T(8,128)(2,1)S(1)} %get-tuple-element.20), channel_id=1, source_target_pairs={{0,504},{8,0},{16,8},{24,16},{32,24},{40,32},{48,40},{56,48},{64,5... | collective-permute-start | bytes 196616 | tf_op jit(solution)/shard_map/ppermute | solution.py:356
  67.8 1.0 copy-start.4
  68.8 5.9 %copy-start = (bf16[2048,256]{1,0:T(8,128)(2,1)S(1)}, bf16[2048,256]{1,0:T(8,128)(2,1)}, u32[]{:S(2)}) copy-start(bf16[2048,256]{1,0:T(8,128)(2,1)} %wk_ref.1) | copy-start | bytes 3145732
  68.8 5.9 %copy-start.1 = (bf16[2048,256]{1,0:T(8,128)(2,1)S(1)}, bf16[2048,256]{1,0:T(8,128)(2,1)}, u32[]{:S(2)}) copy-start(bf16[2048,256]{1,0:T(8,128)(2,1)} %wv_ref.1) | copy-start | bytes 3145732
  68.8 34.4 %all-to-all-start.2 = ((bf16[64,8,1024]{2,1,0:T(8,128)(2,1)}), bf16[64,8,1024]{2,1,0:T(8,128)(2,1)S(1)}, u32[]{:S(2)}, u32[]{:S(2)}) async-start(bf16[64,8,1024]{2,1,0:T(8,128)(2,1)} %bitcast.21), calls=%async_computation.2 | async-start | bytes 2097152 | tf_op jit(solution)/shard_map/all_to_all | solution.py:308
  74.7 1.2 copy-start.5
  78.3 0.7 copy-start.6
  79.0 11.6 %collective-permute-start.2 = (bf16[256,512]{1,0:T(8,128)(2,1)}, bf16[256,512]{1,0:T(8,128)(2,1)S(1)}, u32[]{:S(2)}, u32[]{:S(2)}) collective-permute-start(bf16[256,512]{1,0:T(8,128)(2,1)} %get-tuple-element.25), channel_id=1, source_target_pairs={{0,1},{1,2},{2,3},{3,0},{4,5},{5,6},{6,7},{7,4},{8,9},{9,10},{10,1... | collective-permute-start | bytes 786440 | tf_op jit(solution)/shard_map/ppermute | solution.py:377
  82.1 14.3 %collective-permute-start.3 = (bf16[256,512]{1,0:T(8,128)(2,1)}, bf16[256,512]{1,0:T(8,128)(2,1)}, u32[]{:S(2)}, u32[]{:S(2)}) collective-permute-start(bf16[256,512]{1,0:T(8,128)(2,1)} %get-tuple-element.26), channel_id=1, source_target_pairs={{0,2},{1,3},{2,0},{3,1},{4,6},{5,7},{6,4},{7,5},{8,10},{9,11},{10,... | collective-permute-start | bytes 786440 | tf_op jit(solution)/shard_map/ppermute | solution.py:377
  86.5 3.1 %copy-start.11 = (s32[64,12]{1,0:T(8,128)S(1)}, s32[64,12]{1,0:T(8,128)}, u32[]{:S(2)}) copy-start(s32[64,12]{1,0:T(8,128)} %copy-done.10) | copy-start | bytes 9220
  86.5 11.1 %collective-permute-start.4 = (bf16[256,512]{1,0:T(8,128)(2,1)}, bf16[256,512]{1,0:T(8,128)(2,1)}, u32[]{:S(2)}, u32[]{:S(2)}) collective-permute-start(bf16[256,512]{1,0:T(8,128)(2,1)} %get-tuple-element.27), channel_id=1, source_target_pairs={{0,3},{1,0},{2,1},{3,2},{4,7},{5,4},{6,5},{7,6},{8,11},{9,8},{10,9... | collective-permute-start | bytes 786440 | tf_op jit(solution)/shard_map/ppermute | solution.py:377
  89.6 0.8 copy-start.12
  106.0 4.2 %copy-start.7 = (bf16[256,512]{1,0:T(8,128)(2,1)S(1)}, bf16[256,512]{1,0:T(8,128)(2,1)}, u32[]{:S(2)}) copy-start(bf16[256,512]{1,0:T(8,128)(2,1)} %copy-done.6) | copy-start | bytes 786436
  106.0 17.7 %all-to-all-start.3 = ((bf16[4,256,512]{2,1,0:T(8,128)(2,1)}), bf16[4,256,512]{2,1,0:T(8,128)(2,1)S(1)}, u32[]{:S(2)}, u32[]{:S(2)}) async-start(bf16[4,256,512]{2,1,0:T(8,128)(2,1)} %project.1), calls=%async_computation.3 | async-start | bytes 2097152 | tf_op jit(solution)/shard_map/all_to_all | solution.py:406
  111.4 11.4 %collective-permute-start.5 = (bf16[256,256]{1,0:T(8,128)(2,1)S(1)}, bf16[256,256]{1,0:T(8,128)(2,1)S(1)}, u32[]{:S(2)}, u32[]{:S(2)}) collective-permute-start(bf16[256,256]{1,0:T(8,128)(2,1)S(1)} %get-tuple-element.29), channel_id=1, source_target_pairs={{0,4},{4,0},{1,5},{5,1},{2,6},{6,2},{3,7},{7,3},{8,12},{12,8},{9,1... | collective-permute-start | bytes 393224 | tf_op jit(solution)/shard_map/ppermute | solution.py:386
